TPU v7x, 128 devices: a whole 4x4x4 slice. The times are simulated.
128 devices in a mesh: section: 2 (over y_hi), dp: 16 (over y_lo, z, core), tensor: 4 (over x).
Axes of the slice: x: 4, y: 4 (y_hi: 2, y_lo: 2; y = y_hi * 2 + y_lo), z: 4, core: 2. Of those that a mesh axis runs over, the one named last changes fastest.
Arguments:
- words: bfloat16 [2, 128, 20, 768], P('section', 'dp'), may hold values from -6 to 6
- regions: bfloat16 [2, 128, 36, 768], P('section', 'dp'), may hold values from -6 to 6
- word_lengths: int32 [128], P('dp'), may hold values from 3 to 20, as said below
- task_flags: int32 [128], P('dp'), may hold values from 0 to 2
- attn_qkv: bfloat16 [2, 2, 768, 3, 768], P('section', None, None, None, 'tensor'), may hold values from -0.21875 to 0.21875
- attn_qv_bias: float32 [2, 2, 2, 12, 64], P('section', None, None, 'tensor'), may hold values from -3 to 3
- attn_out: bfloat16 [2, 2, 768, 768], P('section', None, 'tensor'), may hold values from -0.875 to 0.875
- ffn_in: bfloat16 [2, 2, 768, 3072], P('section', None, None, 'tensor'), may hold values from -0.21875 to 0.21875
- ffn_in_bias: float32 [2, 2, 24, 128], P('section', None, 'tensor'), may hold values from -3 to 3
- ffn_out: bfloat16 [2, 2, 3072, 768], P('section', None, 'tensor'), may hold values from -0.109375 to 0.109375
- out_bias: float32 [2, 2, 2, 768], P('section'), may hold values from -2 to 2
- norm_gain: float32 [2, 2, 2, 768], P('section'), may hold values from 0.5 to 1.5
- norm_bias: float32 [2, 2, 2, 768], P('section'), may hold values from -2 to 2
- cross_qkv: bfloat16 [768, 3, 768], P(None, None, 'tensor'), may hold values from -0.21875 to 0.21875
- cross_qv_bias: float32 [2, 12, 64], P(None, 'tensor'), may hold values from -3 to 3
- cross_out: bfloat16 [768, 768], P('tensor'), may hold values from -0.875 to 0.875
- cross_out_bias: float32 [768], replicated, may hold values from -2 to 2
- cross_norm_gain: float32 [768], replicated, may hold values from 0.5 to 1.5
- cross_norm_bias: float32 [768], replicated, may hold values from -2 to 2
Outputs:
- words_out: float32 [2, 128, 20, 768], P('section', 'dp')
- regions_out: float32 [2, 128, 36, 768], P('section', 'dp')
- attn_qkv_grad: float32 [2, 2, 768, 3, 768], P('section', None, 'dp', None, 'tensor')
- attn_qv_bias_grad: float32 [2, 2, 2, 12, 64], P('section', None, None, 'tensor', 'dp')
- attn_out_grad: float32 [2, 2, 768, 768], P('section', None, 'tensor', 'dp')
- ffn_in_grad: float32 [2, 2, 768, 3072], P('section', None, 'dp', 'tensor')
- ffn_in_bias_grad: float32 [2, 2, 24, 128], P('section', None, 'tensor', 'dp')
- ffn_out_grad: float32 [2, 2, 3072, 768], P('section', None, 'tensor', 'dp')
- out_bias_grad: float32 [2, 2, 2, 768], P('section', None, None, 'dp')
- norm_gain_grad: float32 [2, 2, 2, 768], P('section', None, None, 'dp')
- norm_bias_grad: float32 [2, 2, 2, 768], P('section', None, None, 'dp')
- cross_qkv_grad: float32 [768, 3, 768], P(('section', 'dp'), None, 'tensor')
- cross_qv_bias_grad: float32 [2, 12, 64], P(None, 'tensor', ('section', 'dp'))
- cross_out_grad: float32 [768, 768], P('tensor', ('section', 'dp'))
- cross_out_bias_grad: float32 [768], P(('section', 'dp'))
- cross_norm_gain_grad: float32 [768], P(('section', 'dp'))
- cross_norm_bias_grad: float32 [768], P(('section', 'dp'))
Inputs may be any that keep to these rules, and one draw needn't show every extreme that they name: `word_lengths`: valid words of an item, counted from its first word; some item has 20. `task_flags`: 0 masked words, 1 masked regions, 2 matching or answering.
All inputs are finite; a program needn't handle non-finite values.
Results may differ from a plain program's by a relative error of at most 0.035.
Values may be sent and summed in bfloat16 or wider, within the bound.
A program may use at most 384 MiB of HBM per device.

v0:
```python
import functools

import jax
import jax.numpy as jnp
from jax import lax
from jax.experimental import pallas as pl
from jax.experimental.pallas import tpu as pltpu
from jax.sharding import PartitionSpec as P

MESH = pl.DeviceIdType.MESH
BF = jnp.bfloat16
F32 = jnp.float32
HEAD_DIM = 64
LOCAL_HEADS = 3
HW = HEAD_DIM * LOCAL_HEADS
WORDS = 20
REGIONS = 36
D = 768
ITEMS_LOCAL = 8
TENSOR = 4

ITEMS_MB = 2
MB = ITEMS_LOCAL // ITEMS_MB
RW = 48
RR = 80
R = RW + RR
C = R // TENSOR
SPANS = ((0, RW), (RW, R))

EPSILON = 1e-06
MASKED = -1000000000.0
SCALING = HEAD_DIM ** (-0.5)


def dot(a, b):
    return lax.dot_general(a, b, (((1,), (0,)), ((), ())), preferred_element_type=F32)


def dot_nt(a, b):
    return lax.dot_general(a, b, (((1,), (1,)), ((), ())), preferred_element_type=F32)


def dot_tn(a, b):
    return lax.dot_general(a, b, (((0,), (0,)), ((), ())), preferred_element_type=F32)


def head_masks():
    lane = lax.broadcasted_iota(jnp.int32, (1, HW), 1)
    return [
        ((lane >= h * HEAD_DIM) & (lane < (h + 1) * HEAD_DIM)).astype(F32) for h in range(LOCAL_HEADS)
    ]


def by_head(a):
    masks = [m.astype(BF) for m in head_masks()]
    return jnp.concatenate([a * m for m in masks], axis=0)


def join_heads(stacked):
    rows = stacked.shape[0] // LOCAL_HEADS
    masks = head_masks()
    total = stacked[:rows] * masks[0]
    for h in range(1, LOCAL_HEADS):
        total = total + stacked[h * rows : (h + 1) * rows] * masks[h]
    return total


def item_of(shape, axis, length):
    index = lax.broadcasted_iota(jnp.int32, shape, axis)
    item = jnp.zeros(shape, jnp.int32)
    for k in range(1, ITEMS_MB + 1):
        item = item + (index >= k * length).astype(jnp.int32)
    return item


def key_mask(q_rows, q_len, k_rows, k_len, key_valid):
    shape = (q_rows, k_rows)
    same = item_of(shape, 0, q_len) == item_of(shape, 1, k_len)
    inside = lax.broadcasted_iota(jnp.int32, shape, 1) < ITEMS_MB * k_len
    mask = same & inside
    if key_valid is not None:
        mask = mask & (jnp.broadcast_to(key_valid, shape) > 0.5)
    return mask


def attend(q, k, v, mask):
    scores = dot_nt(by_head(q), k) * SCALING
    mask = jnp.concatenate([mask] * LOCAL_HEADS, axis=0)
    scores = jnp.where(mask, scores, MASKED)
    e = jnp.exp(scores - jnp.max(scores, axis=-1, keepdims=True))
    probs = e / jnp.sum(e, axis=-1, keepdims=True)
    mixed = join_heads(dot(probs.astype(BF), v)).astype(BF)
    return probs, mixed


def attend_back(dmix, probs, q, k, v):
    d3 = by_head(dmix)
    dp = dot_nt(d3, v)
    ds = (probs * (dp - jnp.sum(probs * dp, axis=-1, keepdims=True))).astype(BF)
    dv = dot_tn(probs.astype(BF), d3).astype(BF)
    dq = (join_heads(dot(ds, k)) * SCALING).astype(BF)
    dk = (dot_tn(ds, by_head(q)) * SCALING).astype(BF)
    return dq, dk, dv


def norm_forward(r, gain, shift):
    center = r - jnp.mean(r, axis=-1, keepdims=True)
    spread = jnp.mean(center * center, axis=-1, keepdims=True)
    rstd = lax.rsqrt(spread + EPSILON)
    n = center * rstd
    return n, rstd, n * gain + shift


def norm_back(dh, n, rstd, gain):
    dn = dh * gain
    return rstd * (
        dn - jnp.mean(dn, axis=-1, keepdims=True) - n * jnp.mean(dn * n, axis=-1, keepdims=True)
    )


def kernel(
    x_ref, scale_ref, valid_ref, wqkv_ref, bqkv_ref, wo_ref, w1_ref, b1_ref, w2_ref, vec_ref,
    cwqkv_ref, cbqkv_ref, cwo_ref, cvec_ref,
    y_ref, g_ref, s_ref,
    send, recv, xlow, midf, alow, dyf, dya, dyc, ybuf, back,
    qkv, mixed, dqkv, cqkv, cmixed, cdqkv, act, dup, dgelu,
    p_w, p_r, cp_w, cp_r, cur, res, nrm, rstd, acc, rowp, bsum, bqsum,
    rs_send, rs_recv, ag_send, ag_recv, y_send, y_recv, sec_send, sec_recv,
):
    sec = lax.axis_index("section")
    me = lax.axis_index("tensor")
    head = sec == 0
    cross = sec == 1
    own = pl.ds(pl.multiple_of(me * C, C), C)

    def peer(o):
        return {"tensor": lax.rem(me + o, TENSOR)}

    def rows_of(t):
        return pl.ds(pl.multiple_of(t * C, C), C)

    partner = {"section": 1 - sec}

    barrier = pltpu.get_barrier_semaphore()
    for o in range(1, TENSOR):
        pl.semaphore_signal(barrier, inc=1, device_id=peer(o), device_id_type=MESH)
    pl.semaphore_signal(barrier, inc=1, device_id=partner, device_id_type=MESH)

    row = lax.broadcasted_iota(jnp.int32, (C, 1), 0) + me * C
    is_word = row < RW
    for k in range(6):
        rowp[k] = jnp.where(is_word, vec_ref[2 * k : 2 * k + 1, :], vec_ref[2 * k + 1 : 2 * k + 2, :])
    acc[...] = jnp.zeros_like(acc)
    bsum[...] = jnp.zeros_like(bsum)
    bqsum[...] = jnp.zeros_like(bqsum)

    pl.semaphore_wait(barrier, TENSOR)

    def rs_copies(m):
        return [
            pltpu.make_async_remote_copy(
                src_ref=send.at[m, rows_of(lax.rem(me + o, TENSOR))],
                dst_ref=recv.at[m, o - 1],
                send_sem=rs_send.at[m, o - 1],
                recv_sem=rs_recv.at[m, o - 1],
                device_id=peer(o),
                device_id_type=MESH,
            )
            for o in range(1, TENSOR)
        ]

    def rs_start(m):
        for copy in rs_copies(m):
            copy.start()

    def rs_finish(m):
        for copy in rs_copies(m):
            copy.wait()
        total = send[m, own].astype(F32)
        for o in range(TENSOR - 1):
            total = total + recv[m, o].astype(F32)
        return total

    def ag_copies(buf, m, ss, rs):
        return [
            pltpu.make_async_remote_copy(
                src_ref=buf.at[m, own],
                dst_ref=buf.at[m, own],
                send_sem=ss.at[m, o - 1],
                recv_sem=rs.at[m, o - 1],
                device_id=peer(o),
                device_id_type=MESH,
            )
            for o in range(1, TENSOR)
        ]

    def ag_start(buf, m, ss=ag_send, rs=ag_recv):
        for copy in ag_copies(buf, m, ss, rs):
            copy.start()

    def ag_finish(buf, m, ss=ag_send, rs=ag_recv):
        for copy in ag_copies(buf, m, ss, rs):
            copy.wait()

    def sec_copy(buf, m):
        return pltpu.make_async_remote_copy(
            src_ref=buf.at[m, own],
            dst_ref=buf.at[m, own],
            send_sem=sec_send.at[m],
            recv_sem=sec_recv.at[m],
            device_id=partner,
            device_id_type=MESH,
        )

    def save_norm(l, m, n, r):
        nrm[l, m] = n
        rstd[l, m] = jnp.broadcast_to(r, (C, 128))

    def norm_step_back(l, m, dh, gain):
        n = nrm[l, m]
        dr = norm_back(dh, n, rstd[l, m][:, :1], gain)
        low = dr.astype(BF)
        acc[3 * l] += dh * n
        acc[3 * l + 1] += dh
        acc[3 * l + 2] += low.astype(F32)
        res[m] = dr
        return low

    def word_keys(m, q_rows, q_len):
        return key_mask(q_rows, q_len, RW, WORDS, valid_ref[m])

    def region_keys(q_rows, q_len):
        return key_mask(q_rows, q_len, RR, REGIONS, None)

    def cross_a(m):
        sec_copy(midf, m).wait_recv()
        ag_start(midf, m)

    def cross_b(m):
        ag_finish(midf, m)
        out = dot(midf[m], cwqkv_ref[...]) + cbqkv_ref[...]
        out = out.astype(BF)
        q, k, v = out[:, :HW], out[:, HW : 2 * HW], out[:, 2 * HW :]
        cqkv[0, m], cqkv[1, m], cqkv[2, m] = q, k, v
        probs, mix = attend(q[:RW], k[RW:], v[RW:], region_keys(RW, WORDS))
        cp_w[m] = probs
        cmixed[m, :RW] = mix
        probs, mix = attend(q[RW:], k[:RW], v[:RW], word_keys(m, RR, REGIONS))
        cp_r[m] = probs
        cmixed[m, RW:] = mix
        send[m] = dot(cmixed[m], cwo_ref[...]).astype(BF)
        rs_start(m)

    def cross_c(m):
        r = midf[m, own].astype(F32) + rs_finish(m) + cvec_ref[0:1, :]
        n, rs, h = norm_forward(r, cvec_ref[1:2, :], cvec_ref[2:3, :])
        save_norm(2, m, n, rs)
        cur[m] = h
        xlow[m, own] = h.astype(BF)
        ag_start(xlow, m)

    def layer_a(m):
        @pl.when(head)
        def _():
            xlow[m] = x_ref[m]
            cur[m] = x_ref[m, own].astype(F32)

        @pl.when(cross)
        def _():
            ag_finish(xlow, m)

        for mod, (lo, hi) in enumerate(SPANS):
            out = (dot(xlow[m, lo:hi], wqkv_ref[mod]) + bqkv_ref[mod]).astype(BF)
            q, k, v = out[:, :HW], out[:, HW : 2 * HW], out[:, 2 * HW :]
            qkv[0, m, lo:hi], qkv[1, m, lo:hi], qkv[2, m, lo:hi] = q, k, v
            if mod == 0:
                probs, mix = attend(q, k, v, word_keys(m, RW, WORDS))
                p_w[m] = probs
            else:
                probs, mix = attend(q, k, v, region_keys(RR, REGIONS))
                p_r[m] = probs
            mixed[m, lo:hi] = mix
            send[m, lo:hi] = dot(mix, wo_ref[mod]).astype(BF)
        rs_start(m)

    def layer_b(m):
        r = cur[m] + rs_finish(m) + rowp[0]
        n, rs, h = norm_forward(r, rowp[2], rowp[4])
        save_norm(0, m, n, rs)
        cur[m] = h
        alow[m, own] = h.astype(BF)
        ag_start(alow, m)

    def layer_c(m):
        ag_finish(alow, m)
        for mod, (lo, hi) in enumerate(SPANS):
            up = dot(alow[m, lo:hi], w1_ref[mod]) + b1_ref[mod]
            cdf = 0.5 * (1.0 + lax.erf(up * (0.5**0.5)))
            dgelu[m, lo:hi] = cdf + up * jnp.exp(-0.5 * up * up) * 0.3989422804014327
            active = (up * cdf).astype(BF)
            act[m, lo:hi] = active
            send[m, lo:hi] = dot(active, w2_ref[mod]).astype(BF)
        rs_start(m)

    def layer_d(m):
        r = cur[m] + rs_finish(m) + rowp[1]
        n, rs, h = norm_forward(r, rowp[3], rowp[5])
        save_norm(1, m, n, rs)
        return h

    def back_e(m, dh):
        low = norm_step_back(1, m, dh, rowp[3])
        dyf[m, own] = low
        ag_start(dyf, m)

    def back_f(m):
        ag_finish(dyf, m)
        for mod, (lo, hi) in enumerate(SPANS):
            d = (dot_nt(dyf[m, lo:hi], w2_ref[mod]) * dgelu[m, lo:hi]).astype(BF)
            dup[m, lo:hi] = d
            bsum[mod] += jnp.sum(d.astype(F32), axis=0, keepdims=True)
            send[m, lo:hi] = dot_nt(d, w1_ref[mod]).astype(BF)
        rs_start(m)

    def back_g(m):
        dh = res[m] + rs_finish(m)
        low = norm_step_back(0, m, dh, rowp[2])
        dya[m, own] = low
        ag_start(dya, m)

    def back_h(m):
        ag_finish(dya, m)
        for mod, (lo, hi) in enumerate(SPANS):
            dmix = dot_nt(dya[m, lo:hi], wo_ref[mod]).astype(BF)
            probs = p_w[m] if mod == 0 else p_r[m]
            parts = attend_back(
                dmix, probs, qkv[0, m, lo:hi], qkv[1, m, lo:hi], qkv[2, m, lo:hi]
            )
            d = jnp.concatenate(parts, axis=1)
            dqkv[m, lo:hi] = d
            bqsum[mod] += jnp.sum(d.astype(F32), axis=0, keepdims=True)
            send[m, lo:hi] = dot_nt(d, wqkv_ref[mod]).astype(BF)
        rs_start(m)

    def cross_back_a(m):
        dh = res[m] + rs_finish(m)
        low = norm_step_back(2, m, dh, cvec_ref[1:2, :])
        dyc[m, own] = low
        ag_start(dyc, m)

    def cross_back_b(m):
        ag_finish(dyc, m)
        dmix = dot_nt(dyc[m], cwo_ref[...]).astype(BF)
        q, k, v = cqkv[0, m], cqkv[1, m], cqkv[2, m]
        dq_w, dk_r, dv_r = attend_back(dmix[:RW], cp_w[m], q[:RW], k[RW:], v[RW:])
        dq_r, dk_w, dv_w = attend_back(dmix[RW:], cp_r[m], q[RW:], k[:RW], v[:RW])
        cdqkv[m, :RW] = jnp.concatenate([dq_w, dk_w, dv_w], axis=1)
        cdqkv[m, RW:] = jnp.concatenate([dq_r, dk_r, dv_r], axis=1)
        d = cdqkv[m]
        bqsum[2] += jnp.sum(d.astype(F32), axis=0, keepdims=True)
        send[m] = dot_nt(d, cwqkv_ref[...]).astype(BF)
        rs_start(m)

    def cross_back_c(m):
        back[m, own] = (res[m] + rs_finish(m)).astype(BF)
        sec_copy(back, m).start()

    def outer(left, right, lo, hi, store):
        def tile(j):
            columns = pl.ds(pl.multiple_of(j * (D // 2), D // 2), D // 2)
            a = left[:, lo:hi, columns].reshape(MB * (hi - lo), D // 2)
            b = right[:, lo:hi, :].reshape(MB * (hi - lo), right.shape[-1])
            store(j, dot_tn(a, b).astype(BF))

        pl.loop(0, 2)(tile)

    def store_at(block, lo, hi):
        def store(j, value):
            g_ref[block, j, :, :, :, lo:hi] = value.reshape(4, 2, 48, hi - lo)

        return store

    def ffn_outer():
        for mod, (lo, hi) in enumerate(SPANS):
            outer(alow, dup, lo, hi, store_at(2 + 2 * mod, 0, D))
            outer(dyf, act, lo, hi, store_at(3 + 2 * mod, 0, D))

    def attn_outer():
        for mod, (lo, hi) in enumerate(SPANS):
            outer(xlow, dqkv, lo, hi, store_at(mod, 0, 3 * HW))
            outer(dya, mixed, lo, hi, store_at(mod, 3 * HW, D))

    def cross_outer():
        outer(midf, cdqkv, 0, R, store_at(6, 0, 3 * HW))
        outer(dyc, cmixed, 0, R, store_at(6, 3 * HW, D))

    def each(*steps):
        def body(m):
            for step in steps:
                step(m)

        pl.loop(0, MB)(body)

    @pl.when(cross)
    def _():
        each(cross_a)
        each(cross_b)
        each(cross_c)

    each(layer_a)
    each(layer_b)
    each(layer_c)

    @pl.when(head)
    def _():
        def to_partner(m):
            midf[m, own] = layer_d(m).astype(BF)
            sec_copy(midf, m).start()

        def from_partner(m):
            sec_copy(midf, m).wait_send()
            sec_copy(back, m).wait_recv()
            back_e(m, back[m, own].astype(F32))

        each(to_partner)
        each(from_partner)

    @pl.when(cross)
    def _():
        def turn(m):
            h = layer_d(m)
            back_e(m, x_ref[m, own].astype(F32) * scale_ref[m, own])
            ybuf[m, own] = h.astype(BF)
            ag_start(ybuf, m, y_send, y_recv)

        each(turn)

    each(back_f)
    each(back_g)
    each(back_h)

    @pl.when(head)
    def _():
        def last(m):
            ybuf[m, own] = (res[m] + rs_finish(m)).astype(BF)
            ag_start(ybuf, m, y_send, y_recv)

        each(last)
        g_ref[6] = jnp.zeros(g_ref.shape[1:], BF)

    @pl.when(cross)
    def _():
        each(cross_back_a)
        each(cross_back_b)
        each(cross_back_c)
        cross_outer()

    ffn_outer()
    attn_outer()

    def write(m):
        ag_finish(ybuf, m, y_send, y_recv)
        y_ref[m] = ybuf[m]

    each(write)

    @pl.when(cross)
    def _():
        each(lambda m: sec_copy(back, m).wait_send())

    s_ref[...] = jnp.zeros_like(s_ref)
    for l in range(2):
        for k in range(3):
            a = acc[3 * l + k]
            at = 2 * (3 * l + k)
            s_ref[at : at + 1, :] = jnp.sum(jnp.where(is_word, a, 0.0), axis=0, keepdims=True)
            s_ref[at + 1 : at + 2, :] = jnp.sum(jnp.where(is_word, 0.0, a), axis=0, keepdims=True)
    for k in range(3):
        s_ref[12 + k : 13 + k, :] = jnp.sum(acc[6 + k], axis=0, keepdims=True)
    for mod in range(2):
        s_ref[16 + mod : 17 + mod, :] = bsum[mod]
    for k in range(3):
        s_ref[18 + k : 19 + k, : 3 * HW] = bqsum[k]


def local(
    words, regions, word_lengths, task_flags, attn_qkv, attn_qv_bias, attn_out, ffn_in, ffn_in_bias,
    ffn_out, out_bias, norm_gain, norm_bias, cross_qkv, cross_qv_bias, cross_out, cross_out_bias,
    cross_norm_gain, cross_norm_bias,
):
    def rows(w, r):
        w = w.reshape(MB, ITEMS_MB * WORDS, -1)
        r = r.reshape(MB, ITEMS_MB * REGIONS, -1)
        w = jnp.pad(w, ((0, 0), (0, RW - w.shape[1]), (0, 0)))
        r = jnp.pad(r, ((0, 0), (0, RR - r.shape[1]), (0, 0)))
        return jnp.concatenate([w, r], axis=1)

    x = rows(words[0], regions[0])
    word_scale = jnp.where(task_flags == 1, 0.25, 1.0).astype(F32)
    region_scale = jnp.where(task_flags == 0, 0.25, 1.0).astype(F32)
    scale = rows(
        jnp.broadcast_to(word_scale[:, None], (ITEMS_LOCAL, WORDS)),
        jnp.broadcast_to(region_scale[:, None], (ITEMS_LOCAL, REGIONS)),
    )
    valid = (jnp.arange(WORDS)[None, :] < word_lengths[:, None]).astype(F32)
    valid = valid.reshape(MB, 1, ITEMS_MB * WORDS)
    valid = jnp.pad(valid, ((0, 0), (0, 0), (0, RW - ITEMS_MB * WORDS)))

    def qkv_bias(b):
        b = b.reshape(*b.shape[:-3], 2, HW)
        return jnp.concatenate(
            [b[..., 0:1, :], jnp.zeros_like(b[..., 0:1, :]), b[..., 1:2, :]], axis=-1
        )

    vec = jnp.concatenate(
        [a[0][:, k] for a in (out_bias, norm_gain, norm_bias) for k in range(2)], axis=0
    )
    cvec = jnp.stack([cross_out_bias, cross_norm_gain, cross_norm_bias])
    inputs = (
        x, scale, valid, attn_qkv[0].reshape(2, D, 3 * HW), qkv_bias(attn_qv_bias[0]), attn_out[0],
        ffn_in[0], ffn_in_bias[0].reshape(2, 1, D), ffn_out[0], vec,
        cross_qkv.reshape(D, 3 * HW), qkv_bias(cross_qv_bias), cross_out, cvec,
    )

    vmem = pl.BlockSpec(memory_space=pltpu.VMEM)
    mb_rows = lambda width, dtype: pltpu.VMEM((MB, R, width), dtype)
    own_rows = lambda count: pltpu.VMEM((count, MB, C, D), F32)
    y, g, s = pl.pallas_call(
        kernel,
        out_shape=(
            jax.ShapeDtypeStruct((MB, R, D), BF),
            jax.ShapeDtypeStruct((7, 2, 4, 2, 48, D), BF),
            jax.ShapeDtypeStruct((24, D), F32),
        ),
        in_specs=[vmem] * len(inputs),
        out_specs=[vmem] * 3,
        scratch_shapes=[
            mb_rows(D, BF),
            pltpu.VMEM((MB, TENSOR - 1, C, D), BF),
            *[mb_rows(D, BF) for _ in range(8)],
            pltpu.VMEM((3, MB, R, HW), BF),
            mb_rows(HW, BF),
            mb_rows(3 * HW, BF),
            pltpu.VMEM((3, MB, R, HW), BF),
            mb_rows(HW, BF),
            mb_rows(3 * HW, BF),
            mb_rows(D, BF),
            mb_rows(D, BF),
            mb_rows(D, F32),
            pltpu.VMEM((MB, 3 * RW, RW), F32),
            pltpu.VMEM((MB, 3 * RR, RR), F32),
            pltpu.VMEM((MB, 3 * RW, RR), F32),
            pltpu.VMEM((MB, 3 * RR, RW), F32),
            pltpu.VMEM((MB, C, D), F32),
            pltpu.VMEM((MB, C, D), F32),
            own_rows(3),
            pltpu.VMEM((3, MB, C, 128), F32),
            pltpu.VMEM((9, C, D), F32),
            pltpu.VMEM((6, C, D), F32),
            pltpu.VMEM((2, 1, D), F32),
            pltpu.VMEM((3, 1, 3 * HW), F32),
            *[pltpu.SemaphoreType.DMA((MB, TENSOR - 1)) for _ in range(6)],
            pltpu.SemaphoreType.DMA((MB,)),
            pltpu.SemaphoreType.DMA((MB,)),
        ],
        compiler_params=pltpu.CompilerParams(
            collective_id=0, has_side_effects=True, vmem_limit_bytes=60 * 2**20
        ),
    )(*inputs)

    g = g.reshape(7, D, D)
    layer = lax.psum_scatter(g[:6], "dp", scatter_dimension=1, tiled=True).astype(F32)
    s_dp = lax.psum(s, "dp")
    s_all = lax.psum(s_dp[:16], "tensor")
    dp = lax.axis_index("dp")
    both = lax.axis_index("section") * 16 + dp

    def part(a, index, width):
        return lax.dynamic_slice_in_dim(a, index * width, width, axis=a.ndim - 1)

    qkv_g = layer[:2, :, : 3 * HW].reshape(1, 2, 48, 3, HW)
    out_g = jnp.swapaxes(layer[:2, :, 3 * HW :], 1, 2)[None]
    in_g = layer[2:6:2][None]
    ffo_g = jnp.swapaxes(layer[3:6:2], 1, 2)[None]
    qb = s_dp[18:21, : 3 * HW].reshape(3, 3, LOCAL_HEADS, HEAD_DIM)[:, 0::2]
    qv_bias_g = part(qb[:2], dp, 4)[None]
    b1_g = part(s_dp[16:18].reshape(2, 6, 128), dp, 8)[None]
    small = part(s_all[:12].reshape(2, 3, 2, D), dp, 48)
    gain_g, shift_g, obias_g = (jnp.swapaxes(small[:, k], 0, 1)[None] for k in range(3))

    c = lax.psum(g[6].astype(F32), ("section", "dp"))
    c = lax.dynamic_slice_in_dim(c, both * 24, 24, axis=0)
    cs = lax.psum(s_all[12:15], "section")
    cqb = lax.psum(qb[2], "section")
    c_small = part(cs, both, 24)
    word_rows = y[:, : ITEMS_MB * WORDS].reshape(1, ITEMS_LOCAL, WORDS, D).astype(F32)
    region_rows = y[:, RW : RW + ITEMS_MB * REGIONS].reshape(1, ITEMS_LOCAL, REGIONS, D).astype(F32)
    return (
        word_rows, region_rows, qkv_g, qv_bias_g, out_g, in_g, b1_g, ffo_g, obias_g, gain_g, shift_g,
        c[:, : 3 * HW].reshape(24, 3, HW), part(cqb, both, 2), c[:, 3 * HW :].T,
        c_small[2], c_small[0], c_small[1],
    )


def solution(mesh):
    in_specs = (
        P("section", "dp", None, None),
        P("section", "dp", None, None),
        P("dp"),
        P("dp"),
        P("section", None, None, None, "tensor"),
        P("section", None, None, "tensor", None),
        P("section", None, "tensor", None),
        P("section", None, None, "tensor"),
        P("section", None, "tensor", None),
        P("section", None, "tensor", None),
        P("section", None, None, None),
        P("section", None, None, None),
        P("section", None, None, None),
        P(None, None, "tensor"),
        P(None, "tensor", None),
        P("tensor", None),
        P(),
        P(),
        P(),
    )
    out_specs = (
        P("section", "dp", None, None),
        P("section", "dp", None, None),
        P("section", None, "dp", None, "tensor"),
        P("section", None, None, "tensor", "dp"),
        P("section", None, "tensor", "dp"),
        P("section", None, "dp", "tensor"),
        P("section", None, "tensor", "dp"),
        P("section", None, "tensor", "dp"),
        P("section", None, None, "dp"),
        P("section", None, None, "dp"),
        P("section", None, None, "dp"),
        P(("section", "dp"), None, "tensor"),
        P(None, "tensor", ("section", "dp")),
        P("tensor", ("section", "dp")),
        P(("section", "dp")),
        P(("section", "dp")),
        P(("section", "dp")),
    )
    return jax.shard_map(local, mesh=mesh, in_specs=in_specs, out_specs=out_specs, check_vma=False)
```

profile of v0, /device:TPU:0, one launch (start us, length us, event | category | flops | bytes accessed | tf_op | source)
XLA Modules:
  0.0 521.6 jit_solution(12970218639662079153)
XLA Ops:
  7.3 0.9 copy.107
  8.1 0.7 copy.108
  8.8 0.7 copy.109
  9.5 0.7 copy.73
  10.3 0.8 slice_reduce_fusion.1
  12.5 0.9 copy.78.scale_ref
  13.4 1.1 copy.72
  14.8 2.3 copy.79.wqkv_ref
  17.1 1.3 copy.81.cwqkv_ref
  21.3 0.9 fusion.2.x_ref
  22.8 1.3 concatenate.18.vec_ref
  24.1 195.0 %shard_map.314 = (bf16[4,128,768]{2,1,0:T(8,128)(2,1)}, bf16[7,2,4,2,48,768]{5,4,3,2,1,0:T(8,128)(2,1)}, f32[24,768]{1,0:T(8,128)}) custom-call(bf16[4,128,768]{2,1,0:T(8,128)(2,1)} %fusion.2.x_ref, f32[4,128,1]{2,1,0:T(8,128)} %copy.78.scale_ref, f32[4,1,48]{2,1,0:T(1,128)} %pad_convert_fusion.valid_ref, bf16[2,768,576]{2,1,0:T(8,128)(2,1)} %copy.79.wqkv_ref, ...), custom_call_target="tpu_custom_call" | custom-call | tf_op jit(solution)/shard_map/pallas_call | solution.py:528
  219.2 1.3 slice.141
  220.5 1.7 bitcast_convert_fusion
  222.4 6.4 %slice.126 = bf16[6,2,4,2,48,768]{5,4,3,2,1,0:T(8,128)(2,1)} slice(bf16[7,2,4,2,48,768]{5,4,3,2,1,0:T(8,128)(2,1)} %get-tuple-element.21), slice={[0:6], [0:2], [0:4], [0:2], [0:48], [0:768]} | slice | bytes 14155776 | tf_op jit(solution)/shard_map/slice | solution.py:572
  228.9 1.1 copy-done.3
  230.2 1.2 copy.87
  231.4 0.9 copy.86
  232.4 91.1 %all-reduce.9.cloned.1.call-done = f32[24,768]{1,0:T(8,128)} async-done(((f32[24,768]{1,0:T(8,128)}), f32[24,768]{1,0:T(8,128)}) %all-reduce.9.cloned.1.call-update) | async-done | bytes 73744 | tf_op jit(solution)/shard_map/psum | solution.py:573
  323.4 0.7 slice.158
  324.4 0.8 slice.162
  325.2 17.3 %psum.36 = f32[16,768]{1,0:T(8,128)S(1)} all-reduce(f32[16,768]{1,0:T(8,128)S(1)} %slice.162), channel_id=1, replica_groups=mesh['section'=2,'dp'=16,'tensor'=4] {'tensor'}, use_global_device_ids=true, to_apply=%region_2.3 | all-reduce | flops 12288 | bytes 98304 | tf_op jit(solution)/shard_map/psum | solution.py:574
  345.1 0.7 slice.161
  346.5 12.2 %all-reduce.5 = (f32[2,3,64]{1,2,0:T(8,128)S(1)}, f32[3,768]{1,0:T(4,128)S(1)}) all-reduce(f32[2,3,64]{1,2,0:T(8,128)S(1)} %bitcast.84, f32[3,768]{1,0:T(4,128)S(1)} %slice.165), channel_id=1, replica_groups=mesh['section'=2,'dp'=16,'tensor'=4] {'section'}, use_global_device_ids=true, to_apply=%region_4.5 | all-reduce | flops 2688 | bytes 21504 | tf_op jit(solution)/shard_map/psum | solution.py:594
  359.8 76.9 %all-reduce.11.cloned.1.call-done = f32[768,768]{1,0:T(8,128)} async-done(((f32[768,768]{1,0:T(8,128)}), f32[768,768]{1,0:T(8,128)}) %all-reduce.11.cloned.1.call-update) | async-done | bytes 2359312 | tf_op jit(solution)/shard_map/psum | solution.py:591
  436.7 0.8 constant_dynamic-slice_fusion
  438.3 1.4 dynamic-slice_bitcast_fusion
  439.8 71.6 %reduce-scatter.2.cloned.1.call-done = bf16[6,48,768]{2,1,0:T(8,128)(2,1)} async-done(((bf16[6,768,768]{2,1,0:T(8,128)(2,1)}), bf16[6,48,768]{2,1,0:T(8,128)(2,1)}) %reduce-scatter.2.cloned.1.call-update) | async-done | bytes 442384 | tf_op jit(solution)/shard_map/reduce_scatter | solution.py:572
  511.3 1.2 convert_element_type.59
  512.5 0.8 slice_bitcast_fusion
  513.3 0.7 slice_bitcast_fusion.2
  514.3 0.8 copy.88
  (85 shorter events, 11.3 us)
Async XLA Ops:
  7.2 7.4 %copy-start.4 = (bf16[1,8,20,768]{3,1,2,0:T(8,128)(2,1)S(1)}, bf16[1,8,20,768]{3,1,2,0:T(8,128)(2,1)}, u32[]{:S(2)}) copy-start(bf16[1,8,20,768]{3,1,2,0:T(8,128)(2,1)} %param.19) | copy-start | bytes 737284
  7.2 7.5 %copy-start = (bf16[1,2,768,3,192]{2,4,3,1,0:T(8,128)(2,1)S(1)}, bf16[1,2,768,3,192]{2,4,3,1,0:T(8,128)(2,1)}, u32[]{:S(2)}) copy-start(bf16[1,2,768,3,192]{2,4,3,1,0:T(8,128)(2,1)} %param.23) | copy-start | bytes 5308420
  7.2 316.2 %all-reduce.9.cloned.1.call-start = ((), (), s32[]{:S(2)}) async-start(), calls=%async_computation.2 | async-start | bytes 147456 | tf_op jit(solution)/shard_map/psum | solution.py:573
  14.7 2.4 copy-start.2
  14.7 3.7 copy-start.6
  14.7 3.7 copy-start.7
  14.7 3.7 copy-start.8
  14.7 3.7 copy-start.9
  14.7 4.6 copy-start.5
  219.1 217.6 %all-reduce.11.cloned.1.call-start = ((), (), s32[]{:S(2)}) async-start(), calls=%async_computation.3 | async-start | bytes 4718592 | tf_op jit(solution)/shard_map/psum | solution.py:591
  222.2 289.1 %reduce-scatter.2.cloned.1.call-start = ((), (), s32[]{:S(2)}) async-start(), calls=%async_computation.1 | async-start | bytes 7520256 | tf_op jit(solution)/shard_map/reduce_scatter | solution.py:572
  228.9 1.1 copy-start.3
  511.3 2.7 copy-start.1
Sparse Core Ops, SparseCore 0:
  219.2 104.1 all-reduce.8
  327.1 109.5 all-reduce.10
  439.3 71.9 reduce-scatter.1
where the time goes:
time: 522 us
  waiting for transfers between devices  240 us (46%)
  Pallas kernels  195 us (37%)
  local copies, waits for them, and re-layouts  36.2 us (7%)
  blocking collectives  29.4 us (6%)
  between operations  14.1 us (3%)
  other arithmetic  6.98 us (1%)
    pallas_call x1, Pallas kernels, local(): pl.pallas_call(kernel, out_shape=(jax.ShapeDtypeStruct((MB, R, D), BF), j...  195 us
    psum x1, waiting for transfers between devices, local(): s_dp = lax.psum(s, 'dp')  91.1 us
    psum x1, waiting for transfers between devices, local(): c = lax.psum(g[6].astype(F32), ('section', 'dp'))  76.9 us
    reduce_scatter x1, waiting for transfers between devices, local(): lax.psum_scatter(g[:6], 'dp', scatter_dimension=1, tiled=True).astype(F32)  71.6 us
    psum x1, blocking collectives, local(): s_all = lax.psum(s_dp[:16], 'tensor')  17.3 us
    psum x1, blocking collectives, local(): cqb = lax.psum(qb[2], 'section')  12.2 us
    unnamed x34, local copies, waits for them, and re-layouts  10.6 us
  transfers between devices with their start and end apart: 3, of which 3 were waited for; matrix products, arithmetic and copies ran while one was open for 4% of the time, Pallas kernels for 0%

commit v1 on v0

--- a/solution.py
+++ b/solution.py
@@ -121,11 +121,13 @@
 def kernel(
     x_ref, scale_ref, valid_ref, wqkv_ref, bqkv_ref, wo_ref, w1_ref, b1_ref, w2_ref, vec_ref,
     cwqkv_ref, cbqkv_ref, cwo_ref, cvec_ref,
-    y_ref, g_ref, s_ref,
+    y_ref, dw_ref, s_ref, dc_ref, sc_ref,
     send, recv, xlow, midf, alow, dyf, dya, dyc, ybuf, back,
     qkv, mixed, dqkv, cqkv, cmixed, cdqkv, act, dup, dgelu,
     p_w, p_r, cp_w, cp_r, cur, res, nrm, rstd, acc, rowp, bsum, bqsum,
+    g_ref, from_core, from_y, from_zs, from_z, from_ys, wide, sums, sums_t, sums_c, sums_y, sums_z, pack,
     rs_send, rs_recv, ag_send, ag_recv, y_send, y_recv, sec_send, sec_recv,
+    dw_send, dw_recv, sm_send, sm_recv, pk_send, pk_recv,
 ):
     sec = lax.axis_index("section")
     me = lax.axis_index("tensor")
@@ -140,11 +142,23 @@
         return pl.ds(pl.multiple_of(t * C, C), C)
 
     partner = {"section": 1 - sec}
+    place = lax.axis_index("dp")
+    y_at, z_at, core = place // 8, lax.rem(place // 2, 4), lax.rem(place, 2)
+
+    def dp_device(y, z, c):
+        return {"dp": (y * 4 + z) * 2 + c}
+
+    other_core = dp_device(y_at, z_at, 1 - core)
+    other_y = dp_device(1 - y_at, z_at, core)
+
+    def z_next(o):
+        return lax.rem(z_at + o, 4)
 
     barrier = pltpu.get_barrier_semaphore()
     for o in range(1, TENSOR):
         pl.semaphore_signal(barrier, inc=1, device_id=peer(o), device_id_type=MESH)
-    pl.semaphore_signal(barrier, inc=1, device_id=partner, device_id_type=MESH)
+    for device in (partner, other_core, other_y, *(dp_device(y_at, z_next(o), core) for o in (1, 2, 3))):
+        pl.semaphore_signal(barrier, inc=1, device_id=device, device_id_type=MESH)
 
     row = lax.broadcasted_iota(jnp.int32, (C, 1), 0) + me * C
     is_word = row < RW
@@ -154,7 +168,7 @@
     bsum[...] = jnp.zeros_like(bsum)
     bqsum[...] = jnp.zeros_like(bqsum)
 
-    pl.semaphore_wait(barrier, TENSOR)
+    pl.semaphore_wait(barrier, 9)
 
     def rs_copies(m):
         return [
@@ -370,29 +384,200 @@
             columns = pl.ds(pl.multiple_of(j * (D // 2), D // 2), D // 2)
             a = left[:, lo:hi, columns].reshape(MB * (hi - lo), D // 2)
             b = right[:, lo:hi, :].reshape(MB * (hi - lo), right.shape[-1])
-            store(j, dot_tn(a, b).astype(BF))
+            store(j, dot_tn(a, b))
 
         pl.loop(0, 2)(tile)
 
     def store_at(block, lo, hi):
         def store(j, value):
-            g_ref[block, j, :, :, :, lo:hi] = value.reshape(4, 2, 48, hi - lo)
+            g_ref[block, j, :, :, :, lo:hi] = value.astype(BF).reshape(4, 2, 48, hi - lo)
 
         return store
 
     def ffn_outer():
         for mod, (lo, hi) in enumerate(SPANS):
-            outer(alow, dup, lo, hi, store_at(2 + 2 * mod, 0, D))
-            outer(dyf, act, lo, hi, store_at(3 + 2 * mod, 0, D))
+            outer(alow, dup, lo, hi, store_at(1 + 4 * mod, 0, D))
+            outer(dyf, act, lo, hi, store_at(2 + 4 * mod, 0, D))
 
     def attn_outer():
         for mod, (lo, hi) in enumerate(SPANS):
-            outer(xlow, dqkv, lo, hi, store_at(mod, 0, 3 * HW))
-            outer(dya, mixed, lo, hi, store_at(mod, 3 * HW, D))
+            outer(xlow, dqkv, lo, hi, store_at(4 * mod, 0, 3 * HW))
+            outer(dya, mixed, lo, hi, store_at(4 * mod, 3 * HW, D))
 
     def cross_outer():
-        outer(midf, cdqkv, 0, R, store_at(6, 0, 3 * HW))
-        outer(dyc, cmixed, 0, R, store_at(6, 3 * HW, D))
+        def store(lo, hi):
+            def put(j, value):
+                wide[j, :, :, lo:hi] = value.reshape(16, 24, hi - lo)
+
+            return put
+
+        outer(midf, cdqkv, 0, R, store(0, 3 * HW))
+        outer(dyc, cmixed, 0, R, store(3 * HW, D))
+        for y in range(2):
+            for z in range(4):
+                for c in range(2):
+                    at = (y * 4 + z) * 2 + c
+                    both = jnp.concatenate([wide[0, at], wide[1, at]], axis=0)
+                    g_ref[3, y, z, c] = both.astype(BF)
+
+    def moved(src, dst, send_sem, recv_sem, device):
+        return pltpu.make_async_remote_copy(
+            src_ref=src, dst_ref=dst, send_sem=send_sem, recv_sem=recv_sem, device_id=device,
+            device_id_type=MESH,
+        )
+
+    def dw_copies(group, phase):
+        (a0, a1), (b0, b1) = group[1:]
+        sems = lambda k: (dw_send.at[group[0], k], dw_recv.at[group[0], k])
+        na, nb = slice(a0, a1), slice(b0, b1)
+        nbr = slice(b0 - 4, b1 - 4)
+        copies = []
+        if phase == 0:
+            copies.append(
+                moved(g_ref.at[na, :, :, 1 - core], from_core.at[na], *sems(0), other_core)
+            )
+            if b1 > b0:
+                copies.append(
+                    moved(g_ref.at[nb, :, :, 1 - core], from_core.at[nb], *sems(1), other_core)
+                )
+        if phase == 1:
+            copies.append(moved(g_ref.at[na, 1 - y_at, :, core], from_y.at[na], *sems(2), other_y))
+            if b1 > b0:
+                for o in (1, 2, 3):
+                    copies.append(
+                        moved(
+                            g_ref.at[nb, :, z_next(o), core], from_zs.at[nbr, o - 1], *sems(2 + o),
+                            dp_device(y_at, z_next(o), core),
+                        )
+                    )
+        if phase == 2:
+            for o in (1, 2, 3):
+                copies.append(
+                    moved(
+                        g_ref.at[na, y_at, z_next(o), core], from_z.at[na, o - 1], *sems(5 + o),
+                        dp_device(y_at, z_next(o), core),
+                    )
+                )
+            if b1 > b0:
+                copies.append(
+                    moved(g_ref.at[nb, 1 - y_at, z_at, core], from_ys.at[nbr], *sems(9), other_y)
+                )
+        return copies
+
+    def dw_start(group, phase):
+        for copy in dw_copies(group, phase):
+            copy.start()
+
+    def dw_finish(group, phase):
+        for copy in dw_copies(group, phase):
+            copy.wait()
+        (a0, a1), (b0, b1) = group[1:]
+        if phase == 0:
+            for lo, hi in ((a0, a1), (b0, b1)):
+
+                def add(k, lo=lo):
+                    b, y = lo + k // 2, lax.rem(k, 2)
+                    mine = g_ref[b, y, :, core].astype(F32)
+                    g_ref[b, y, :, core] = (mine + from_core[b, y].astype(F32)).astype(BF)
+
+                pl.loop(0, 2 * (hi - lo))(add)
+        if phase == 1:
+
+            def add_a(b):
+                mine = g_ref[b, y_at, :, core].astype(F32)
+                g_ref[b, y_at, :, core] = (mine + from_y[b].astype(F32)).astype(BF)
+
+            def add_b(b):
+                total = g_ref[b, :, z_at, core].astype(F32)
+                for o in range(3):
+                    total = total + from_zs[b - 4, o].astype(F32)
+                g_ref[b, :, z_at, core] = total.astype(BF)
+
+            pl.loop(a0, a1)(add_a)
+            pl.loop(b0, b1)(add_b)
+        if phase == 2:
+
+            def last_a(b):
+                total = g_ref[b, y_at, z_at, core].astype(F32)
+                for o in range(3):
+                    total = total + from_z[b, o].astype(F32)
+                dw_ref[b] = total
+
+            def last_b(b):
+                dw_ref[b] = g_ref[b, y_at, z_at, core].astype(F32) + from_ys[b - 4].astype(F32)
+
+            pl.loop(a0, a1)(last_a)
+            pl.loop(b0, b1)(last_b)
+
+    FFN = (0, (1, 3), (5, 7))
+    ATTN = (1, (0, 1), (4, 5))
+    CROSS = (2, (3, 4), (4, 4))
+
+    def sm_copies(step):
+        sems = lambda k: (sm_send.at[k], sm_recv.at[k])
+        if step == 0:
+            return [
+                moved(sums_t.at[me], sums_t.at[me], *sems(o - 1), peer(o)) for o in range(1, TENSOR)
+            ]
+        if step == 1:
+            return [moved(sums.at[0], sums_c, *sems(3), other_core)]
+        if step == 2:
+            return [moved(sums.at[1], sums_y, *sems(4), other_y)]
+        return [
+            moved(
+                sums.at[2], sums_z.at[o - 1], *sems(4 + o), dp_device(y_at, z_next(o), core)
+            )
+            for o in (1, 2, 3)
+        ]
+
+    def sm_start(step):
+        for copy in sm_copies(step):
+            copy.start()
+
+    def sm_wait(step):
+        for copy in sm_copies(step):
+            copy.wait()
+
+    def small_norms():
+        sums_t[me] = jnp.zeros((16, D), F32)
+        for l in range(2):
+            for k in range(3):
+                a = acc[3 * l + k]
+                at = 2 * (3 * l + k)
+                sums_t[me, at : at + 1, :] = jnp.sum(jnp.where(is_word, a, 0.0), axis=0, keepdims=True)
+                sums_t[me, at + 1 : at + 2, :] = jnp.sum(
+                    jnp.where(is_word, 0.0, a), axis=0, keepdims=True
+                )
+        for k in range(3):
+            sums_t[me, 12 + k : 13 + k, :] = jnp.sum(acc[6 + k], axis=0, keepdims=True)
+        sm_start(0)
+
+    def small_biases():
+        sm_wait(0)
+        sums[0] = jnp.zeros((24, D), F32)
+        sums[0, :16] = sums_t[0] + sums_t[1] + sums_t[2] + sums_t[3]
+        for mod in range(2):
+            sums[0, 16 + mod : 17 + mod, :] = bsum[mod]
+        for k in range(3):
+            sums[0, 18 + k : 19 + k, : 3 * HW] = bqsum[k]
+        sm_start(1)
+
+    def small_y():
+        sm_wait(1)
+        sums[1] = sums[0] + sums_c[...]
+        sm_start(2)
+
+    def small_z():
+        sm_wait(2)
+        sums[2] = sums[1] + sums_y[...]
+        sm_start(3)
+
+    def small_last():
+        sm_wait(3)
+        s_ref[...] = sums[2] + sums_z[0] + sums_z[1] + sums_z[2]
+
+    def packet():
+        return moved(pack.at[0], pack.at[1], pk_send, pk_recv, partner)
 
     def each(*steps):
         def body(m):
@@ -436,7 +621,19 @@
         each(turn)
 
     each(back_f)
+
+    @pl.when(head)
+    def _():
+        ffn_outer()
+        dw_start(FFN, 0)
+
     each(back_g)
+
+    @pl.when(head)
+    def _():
+        dw_finish(FFN, 0)
+        dw_start(FFN, 1)
+
     each(back_h)
 
     @pl.when(head)
@@ -445,42 +642,72 @@
             ybuf[m, own] = (res[m] + rs_finish(m)).astype(BF)
             ag_start(ybuf, m, y_send, y_recv)
 
+        attn_outer()
+        dw_start(ATTN, 0)
+        small_norms()
         each(last)
-        g_ref[6] = jnp.zeros(g_ref.shape[1:], BF)
+        dw_finish(FFN, 1)
+        dw_start(FFN, 2)
+        small_biases()
+        dw_finish(ATTN, 0)
+        dw_start(ATTN, 1)
+        small_y()
+        small_z()
 
     @pl.when(cross)
     def _():
         each(cross_back_a)
         each(cross_back_b)
         each(cross_back_c)
+        ffn_outer()
+        dw_start(FFN, 0)
+        small_norms()
+        attn_outer()
+        dw_start(ATTN, 0)
+        dw_finish(FFN, 0)
+        dw_start(FFN, 1)
+        small_biases()
         cross_outer()
-
-    ffn_outer()
-    attn_outer()
+        dw_start(CROSS, 0)
+        dw_finish(ATTN, 0)
+        dw_start(ATTN, 1)
+        small_y()
+        dw_finish(CROSS, 0)
+        dw_start(CROSS, 1)
+        small_z()
+        dw_finish(FFN, 1)
+        dw_start(FFN, 2)
 
     def write(m):
         ag_finish(ybuf, m, y_send, y_recv)
         y_ref[m] = ybuf[m]
 
     each(write)
+    small_last()
+    dw_finish(FFN, 2)
+    dw_finish(ATTN, 1)
+    dw_start(ATTN, 2)
 
     @pl.when(cross)
     def _():
         each(lambda m: sec_copy(back, m).wait_send())
-
-    s_ref[...] = jnp.zeros_like(s_ref)
-    for l in range(2):
-        for k in range(3):
-            a = acc[3 * l + k]
-            at = 2 * (3 * l + k)
-            s_ref[at : at + 1, :] = jnp.sum(jnp.where(is_word, a, 0.0), axis=0, keepdims=True)
-            s_ref[at + 1 : at + 2, :] = jnp.sum(jnp.where(is_word, 0.0, a), axis=0, keepdims=True)
-    for k in range(3):
-        s_ref[12 + k : 13 + k, :] = jnp.sum(acc[6 + k], axis=0, keepdims=True)
-    for mod in range(2):
-        s_ref[16 + mod : 17 + mod, :] = bsum[mod]
-    for k in range(3):
-        s_ref[18 + k : 19 + k, : 3 * HW] = bqsum[k]
+        dw_finish(CROSS, 1)
+        dw_start(CROSS, 2)
+        dw_finish(CROSS, 2)
+        pack[0, :24] = dw_ref[3, :24]
+        pack[0, 24:] = s_ref[...]
+        packet().start()
+        dc_ref[...] = dw_ref[3, 24:]
+        sc_ref[...] = s_ref[...]
+        packet().wait_send()
+
+    dw_finish(ATTN, 2)
+
+    @pl.when(head)
+    def _():
+        packet().wait_recv()
+        dc_ref[...] = pack[1, :24]
+        sc_ref[...] = pack[1, 24:]
 
 
 def local(
@@ -525,15 +752,17 @@
     vmem = pl.BlockSpec(memory_space=pltpu.VMEM)
     mb_rows = lambda width, dtype: pltpu.VMEM((MB, R, width), dtype)
     own_rows = lambda count: pltpu.VMEM((count, MB, C, D), F32)
-    y, g, s = pl.pallas_call(
+    y, g, s, dc, sc = pl.pallas_call(
         kernel,
         out_shape=(
             jax.ShapeDtypeStruct((MB, R, D), BF),
-            jax.ShapeDtypeStruct((7, 2, 4, 2, 48, D), BF),
+            jax.ShapeDtypeStruct((7, 48, D), F32),
+            jax.ShapeDtypeStruct((24, D), F32),
+            jax.ShapeDtypeStruct((24, D), F32),
             jax.ShapeDtypeStruct((24, D), F32),
         ),
         in_specs=[vmem] * len(inputs),
-        out_specs=[vmem] * 3,
+        out_specs=[vmem] * 5,
         scratch_shapes=[
             mb_rows(D, BF),
             pltpu.VMEM((MB, TENSOR - 1, C, D), BF),
@@ -559,45 +788,60 @@
             pltpu.VMEM((6, C, D), F32),
             pltpu.VMEM((2, 1, D), F32),
             pltpu.VMEM((3, 1, 3 * HW), F32),
+            pltpu.VMEM((7, 2, 4, 2, 48, D), BF),
+            pltpu.VMEM((7, 2, 4, 48, D), BF),
+            pltpu.VMEM((4, 4, 48, D), BF),
+            pltpu.VMEM((3, 3, 2, 48, D), BF),
+            pltpu.VMEM((4, 3, 48, D), BF),
+            pltpu.VMEM((3, 48, D), BF),
+            pltpu.VMEM((2, 16, 24, D), F32),
+            pltpu.VMEM((3, 24, D), F32),
+            pltpu.VMEM((TENSOR, 16, D), F32),
+            pltpu.VMEM((24, D), F32),
+            pltpu.VMEM((24, D), F32),
+            pltpu.VMEM((3, 24, D), F32),
+            pltpu.VMEM((2, 48, D), F32),
             *[pltpu.SemaphoreType.DMA((MB, TENSOR - 1)) for _ in range(6)],
             pltpu.SemaphoreType.DMA((MB,)),
             pltpu.SemaphoreType.DMA((MB,)),
+            pltpu.SemaphoreType.DMA((3, 10)),
+            pltpu.SemaphoreType.DMA((3, 10)),
+            pltpu.SemaphoreType.DMA((8,)),
+            pltpu.SemaphoreType.DMA((8,)),
+            pltpu.SemaphoreType.DMA,
+            pltpu.SemaphoreType.DMA,
         ],
         compiler_params=pltpu.CompilerParams(
             collective_id=0, has_side_effects=True, vmem_limit_bytes=60 * 2**20
         ),
     )(*inputs)
 
-    g = g.reshape(7, D, D)
-    layer = lax.psum_scatter(g[:6], "dp", scatter_dimension=1, tiled=True).astype(F32)
-    s_dp = lax.psum(s, "dp")
-    s_all = lax.psum(s_dp[:16], "tensor")
     dp = lax.axis_index("dp")
     both = lax.axis_index("section") * 16 + dp
 
     def part(a, index, width):
         return lax.dynamic_slice_in_dim(a, index * width, width, axis=a.ndim - 1)
 
-    qkv_g = layer[:2, :, : 3 * HW].reshape(1, 2, 48, 3, HW)
-    out_g = jnp.swapaxes(layer[:2, :, 3 * HW :], 1, 2)[None]
-    in_g = layer[2:6:2][None]
-    ffo_g = jnp.swapaxes(layer[3:6:2], 1, 2)[None]
-    qb = s_dp[18:21, : 3 * HW].reshape(3, 3, LOCAL_HEADS, HEAD_DIM)[:, 0::2]
-    qv_bias_g = part(qb[:2], dp, 4)[None]
-    b1_g = part(s_dp[16:18].reshape(2, 6, 128), dp, 8)[None]
-    small = part(s_all[:12].reshape(2, 3, 2, D), dp, 48)
+    def pair(k):
+        return jnp.stack([g[k], g[k + 4]])
+
+    qkv_g = pair(0)[:, :, : 3 * HW].reshape(1, 2, 48, 3, HW)
+    out_g = jnp.swapaxes(pair(0)[:, :, 3 * HW :], 1, 2)[None]
+    in_g = pair(1)[None]
+    ffo_g = jnp.swapaxes(pair(2), 1, 2)[None]
+    qb = s[18:20, : 3 * HW].reshape(2, 3, LOCAL_HEADS, HEAD_DIM)[:, 0::2]
+    qv_bias_g = part(qb, dp, 4)[None]
+    b1_g = part(s[16:18].reshape(2, 6, 128), dp, 8)[None]
+    small = part(s[:12].reshape(2, 3, 2, D), dp, 48)
     gain_g, shift_g, obias_g = (jnp.swapaxes(small[:, k], 0, 1)[None] for k in range(3))
 
-    c = lax.psum(g[6].astype(F32), ("section", "dp"))
-    c = lax.dynamic_slice_in_dim(c, both * 24, 24, axis=0)
-    cs = lax.psum(s_all[12:15], "section")
-    cqb = lax.psum(qb[2], "section")
-    c_small = part(cs, both, 24)
+    cqb = sc[20, : 3 * HW].reshape(3, LOCAL_HEADS, HEAD_DIM)[0::2]
+    c_small = part(sc[12:15], both, 24)
     word_rows = y[:, : ITEMS_MB * WORDS].reshape(1, ITEMS_LOCAL, WORDS, D).astype(F32)
     region_rows = y[:, RW : RW + ITEMS_MB * REGIONS].reshape(1, ITEMS_LOCAL, REGIONS, D).astype(F32)
     return (
         word_rows, region_rows, qkv_g, qv_bias_g, out_g, in_g, b1_g, ffo_g, obias_g, gain_g, shift_g,
-        c[:, : 3 * HW].reshape(24, 3, HW), part(cqb, both, 2), c[:, 3 * HW :].T,
+        dc[:, : 3 * HW].reshape(24, 3, HW), part(cqb, both, 2), dc[:, 3 * HW :].T,
         c_small[2], c_small[0], c_small[1],
     )
 

time: 522 us -> 246 us (0.47)
  waiting for transfers between devices: 240 us -> 0 us
  blocking collectives: 29.4 us -> 0 us
  Pallas kernels: 195 us -> 213 us
  between operations: 14.1 us -> 0.87 us
  local copies, waits for them, and re-layouts: 36.2 us -> 25.2 us
    psum x2 -> x0, waiting for transfers between devices: 168 us -> none  [the longest x1 91.1 us: local(): s_dp = lax.psum(s, 'dp')]
    reduce_scatter x1 -> x0, waiting for transfers between devices: 71.6 us -> none  [local(): lax.psum_scatter(g[:6], 'dp', scatter_dimension=1, tiled=True).astype(F32)]
    psum x2 -> x0, blocking collectives: 29.4 us -> none  [the longest x1 17.3 us: local(): s_all = lax.psum(s_dp[:16], 'tensor')]
    pallas_call x1, Pallas kernels: 195 us -> 213 us  [local(): pl.pallas_call(kernel, out_shape=(jax.ShapeDtypeStruct((MB, R, D), BF), j...]
    slice x11 -> x9, local copies, waits for them, and re-layouts: 10.9 us -> 2.82 us  [the longest x1 1.31 us: pair(): return jnp.stack([g[k], g[k + 4]])]
    unnamed x34 -> x36, local copies, waits for them, and re-layouts: 10.6 us -> 10.6 us
  transfers between devices with their start and end apart: 3 -> 0, of which waited for: 3 -> 0; matrix products, arithmetic and copies ran while one was open for 4% -> 0% of each run, Pallas kernels for 0% -> 0%
where the time goes in v1:
time: 246 us
  Pallas kernels  213 us (87%)
  local copies, waits for them, and re-layouts  25.2 us (10%)
  other arithmetic  6.38 us (3%)
    pallas_call x1, Pallas kernels, local(): pl.pallas_call(kernel, out_shape=(jax.ShapeDtypeStruct((MB, R, D), BF), j...  213 us
    unnamed x36, local copies, waits for them, and re-layouts  10.6 us

profile of v1, /device:TPU:0, one launch (start us, length us, event | category | flops | bytes accessed | tf_op | source)
XLA Modules:
  0.0 245.6 jit_solution(14828160748192391058)
XLA Ops:
  0.7 0.8 copy.106
  1.4 0.7 copy.107
  2.1 0.7 copy.108
  2.9 1.3 concatenate.18.vec_ref
  4.1 0.7 copy.75
  5.0 0.6 pad_maximum_fusion.2.bqkv_ref
  5.6 0.8 slice_reduce_fusion.2
  7.1 0.7 compare_select_fusion.1
  8.3 0.9 copy.80.scale_ref
  9.2 1.1 copy.74
  10.5 0.9 fusion.2.x_ref
  11.5 0.6 copy-done
  12.1 2.2 copy.81.wqkv_ref
  14.3 1.4 copy.83.cwqkv_ref
  15.7 0.6 pad_maximum_fusion.1.cvec_ref
  16.7 0.6 pad_convert_fusion.valid_ref
  17.3 0.6 copy.82.b1_ref
  17.9 213.2 %shard_map.314 = (bf16[4,128,768]{2,1,0:T(8,128)(2,1)}, f32[7,48,768]{2,1,0:T(8,128)}, f32[24,768]{1,0:T(8,128)}, f32[24,768]{1,0:T(8,128)}, f32[24,768]{1,0:T(8,128)}) custom-call(bf16[4,128,768]{2,1,0:T(8,128)(2,1)} %fusion.2.x_ref, f32[4,128,1]{2,1,0:T(8,128)} %copy.80.scale_ref, f32[4,1,48]{2,1,0:T(1,128)} %pad_convert_fusion.valid_ref, ...), custom_call_target="tpu_custom_call" | custom-call | tf_op jit(solution)/shard_map/pallas_call | solution.py:755
  231.0 1.3 fusion.6
  232.4 0.7 fusion.4
  233.3 0.8 copy.90
  234.1 0.7 maximum_bitcast_fusion.1
  234.8 0.7 maximum_bitcast_fusion
  235.5 0.7 slice.146
  236.9 0.7 slice_reduce_fusion
  237.8 0.7 copy.97
  240.5 0.6 copy.110
  241.2 0.6 copy.109
  242.0 1.2 copy.89
  243.3 0.9 copy.88
  244.3 0.6 copy.91
  244.9 0.7 slice_bitcast_fusion
  (75 shorter events, 5.5 us)
Async XLA Ops:
  0.7 9.8 %copy-start.3 = (bf16[1,8,20,768]{3,1,2,0:T(8,128)(2,1)S(1)}, bf16[1,8,20,768]{3,1,2,0:T(8,128)(2,1)}, u32[]{:S(2)}) copy-start(bf16[1,8,20,768]{3,1,2,0:T(8,128)(2,1)} %param.19) | copy-start | bytes 737284
  10.3 1.8 copy-start
  12.1 2.3 copy-start.1
  14.3 1.4 copy-start.7
  14.3 1.4 copy-start.8
  14.3 1.4 copy-start.9
  14.3 2.0 copy-start.10
  14.3 3.0 %copy-start.6 = (f32[1,2,6,128]{3,1,2,0:T(2,128)S(1)}, f32[1,2,6,128]{3,1,2,0:T(2,128)}, u32[]{:S(2)}) copy-start(f32[1,2,6,128]{3,1,2,0:T(2,128)} %param.27) | copy-start | bytes 18436
  233.1 5.4 %copy-start.5 = (f32[24,768]{1,0:T(8,128)S(1)}, f32[24,768]{1,0:T(8,128)}, u32[]{:S(2)}) copy-start(f32[24,768]{1,0:T(8,128)} %get-tuple-element.24) | copy-start | bytes 221188
  233.1 8.7 %copy-start.2 = (bf16[4,128,768]{2,1,0:T(8,128)(2,1)S(1)}, bf16[4,128,768]{2,1,0:T(8,128)(2,1)}, u32[]{:S(2)}) copy-start(bf16[4,128,768]{2,1,0:T(8,128)(2,1)} %get-tuple-element.22) | copy-start | bytes 2359300
  243.2 1.0 copy-start.4

commit v2 on v1

--- a/solution.py
+++ b/solution.py
@@ -73,13 +73,25 @@
     return item
 
 
-def key_mask(q_rows, q_len, k_rows, k_len, key_valid):
+def spread(rows, length, transposed=False):
+    count = ITEMS_LOCAL * length
+    shape = (count, MB * rows) if transposed else (MB * rows, count)
+    at = lax.broadcasted_iota(jnp.int32, shape, 0 if transposed else 1)
+    padded = lax.broadcasted_iota(jnp.int32, shape, 1 if transposed else 0)
+    item, position = at & (ITEMS_LOCAL - 1), at >> 3
+    block, within = item >> (ITEMS_MB.bit_length() - 1), item & (ITEMS_MB - 1)
+    target = block * rows + within * length + position
+    return (target == padded).astype(F32).astype(BF)
+
+
+def key_mask(q_rows, q_len, k_rows, k_len, lengths=None):
     shape = (q_rows, k_rows)
-    same = item_of(shape, 0, q_len) == item_of(shape, 1, k_len)
-    inside = lax.broadcasted_iota(jnp.int32, shape, 1) < ITEMS_MB * k_len
-    mask = same & inside
-    if key_valid is not None:
-        mask = mask & (jnp.broadcast_to(key_valid, shape) > 0.5)
+    item = item_of(shape, 1, k_len)
+    key = lax.broadcasted_iota(jnp.int32, shape, 1)
+    mask = (item_of(shape, 0, q_len) == item) & (key < ITEMS_MB * k_len)
+    if lengths is not None:
+        for k, length in enumerate(lengths):
+            mask = mask & ((item != k) | (key < k * k_len + length))
     return mask
 
 
@@ -119,10 +131,11 @@
 
 
 def kernel(
-    x_ref, scale_ref, valid_ref, wqkv_ref, bqkv_ref, wo_ref, w1_ref, b1_ref, w2_ref, vec_ref,
-    cwqkv_ref, cbqkv_ref, cwo_ref, cvec_ref,
+    words_ref, regions_ref, lengths_ref, flags_ref, wqkv_ref, qv_bias_ref, wo_ref, w1_ref, b1_in_ref,
+    w2_ref, out_bias_ref, gain_ref, shift_ref, cwqkv_ref, cqv_bias_ref, cwo_ref, cout_bias_ref,
+    cgain_ref, cshift_ref,
     y_ref, dw_ref, s_ref, dc_ref, sc_ref,
-    send, recv, xlow, midf, alow, dyf, dya, dyc, ybuf, back,
+    x_ref, bqkv_ref, b1_ref, cvec_ref, send, recv, xlow, midf, alow, dyf, dya, dyc, ybuf, back,
     qkv, mixed, dqkv, cqkv, cmixed, cdqkv, act, dup, dgelu,
     p_w, p_r, cp_w, cp_r, cur, res, nrm, rstd, acc, rowp, bsum, bqsum,
     g_ref, from_core, from_y, from_zs, from_z, from_ys, wide, sums, sums_t, sums_c, sums_y, sums_z, pack,
@@ -162,8 +175,27 @@
 
     row = lax.broadcasted_iota(jnp.int32, (C, 1), 0) + me * C
     is_word = row < RW
-    for k in range(6):
-        rowp[k] = jnp.where(is_word, vec_ref[2 * k : 2 * k + 1, :], vec_ref[2 * k + 1 : 2 * k + 2, :])
+    for k, ref in enumerate((out_bias_ref, gain_ref, shift_ref)):
+        for l in range(2):
+            rowp[2 * k + l] = jnp.where(is_word, ref[0, 0, l : l + 1, :], ref[0, 1, l : l + 1, :])
+
+    def side_by_side(rows):
+        return jnp.concatenate(rows, axis=1)
+
+    for mod in range(2):
+        b1_ref[mod] = side_by_side(
+            [b1_in_ref[0, k, mod : mod + 1, :] for k in range(D // 128)]
+        )
+    for k, ref in enumerate((qv_bias_ref.at[0, 0], qv_bias_ref.at[0, 1], cqv_bias_ref)):
+        heads = lambda j: [ref[h, j : j + 1, :] for h in range(LOCAL_HEADS)]
+        bqkv_ref[k] = side_by_side([*heads(0), jnp.zeros((1, HW), F32), *heads(1)])
+    for k, ref in enumerate((cout_bias_ref, cgain_ref, cshift_ref)):
+        cvec_ref[k : k + 1, :] = ref[...].reshape(1, D)
+
+    for ref, (lo, hi), length in zip((words_ref, regions_ref), SPANS, (WORDS, REGIONS)):
+        given = ref[0].astype(F32).reshape(ITEMS_LOCAL * length, D).astype(BF)
+        placed = dot(spread(hi - lo, length), given).astype(BF)
+        x_ref[:, lo:hi, :] = placed.reshape(MB, hi - lo, D)
     acc[...] = jnp.zeros_like(acc)
     bsum[...] = jnp.zeros_like(bsum)
     bqsum[...] = jnp.zeros_like(bqsum)
@@ -241,10 +273,12 @@
         return low
 
     def word_keys(m, q_rows, q_len):
-        return key_mask(q_rows, q_len, RW, WORDS, valid_ref[m])
+        return key_mask(
+            q_rows, q_len, RW, WORDS, [lengths_ref[ITEMS_MB * m + k] for k in range(ITEMS_MB)]
+        )
 
     def region_keys(q_rows, q_len):
-        return key_mask(q_rows, q_len, RR, REGIONS, None)
+        return key_mask(q_rows, q_len, RR, REGIONS)
 
     def cross_a(m):
         sec_copy(midf, m).wait_recv()
@@ -252,7 +286,7 @@
 
     def cross_b(m):
         ag_finish(midf, m)
-        out = dot(midf[m], cwqkv_ref[...]) + cbqkv_ref[...]
+        out = dot_nt(midf[m], cwqkv_ref[...]) + bqkv_ref[2]
         out = out.astype(BF)
         q, k, v = out[:, :HW], out[:, HW : 2 * HW], out[:, 2 * HW :]
         cqkv[0, m], cqkv[1, m], cqkv[2, m] = q, k, v
@@ -284,7 +318,7 @@
             ag_finish(xlow, m)
 
         for mod, (lo, hi) in enumerate(SPANS):
-            out = (dot(xlow[m, lo:hi], wqkv_ref[mod]) + bqkv_ref[mod]).astype(BF)
+            out = (dot_nt(xlow[m, lo:hi], wqkv_ref[mod]) + bqkv_ref[mod]).astype(BF)
             q, k, v = out[:, :HW], out[:, HW : 2 * HW], out[:, 2 * HW :]
             qkv[0, m, lo:hi], qkv[1, m, lo:hi], qkv[2, m, lo:hi] = q, k, v
             if mod == 0:
@@ -353,7 +387,7 @@
             d = jnp.concatenate(parts, axis=1)
             dqkv[m, lo:hi] = d
             bqsum[mod] += jnp.sum(d.astype(F32), axis=0, keepdims=True)
-            send[m, lo:hi] = dot_nt(d, wqkv_ref[mod]).astype(BF)
+            send[m, lo:hi] = dot(d, wqkv_ref[mod]).astype(BF)
         rs_start(m)
 
     def cross_back_a(m):
@@ -372,7 +406,7 @@
         cdqkv[m, RW:] = jnp.concatenate([dq_r, dk_r, dv_r], axis=1)
         d = cdqkv[m]
         bqsum[2] += jnp.sum(d.astype(F32), axis=0, keepdims=True)
-        send[m] = dot_nt(d, cwqkv_ref[...]).astype(BF)
+        send[m] = dot(d, cwqkv_ref[...]).astype(BF)
         rs_start(m)
 
     def cross_back_c(m):
@@ -612,11 +646,19 @@
 
     @pl.when(cross)
     def _():
+        def scales(m, flag, first, later):
+            value = jnp.where(flags_ref[ITEMS_MB * m] == flag, 0.25, 1.0)
+            scale = jnp.full((C, 1), value, F32)
+            for k in range(1, ITEMS_MB):
+                value = jnp.where(flags_ref[ITEMS_MB * m + k] == flag, 0.25, 1.0)
+                scale = jnp.where(row >= first + k * later, value, scale)
+            return scale
+
         def turn(m):
             h = layer_d(m)
-            back_e(m, x_ref[m, own].astype(F32) * scale_ref[m, own])
+            scale = jnp.where(is_word, scales(m, 1, 0, WORDS), scales(m, 0, RW, REGIONS))
+            back_e(m, x_ref[m, own].astype(F32) * scale)
             ybuf[m, own] = h.astype(BF)
-            ag_start(ybuf, m, y_send, y_recv)
 
         each(turn)
 
@@ -646,12 +688,12 @@
         dw_start(ATTN, 0)
         small_norms()
         each(last)
+        small_biases()
         dw_finish(FFN, 1)
+        small_y()
         dw_start(FFN, 2)
-        small_biases()
         dw_finish(ATTN, 0)
         dw_start(ATTN, 1)
-        small_y()
         small_z()
 
     @pl.when(cross)
@@ -659,6 +701,7 @@
         each(cross_back_a)
         each(cross_back_b)
         each(cross_back_c)
+        each(lambda m: ag_start(ybuf, m, y_send, y_recv))
         ffn_outer()
         dw_start(FFN, 0)
         small_norms()
@@ -683,10 +726,10 @@
         y_ref[m] = ybuf[m]
 
     each(write)
-    small_last()
     dw_finish(FFN, 2)
     dw_finish(ATTN, 1)
     dw_start(ATTN, 2)
+    small_last()
 
     @pl.when(cross)
     def _():
@@ -710,46 +753,77 @@
         sc_ref[...] = pack[1, 24:]
 
 
+def arrange(
+    y_ref, dw_ref, s_ref, dc_ref, sc_ref,
+    words, regions, qkv_g, qv_bias_g, out_g, in_g, b1_g, ffo_g, obias_g, gain_g, shift_g,
+    cqkv_g, cqv_bias_g, cout_g, cobias_g, cgain_g, cshift_g,
+):
+    place = lax.axis_index("dp")
+    both = lax.axis_index("section") * 16 + place
+
+    def from_column(rows, column):
+        return pltpu.roll(rows, lax.rem(D - column, D), 1)
+
+    for ref, (lo, hi), length in zip((words, regions), SPANS, (WORDS, REGIONS)):
+        padded = y_ref[:, lo:hi, :].reshape(MB * (hi - lo), D)
+        rows = dot(spread(hi - lo, length, True), padded)
+        ref[0] = rows.reshape(length, ITEMS_LOCAL, D)
+    small = s_ref[...]
+    for mod in range(2):
+        attn = dw_ref[4 * mod]
+        for j in range(3):
+            qkv_g[0, mod, j] = attn[:, j * HW : (j + 1) * HW]
+        out_g[0, mod] = attn[:, 3 * HW :]
+        in_g[0, mod] = dw_ref[4 * mod + 1]
+        ffo_g[0, mod] = dw_ref[4 * mod + 2]
+    columns = from_column(small, 48 * place)[:, :48]
+    for mod in range(2):
+        for l in range(2):
+            for k, ref in enumerate((gain_g, shift_g, obias_g)):
+                at = 2 * (3 * l + k) + mod
+                ref[0, mod, l : l + 1, :] = columns[at : at + 1]
+    columns = from_column(small, 8 * place)
+    for mod in range(2):
+        for k in range(6):
+            b1_g[0, k, mod : mod + 1, :] = columns[16 + mod : 17 + mod, 128 * k : 128 * k + 8]
+    columns = from_column(small, 4 * place)
+    for mod in range(2):
+        for j in range(2):
+            for h in range(LOCAL_HEADS):
+                lo = 2 * j * HW + h * HEAD_DIM
+                qv_bias_g[0, mod, h, j : j + 1, :] = columns[18 + mod : 19 + mod, lo : lo + 4]
+    wide = dc_ref[...]
+    for j in range(3):
+        cqkv_g[j] = wide[:, j * HW : (j + 1) * HW]
+    cout_g[...] = wide[:, 3 * HW :]
+    small = sc_ref[...]
+    columns = from_column(small, 24 * both)
+    for k, ref in enumerate((cgain_g, cshift_g, cobias_g)):
+        ref[...] = columns[12 + k, :24]
+    columns = from_column(small, 2 * both)[20:21]
+    for j in range(2):
+        heads = []
+        for h in range(LOCAL_HEADS):
+            lo = 2 * j * HW + h * HEAD_DIM
+            heads.append(columns[:, lo : lo + 2])
+        cqv_bias_g[j] = jnp.concatenate(heads, axis=0).T
+
+
 def local(
     words, regions, word_lengths, task_flags, attn_qkv, attn_qv_bias, attn_out, ffn_in, ffn_in_bias,
     ffn_out, out_bias, norm_gain, norm_bias, cross_qkv, cross_qv_bias, cross_out, cross_out_bias,
     cross_norm_gain, cross_norm_bias,
 ):
-    def rows(w, r):
-        w = w.reshape(MB, ITEMS_MB * WORDS, -1)
-        r = r.reshape(MB, ITEMS_MB * REGIONS, -1)
-        w = jnp.pad(w, ((0, 0), (0, RW - w.shape[1]), (0, 0)))
-        r = jnp.pad(r, ((0, 0), (0, RR - r.shape[1]), (0, 0)))
-        return jnp.concatenate([w, r], axis=1)
-
-    x = rows(words[0], regions[0])
-    word_scale = jnp.where(task_flags == 1, 0.25, 1.0).astype(F32)
-    region_scale = jnp.where(task_flags == 0, 0.25, 1.0).astype(F32)
-    scale = rows(
-        jnp.broadcast_to(word_scale[:, None], (ITEMS_LOCAL, WORDS)),
-        jnp.broadcast_to(region_scale[:, None], (ITEMS_LOCAL, REGIONS)),
+    inputs = (
+        words.transpose(0, 2, 1, 3), regions.transpose(0, 2, 1, 3), word_lengths, task_flags,
+        attn_qkv.transpose(0, 1, 3, 4, 2).reshape(2, 3 * HW, D), attn_qv_bias.transpose(0, 1, 3, 2, 4), attn_out[0],
+        ffn_in[0], ffn_in_bias.transpose(0, 2, 1, 3), ffn_out[0], out_bias, norm_gain, norm_bias,
+        cross_qkv.transpose(1, 2, 0).reshape(3 * HW, D), cross_qv_bias.transpose(1, 0, 2), cross_out,
+        cross_out_bias, cross_norm_gain, cross_norm_bias,
     )
-    valid = (jnp.arange(WORDS)[None, :] < word_lengths[:, None]).astype(F32)
-    valid = valid.reshape(MB, 1, ITEMS_MB * WORDS)
-    valid = jnp.pad(valid, ((0, 0), (0, 0), (0, RW - ITEMS_MB * WORDS)))
-
-    def qkv_bias(b):
-        b = b.reshape(*b.shape[:-3], 2, HW)
-        return jnp.concatenate(
-            [b[..., 0:1, :], jnp.zeros_like(b[..., 0:1, :]), b[..., 1:2, :]], axis=-1
-        )
-
-    vec = jnp.concatenate(
-        [a[0][:, k] for a in (out_bias, norm_gain, norm_bias) for k in range(2)], axis=0
-    )
-    cvec = jnp.stack([cross_out_bias, cross_norm_gain, cross_norm_bias])
-    inputs = (
-        x, scale, valid, attn_qkv[0].reshape(2, D, 3 * HW), qkv_bias(attn_qv_bias[0]), attn_out[0],
-        ffn_in[0], ffn_in_bias[0].reshape(2, 1, D), ffn_out[0], vec,
-        cross_qkv.reshape(D, 3 * HW), qkv_bias(cross_qv_bias), cross_out, cvec,
-    )
 
     vmem = pl.BlockSpec(memory_space=pltpu.VMEM)
+    smem = pl.BlockSpec(memory_space=pltpu.SMEM)
     mb_rows = lambda width, dtype: pltpu.VMEM((MB, R, width), dtype)
     own_rows = lambda count: pltpu.VMEM((count, MB, C, D), F32)
     y, g, s, dc, sc = pl.pallas_call(
@@ -761,9 +835,13 @@
             jax.ShapeDtypeStruct((24, D), F32),
             jax.ShapeDtypeStruct((24, D), F32),
         ),
-        in_specs=[vmem] * len(inputs),
+        in_specs=[smem if k in (2, 3) else vmem for k in range(len(inputs))],
         out_specs=[vmem] * 5,
         scratch_shapes=[
+            mb_rows(D, BF),
+            pltpu.VMEM((3, 1, 3 * HW), F32),
+            pltpu.VMEM((2, 1, D), F32),
+            pltpu.VMEM((3, D), F32),
             mb_rows(D, BF),
             pltpu.VMEM((MB, TENSOR - 1, C, D), BF),
             *[mb_rows(D, BF) for _ in range(8)],
@@ -816,34 +894,24 @@
         ),
     )(*inputs)
 
-    dp = lax.axis_index("dp")
-    both = lax.axis_index("section") * 16 + dp
-
-    def part(a, index, width):
-        return lax.dynamic_slice_in_dim(a, index * width, width, axis=a.ndim - 1)
-
-    def pair(k):
-        return jnp.stack([g[k], g[k + 4]])
-
-    qkv_g = pair(0)[:, :, : 3 * HW].reshape(1, 2, 48, 3, HW)
-    out_g = jnp.swapaxes(pair(0)[:, :, 3 * HW :], 1, 2)[None]
-    in_g = pair(1)[None]
-    ffo_g = jnp.swapaxes(pair(2), 1, 2)[None]
-    qb = s[18:20, : 3 * HW].reshape(2, 3, LOCAL_HEADS, HEAD_DIM)[:, 0::2]
-    qv_bias_g = part(qb, dp, 4)[None]
-    b1_g = part(s[16:18].reshape(2, 6, 128), dp, 8)[None]
-    small = part(s[:12].reshape(2, 3, 2, D), dp, 48)
-    gain_g, shift_g, obias_g = (jnp.swapaxes(small[:, k], 0, 1)[None] for k in range(3))
-
-    cqb = sc[20, : 3 * HW].reshape(3, LOCAL_HEADS, HEAD_DIM)[0::2]
-    c_small = part(sc[12:15], both, 24)
-    word_rows = y[:, : ITEMS_MB * WORDS].reshape(1, ITEMS_LOCAL, WORDS, D).astype(F32)
-    region_rows = y[:, RW : RW + ITEMS_MB * REGIONS].reshape(1, ITEMS_LOCAL, REGIONS, D).astype(F32)
-    return (
-        word_rows, region_rows, qkv_g, qv_bias_g, out_g, in_g, b1_g, ffo_g, obias_g, gain_g, shift_g,
-        dc[:, : 3 * HW].reshape(24, 3, HW), part(cqb, both, 2), dc[:, 3 * HW :].T,
-        c_small[2], c_small[0], c_small[1],
+    shapes = (
+        (1, WORDS, ITEMS_LOCAL, D), (1, REGIONS, ITEMS_LOCAL, D), (1, 2, 3, 48, HW),
+        (1, 2, LOCAL_HEADS, 2, 4), (1, 2, 48, HW), (1, 2, 48, D), (1, 6, 2, 8), (1, 2, 48, D),
+        (1, 2, 2, 48), (1, 2, 2, 48), (1, 2, 2, 48), (3, 24, HW), (2, 2, LOCAL_HEADS), (24, HW),
+        (24,), (24,), (24,),
     )
+    orders = {
+        0: (0, 2, 1, 3), 1: (0, 2, 1, 3), 2: (0, 1, 3, 2, 4), 3: (0, 1, 3, 2, 4), 4: (0, 1, 3, 2),
+        6: (0, 2, 1, 3), 7: (0, 1, 3, 2), 11: (1, 0, 2), 12: (0, 2, 1), 13: (1, 0),
+    }
+    outs = pl.pallas_call(
+        arrange,
+        out_shape=tuple(jax.ShapeDtypeStruct(shape, F32) for shape in shapes),
+        in_specs=[vmem] * 5,
+        out_specs=[vmem] * len(shapes),
+        compiler_params=pltpu.CompilerParams(vmem_limit_bytes=60 * 2**20),
+    )(y, g, s, dc, sc)
+    return tuple(out.transpose(orders[k]) if k in orders else out for k, out in enumerate(outs))
 
 
 def solution(mesh):

time: 246 us -> 210 us (0.85)
  local copies, waits for them, and re-layouts: 25.2 us -> 0 us
  other arithmetic: 6.38 us -> 0 us
  Pallas kernels: 213 us -> 208 us
    unnamed x36 -> x0, local copies, waits for them, and re-layouts: 10.6 us -> none
    pallas_call x1, Pallas kernels: 213 us -> 205 us  [local(): pl.pallas_call(kernel, out_shape=(jax.ShapeDtypeStruct((MB, R, D), BF), j...]
    slice x14 -> x0, local copies, waits for them, and re-layouts: 3.85 us -> none  [the longest x1 1.31 us: pair(): return jnp.stack([g[k], g[k + 4]])]
    pallas_call x0 -> x1, Pallas kernels: none -> 3.27 us  [local(): pl.pallas_call(arrange, out_shape=tuple((jax.ShapeDtypeStruct(shape, F32)...]
    another operation x9 -> x0, local copies, waits for them, and re-layouts: 3.15 us -> none  [the longest x1 2.23 us: local(): attn_qkv[0].reshape(2, D, 3 * HW)]
where the time goes in v2:
time: 210 us; the launch traced here: 209 us
  Pallas kernels  208 us (99%)
    pallas_call x1, Pallas kernels, local(): pl.pallas_call(kernel, out_shape=(jax.ShapeDtypeStruct((MB, R, D), BF), j...  205 us

profile of v2, /device:TPU:0, one launch (start us, length us, event | category | flops | bytes accessed | tf_op | source)
XLA Modules:
  0.0 209.3 jit_solution(15048694317675554812)
XLA Ops:
  0.7 205.2 %shard_map.314 = (bf16[4,128,768]{2,1,0:T(8,128)(2,1)}, f32[7,48,768]{2,1,0:T(8,128)}, f32[24,768]{1,0:T(8,128)}, f32[24,768]{1,0:T(8,128)}, f32[24,768]{1,0:T(8,128)}) custom-call(bf16[1,20,8,768]{3,2,1,0:T(8,128)(2,1)} %bitcast.30, bf16[1,36,8,768]{3,2,1,0:T(8,128)(2,1)} %bitcast.29, s32[8]{0:T(128)} %lengths_ref.1, s32[8]{0:T(128)} %flags_ref.1, ...), custom_call_target="tpu_custom_call" | custom-call | tf_op jit(solution)/shard_map/pallas_call | solution.py:829
  205.9 3.3 %shard_map.315 = (f32[1,20,8,768]{3,2,1,0:T(8,128)}, f32[1,36,8,768]{3,2,1,0:T(8,128)}, f32[1,2,3,48,192]{4,3,2,1,0:T(8,128)}, f32[1,2,3,2,4]{4,3,2,1,0:T(2,128)...) custom-call(bf16[4,128,768]{2,1,0:T(8,128)(2,1)} %get-tuple-element., ...), custom_call_target="tpu_custom_call" | custom-call | tf_op jit(solution)/shard_map/pallas_call | solution.py:907

commit v3 on v2

--- a/solution.py
+++ b/solution.py
@@ -131,17 +131,21 @@
 
 
 def kernel(
-    words_ref, regions_ref, lengths_ref, flags_ref, wqkv_ref, qv_bias_ref, wo_ref, w1_ref, b1_in_ref,
-    w2_ref, out_bias_ref, gain_ref, shift_ref, cwqkv_ref, cqv_bias_ref, cwo_ref, cout_bias_ref,
+    words_ref, regions_ref, lengths_ref, flags_ref, wqkv_in, qv_bias_ref, wo_in, w1_in, b1_in_ref,
+    w2_in, out_bias_ref, gain_ref, shift_ref, cwqkv_in, cqv_bias_ref, cwo_in, cout_bias_ref,
     cgain_ref, cshift_ref,
     y_ref, dw_ref, s_ref, dc_ref, sc_ref,
     x_ref, bqkv_ref, b1_ref, cvec_ref, send, recv, xlow, midf, alow, dyf, dya, dyc, ybuf, back,
     qkv, mixed, dqkv, cqkv, cmixed, cdqkv, act, dup, dgelu,
     p_w, p_r, cp_w, cp_r, cur, res, nrm, rstd, acc, rowp, bsum, bqsum,
-    g_ref, from_core, from_y, from_zs, from_z, from_ys, wide, sums, sums_t, sums_c, sums_y, sums_z, pack,
+    wqkv_ref, wo_ref, w1_ref, w2_ref, cwqkv_ref, cwo_ref, wqkv_m, wo_m, w1_m, w2_m, cwqkv_m, cwo_m, bqkv_m, b1_m,
+    got, act_m, dup_m, mixed_m, dqkv_m, cmixed_m, cdqkv_m, cur_f, res_f, nrm_f, rstd_f, row_sums,
+    g_ref, from_core, from_y, from_zs, from_z, from_ys, sums, sums_t, sums_c, sums_y, sums_z, pack,
     rs_send, rs_recv, ag_send, ag_recv, y_send, y_recv, sec_send, sec_recv,
     dw_send, dw_recv, sm_send, sm_recv, pk_send, pk_recv,
+    back_send, back_recv, ar_send, ar_recv, mt_send, mt_recv, ga_send, ga_recv, ps_send, ps_recv, loads,
 ):
+    p = functools.partial
     sec = lax.axis_index("section")
     me = lax.axis_index("tensor")
     head = sec == 0
@@ -167,11 +171,36 @@
     def z_next(o):
         return lax.rem(z_at + o, 4)
 
+    weights = tuple(
+        pltpu.make_async_copy(src, dst, loads.at[k])
+        for k, (src, dst) in enumerate((
+            (wqkv_in, wqkv_ref), (wo_in, wo_ref), (w1_in, w1_ref), (w2_in, w2_ref),
+            (cwqkv_in, cwqkv_ref), (cwo_in, cwo_ref),
+        ))
+    )
+
+    def load_weights(*which):
+        for k in which:
+            weights[k].start()
+
+    def wait_weights(*which):
+        for k in which:
+            weights[k].wait()
+
     barrier = pltpu.get_barrier_semaphore()
     for o in range(1, TENSOR):
         pl.semaphore_signal(barrier, inc=1, device_id=peer(o), device_id_type=MESH)
-    for device in (partner, other_core, other_y, *(dp_device(y_at, z_next(o), core) for o in (1, 2, 3))):
+    mate, halver = {"tensor": me + 1 - 2 * lax.rem(me, 2)}, {"tensor": 3 - me}
+    set_of = lax.rem((me + 1) // 2, 2)
+    for t in range(TENSOR):
+        pl.semaphore_signal(
+            barrier, inc=1, device_id={"section": 1 - sec, "tensor": t}, device_id_type=MESH
+        )
+    for device in (other_core, other_y, *(dp_device(y_at, z_next(o), core) for o in (1, 2, 3))):
         pl.semaphore_signal(barrier, inc=1, device_id=device, device_id_type=MESH)
+
+    load_weights(0, 1, 2, 3)
+    pl.when(cross)(lambda: load_weights(4, 5))
 
     row = lax.broadcasted_iota(jnp.int32, (C, 1), 0) + me * C
     is_word = row < RW
@@ -199,8 +228,15 @@
     acc[...] = jnp.zeros_like(acc)
     bsum[...] = jnp.zeros_like(bsum)
     bqsum[...] = jnp.zeros_like(bqsum)
-
-    pl.semaphore_wait(barrier, 9)
+    row_sums[...] = jnp.zeros_like(row_sums)
+
+    pl.semaphore_wait(barrier, 12)
+
+    def moved(src, dst, send_sem, recv_sem, device):
+        return pltpu.make_async_remote_copy(
+            src_ref=src, dst_ref=dst, send_sem=send_sem, recv_sem=recv_sem, device_id=device,
+            device_id_type=MESH,
+        )
 
     def rs_copies(m):
         return [
@@ -248,15 +284,31 @@
         for copy in ag_copies(buf, m, ss, rs):
             copy.wait()
 
-    def sec_copy(buf, m):
-        return pltpu.make_async_remote_copy(
-            src_ref=buf.at[m, own],
-            dst_ref=buf.at[m, own],
-            send_sem=sec_send.at[m],
-            recv_sem=sec_recv.at[m],
-            device_id=partner,
-            device_id_type=MESH,
+    def mid_copy(m, k, t):
+        return moved(
+            midf.at[m, own], midf.at[m, own], sec_send.at[m, k], sec_recv.at[m, me],
+            {"section": 1 - sec, "tensor": t},
         )
+
+    def mid_arrive(m):
+        for t in range(TENSOR):
+            rows = midf.at[m, pl.ds(t * C, C)]
+            moved(rows, rows, sec_send.at[m, 0], sec_recv.at[m, t], partner).wait_recv()
+
+    def back_copies(j):
+        m = 2 * set_of + j
+        first = 2 * (me // 2)
+        return [
+            moved(
+                back.at[m, rows_of(first + k)], back.at[m, rows_of(first + k)],
+                back_send.at[j, k], back_recv.at[m], {"section": 1 - sec, "tensor": first + k},
+            )
+            for k in range(2)
+        ]
+
+    def back_arrive(m):
+        rows = back.at[m, own]
+        moved(rows, rows, back_send.at[0, 0], back_recv.at[m], partner).wait_recv()
 
     def save_norm(l, m, n, r):
         nrm[l, m] = n
@@ -280,43 +332,9 @@
     def region_keys(q_rows, q_len):
         return key_mask(q_rows, q_len, RR, REGIONS)
 
-    def cross_a(m):
-        sec_copy(midf, m).wait_recv()
-        ag_start(midf, m)
-
-    def cross_b(m):
-        ag_finish(midf, m)
-        out = dot_nt(midf[m], cwqkv_ref[...]) + bqkv_ref[2]
-        out = out.astype(BF)
-        q, k, v = out[:, :HW], out[:, HW : 2 * HW], out[:, 2 * HW :]
-        cqkv[0, m], cqkv[1, m], cqkv[2, m] = q, k, v
-        probs, mix = attend(q[:RW], k[RW:], v[RW:], region_keys(RW, WORDS))
-        cp_w[m] = probs
-        cmixed[m, :RW] = mix
-        probs, mix = attend(q[RW:], k[:RW], v[:RW], word_keys(m, RR, REGIONS))
-        cp_r[m] = probs
-        cmixed[m, RW:] = mix
-        send[m] = dot(cmixed[m], cwo_ref[...]).astype(BF)
-        rs_start(m)
-
-    def cross_c(m):
-        r = midf[m, own].astype(F32) + rs_finish(m) + cvec_ref[0:1, :]
-        n, rs, h = norm_forward(r, cvec_ref[1:2, :], cvec_ref[2:3, :])
-        save_norm(2, m, n, rs)
-        cur[m] = h
-        xlow[m, own] = h.astype(BF)
-        ag_start(xlow, m)
-
     def layer_a(m):
-        @pl.when(head)
-        def _():
-            xlow[m] = x_ref[m]
-            cur[m] = x_ref[m, own].astype(F32)
-
-        @pl.when(cross)
-        def _():
-            ag_finish(xlow, m)
-
+        xlow[m] = x_ref[m]
+        cur[m] = x_ref[m, own].astype(F32)
         for mod, (lo, hi) in enumerate(SPANS):
             out = (dot_nt(xlow[m, lo:hi], wqkv_ref[mod]) + bqkv_ref[mod]).astype(BF)
             q, k, v = out[:, :HW], out[:, HW : 2 * HW], out[:, 2 * HW :]
@@ -390,37 +408,313 @@
             send[m, lo:hi] = dot(d, wqkv_ref[mod]).astype(BF)
         rs_start(m)
 
-    def cross_back_a(m):
-        dh = res[m] + rs_finish(m)
-        low = norm_step_back(2, m, dh, cvec_ref[1:2, :])
-        dyc[m, own] = low
-        ag_start(dyc, m)
-
-    def cross_back_b(m):
-        ag_finish(dyc, m)
-        dmix = dot_nt(dyc[m], cwo_ref[...]).astype(BF)
-        q, k, v = cqkv[0, m], cqkv[1, m], cqkv[2, m]
-        dq_w, dk_r, dv_r = attend_back(dmix[:RW], cp_w[m], q[:RW], k[RW:], v[RW:])
-        dq_r, dk_w, dv_w = attend_back(dmix[RW:], cp_r[m], q[RW:], k[:RW], v[:RW])
-        cdqkv[m, :RW] = jnp.concatenate([dq_w, dk_w, dv_w], axis=1)
-        cdqkv[m, RW:] = jnp.concatenate([dq_r, dk_r, dv_r], axis=1)
-        d = cdqkv[m]
-        bqsum[2] += jnp.sum(d.astype(F32), axis=0, keepdims=True)
-        send[m] = dot(d, cwqkv_ref[...]).astype(BF)
-        rs_start(m)
-
-    def cross_back_c(m):
-        back[m, own] = (res[m] + rs_finish(m)).astype(BF)
-        sec_copy(back, m).start()
+    def block_of(j):
+        return 2 * set_of + j
+
+    def ar_copy(j, mod, turn):
+        lo, hi = SPANS[mod]
+        return moved(
+            send.at[j, lo:hi], got.at[turn, j, lo:hi], ar_send.at[turn, j, mod], ar_recv.at[turn, j, mod],
+            halver,
+        )
+
+    def ar_start(j, mod, turn, part):
+        lo, hi = SPANS[mod]
+        send[j, lo:hi] = part.astype(BF)
+        ar_copy(j, mod, turn).start()
+
+    def ar_finish(j, mod, turn):
+        lo, hi = SPANS[mod]
+        ar_copy(j, mod, turn).wait()
+        return send[j, lo:hi].astype(F32) + got[turn, j, lo:hi].astype(F32)
+
+    shared = (xlow, alow, dyf, dya, dyc, ybuf)
+    for_mate = ((act_m, act), (dup_m, dup), (mixed_m, mixed), (dqkv_m, dqkv), (cmixed_m, cmixed), (cdqkv_m, cdqkv))
+    XLOW, ALOW, DYF, DYA, DYC, YBUF, ACT, DUP, MIXED, DQKV, CMIXED, CDQKV = range(12)
+
+    halves = (DYA, DYC, YBUF)
+
+    def half_rows(which):
+        return pl.ds(pl.multiple_of(which * (R // 2), R // 2), R // 2)
+
+    def mate_copy(k, j, arriving=False):
+        if k < 6:
+            src = dst = shared[k]
+            src = src.at[block_of(j)]
+        else:
+            src, dst = for_mate[k - 6]
+            src = src.at[j]
+        dst = dst.at[2 * (1 - set_of) + j if arriving else block_of(j)]
+        if k in halves:
+            src, dst = src.at[half_rows(me // 2)], dst.at[half_rows(me // 2)]
+        return moved(src, dst, mt_send.at[k, j], mt_recv.at[k, j], mate)
+
+    def mate_start(j, *kinds):
+        for k in kinds:
+            mate_copy(k, j).start()
+
+    def mate_start_all(*kinds):
+        for k in kinds:
+            for j in range(2):
+                mate_copy(k, j).start()
+
+    def mate_wait(*kinds):
+        for k in kinds:
+            for j in range(2):
+                mate_copy(k, j, True).wait_recv()
+                mate_copy(k, j).wait_send()
+
+    def pass_copy(k, j, arriving=False):
+        rows = half_rows(1 - me // 2 if arriving else me // 2)
+        place = shared[k].at[2 * (1 - set_of) + j, rows]
+        return moved(place, place, ps_send.at[k, j], ps_recv.at[k, j], halver)
+
+    def pass_start(k):
+        for j in range(2):
+            pass_copy(k, j).start()
+
+    def pass_wait(k):
+        for j in range(2):
+            pass_copy(k, j, True).wait_recv()
+            pass_copy(k, j).wait_send()
+
+    both_mods = slice(0, 2)
+    half_columns = pl.ds(pl.multiple_of(core * (D // 2), D // 2), D // 2)
+
+    def z_rows(z, count):
+        return pl.ds(pl.multiple_of(z * count, count), count)
+
+    gathered = (
+        (cwqkv_in, cwqkv_m, 3 * HW // 4, False), (cwo_in, cwo_m, HW // 4, False),
+        (wqkv_in, wqkv_m, 3 * HW // 4, True), (wo_in, wo_m, HW // 4, True),
+        (w1_in, w1_m, D // 4, True), (w2_in, w2_m, D // 4, True),
+    )
+    Y_FIRST = (W1,) = (4,)
+    CWQKV, CWO, WQKV, WO, W2 = 0, 1, 2, 3, 5
+
+    def gather_copies(k, step):
+        src, dst, count, by_mod = gathered[k]
+        sems = lambda i: (ga_send.at[k, i], ga_recv.at[k, i])
+        at = lambda mods, rows: (mods, rows, half_columns) if by_mod else (rows, half_columns)
+        mine = at(y_at, z_rows(z_at, count))
+        if step == "x":
+            return [moved(src.at[mine], dst.at[mine], *sems(0), mate)]
+        if step == "y":
+            place = dst.at[mine] if k in Y_FIRST else dst.at[at(y_at, slice(0, 4 * count))]
+            return [moved(place, place, *sems(1), other_y)]
+        if step == "z":
+            place = dst.at[at(both_mods if k in Y_FIRST else y_at, z_rows(z_at, count))]
+            return [
+                moved(place, place, *sems(1 + o), dp_device(y_at, z_next(o), core)) for o in (1, 2, 3)
+            ]
+        place = dst.at[at(both_mods, slice(0, 4 * count))]
+        return [moved(place, place, *sems(5), other_core)]
+
+    def gather_start(step, *arrays):
+        for k in arrays:
+            for copy in gather_copies(k, step):
+                copy.start()
+
+    def gather_wait(step, *arrays):
+        for k in arrays:
+            for copy in gather_copies(k, step):
+                copy.wait()
+
+    def bias_copies():
+        return [
+            moved(bqkv_ref, bqkv_m, ga_send.at[6, 0], ga_recv.at[6, 0], mate),
+            moved(b1_ref, b1_m, ga_send.at[7, 0], ga_recv.at[7, 0], mate),
+        ]
+
+    def save_norm_f(l, j, lo, hi, n, r):
+        nrm_f[l, j, lo:hi] = n
+        rstd_f[l, j, lo:hi] = jnp.broadcast_to(r, (hi - lo, 128))
+
+    def count_rows(l, mod, dh, n, low):
+        for k, value in enumerate((dh * n, dh, low.astype(F32))):
+            at = 12 + k if l == 2 else 2 * (3 * l + k) + mod
+            row_sums[at] += jnp.sum(value, axis=0, keepdims=True)
+
+    def cross_forward(j):
+        m = block_of(j)
+        mid_arrive(m)
+        mid = midf[m]
+        part = None
+        shards = ((cwqkv_ref, bqkv_ref, cwo_ref, cmixed, m), (cwqkv_m, bqkv_m, cwo_m, cmixed_m, j))
+        for sh, (w, bias, w_out, keep, at) in enumerate(shards):
+            slot = 2 * sh + j
+            out = (dot_nt(mid, w[...]) + bias[2]).astype(BF)
+            q, k, v = out[:, :HW], out[:, HW : 2 * HW], out[:, 2 * HW :]
+            cqkv[0, slot], cqkv[1, slot], cqkv[2, slot] = q, k, v
+            probs, mix = attend(q[:RW], k[RW:], v[RW:], region_keys(RW, WORDS))
+            cp_w[slot] = probs
+            keep[at, :RW] = mix
+            probs, mix = attend(q[RW:], k[:RW], v[:RW], word_keys(m, RR, REGIONS))
+            cp_r[slot] = probs
+            keep[at, RW:] = mix
+            one = dot(keep[at], w_out[...])
+            part = one if part is None else part + one
+        for mod, (lo, hi) in enumerate(SPANS):
+            ar_start(j, mod, 0, part[lo:hi])
+        mate_start(j, CMIXED)
+
+    def attn_forward(j):
+        m = block_of(j)
+        shards = (
+            (wqkv_ref, bqkv_ref, wo_ref, mixed, m), (wqkv_m, bqkv_m, wo_m, mixed_m, j),
+        )
+        for mod, (lo, hi) in enumerate(SPANS):
+            r = midf[m, lo:hi].astype(F32) + ar_finish(j, mod, 0) + cvec_ref[0:1, :]
+            n, rs, h = norm_forward(r, cvec_ref[1:2, :], cvec_ref[2:3, :])
+            save_norm_f(1, j, lo, hi, n, rs)
+            cur_f[j, lo:hi] = h
+            low = h.astype(BF)
+            xlow[m, lo:hi] = low
+            part = None
+            for sh, (w, bias, w_out, keep, at) in enumerate(shards):
+                slot = 2 * sh + j
+                out = (dot_nt(low, w[mod]) + bias[mod]).astype(BF)
+                q, k, v = out[:, :HW], out[:, HW : 2 * HW], out[:, 2 * HW :]
+                qkv[0, slot, lo:hi], qkv[1, slot, lo:hi], qkv[2, slot, lo:hi] = q, k, v
+                if mod == 0:
+                    probs, mix = attend(q, k, v, word_keys(m, RW, WORDS))
+                    p_w[slot] = probs
+                else:
+                    probs, mix = attend(q, k, v, region_keys(RR, REGIONS))
+                    p_r[slot] = probs
+                keep[at, lo:hi] = mix
+                one = dot(mix, w_out[mod])
+                part = one if part is None else part + one
+            ar_start(j, mod, 1, part)
+        mate_start(j, XLOW, MIXED)
+
+    def ffn_forward(j):
+        m = block_of(j)
+        shards = ((w1_ref, b1_ref, w2_ref, act, m), (w1_m, b1_m, w2_m, act_m, j))
+        for mod, (lo, hi) in enumerate(SPANS):
+            r = cur_f[j, lo:hi] + ar_finish(j, mod, 1) + out_bias_ref[0, mod, 0:1, :]
+            n, rs, h = norm_forward(r, gain_ref[0, mod, 0:1, :], shift_ref[0, mod, 0:1, :])
+            save_norm_f(0, j, lo, hi, n, rs)
+            cur_f[j, lo:hi] = h
+            low = h.astype(BF)
+            alow[m, lo:hi] = low
+            part = None
+            for sh, (w, bias, w_out, keep, at) in enumerate(shards):
+                up = dot(low, w[mod]) + bias[mod]
+                cdf = 0.5 * (1.0 + lax.erf(up * (0.5**0.5)))
+                dgelu[2 * sh + j, lo:hi] = cdf + up * jnp.exp(-0.5 * up * up) * 0.3989422804014327
+                active = (up * cdf).astype(BF)
+                keep[at, lo:hi] = active
+                one = dot(active, w_out[mod])
+                part = one if part is None else part + one
+            ar_start(j, mod, 0, part)
+        mate_start(j, ALOW, ACT)
+
+    def ffn_turn(j):
+        m = block_of(j)
+        shards = ((w1_ref, w2_ref, dup, m), (w1_m, w2_m, dup_m, j))
+        for mod, (lo, hi) in enumerate(SPANS):
+            r = cur_f[j, lo:hi] + ar_finish(j, mod, 0) + out_bias_ref[0, mod, 1:2, :]
+            gain = gain_ref[0, mod, 1:2, :]
+            n, rs, h = norm_forward(r, gain, shift_ref[0, mod, 1:2, :])
+            ybuf[m, lo:hi] = h.astype(BF)
+            scale = scales(m, 1 - mod, hi - lo, (WORDS, REGIONS)[mod])
+            dh = x_ref[m, lo:hi].astype(F32) * scale
+            dr = norm_back(dh, n, rs, gain)
+            res_f[j, lo:hi] = dr
+            low = dr.astype(BF)
+            dyf[m, lo:hi] = low
+            count_rows(1, mod, dh, n, low)
+            part = None
+            for sh, (w_in, w_out, keep, at) in enumerate(shards):
+                d = (dot_nt(low, w_out[mod]) * dgelu[2 * sh + j, lo:hi]).astype(BF)
+                keep[at, lo:hi] = d
+                one = dot_nt(d, w_in[mod])
+                part = one if part is None else part + one
+            ar_start(j, mod, 1, part)
+        mate_start(j, DYF)
+        pl.when(j == 0)(lambda: mate_start(0, DUP))
+
+    def attn_backward(j):
+        m = block_of(j)
+        shards = ((wqkv_ref, wo_ref, dqkv, m), (wqkv_m, wo_m, dqkv_m, j))
+        for mod, (lo, hi) in enumerate(SPANS):
+            dh = res_f[j, lo:hi] + ar_finish(j, mod, 1)
+            n = nrm_f[0, j, lo:hi]
+            dr = norm_back(dh, n, rstd_f[0, j, lo:hi][:, :1], gain_ref[0, mod, 0:1, :])
+            res_f[j, lo:hi] = dr
+            low = dr.astype(BF)
+            dya[m, lo:hi] = low
+            count_rows(0, mod, dh, n, low)
+            part = None
+            for sh, (w, w_out, keep, at) in enumerate(shards):
+                slot = 2 * sh + j
+                dmix = dot_nt(low, w_out[mod]).astype(BF)
+                probs = p_w[slot] if mod == 0 else p_r[slot]
+                parts = attend_back(
+                    dmix, probs, qkv[0, slot, lo:hi], qkv[1, slot, lo:hi], qkv[2, slot, lo:hi]
+                )
+                d = jnp.concatenate(parts, axis=1)
+                keep[at, lo:hi] = d
+                one = dot(d, w[mod])
+                part = one if part is None else part + one
+            ar_start(j, mod, 0, part)
+
+    def cross_backward(j):
+        m = block_of(j)
+        for mod, (lo, hi) in enumerate(SPANS):
+            dh = res_f[j, lo:hi] + ar_finish(j, mod, 0)
+            n = nrm_f[1, j, lo:hi]
+            dr = norm_back(dh, n, rstd_f[1, j, lo:hi][:, :1], cvec_ref[1:2, :])
+            res_f[j, lo:hi] = dr
+            low = dr.astype(BF)
+            dyc[m, lo:hi] = low
+            count_rows(2, mod, dh, n, low)
+        part = None
+        shards = ((cwqkv_ref, cwo_ref, cdqkv, m), (cwqkv_m, cwo_m, cdqkv_m, j))
+        for sh, (w, w_out, keep, at) in enumerate(shards):
+            slot = 2 * sh + j
+            dmix = dot_nt(dyc[m], w_out[...]).astype(BF)
+            q, k, v = cqkv[0, slot], cqkv[1, slot], cqkv[2, slot]
+            dq_w, dk_r, dv_r = attend_back(dmix[:RW], cp_w[slot], q[:RW], k[RW:], v[RW:])
+            dq_r, dk_w, dv_w = attend_back(dmix[RW:], cp_r[slot], q[RW:], k[:RW], v[:RW])
+            keep[at, :RW] = jnp.concatenate([dq_w, dk_w, dv_w], axis=1)
+            keep[at, RW:] = jnp.concatenate([dq_r, dk_r, dv_r], axis=1)
+            one = dot(keep[at], w[...])
+            part = one if part is None else part + one
+        for mod, (lo, hi) in enumerate(SPANS):
+            ar_start(j, mod, 1, part[lo:hi])
+
+    def to_section_0(j):
+        m = block_of(j)
+        for mod, (lo, hi) in enumerate(SPANS):
+            back[m, lo:hi] = (res_f[j, lo:hi] + ar_finish(j, mod, 1)).astype(BF)
+        for copy in back_copies(j):
+            copy.start()
+
+    def column_sums(buf, lo, hi):
+        rows = buf[:, lo:hi, :].astype(F32).reshape(MB * (hi - lo), buf.shape[-1])
+        return jnp.sum(rows, axis=0, keepdims=True)
+
+    def scales(m, flag, count, length):
+        index = lax.broadcasted_iota(jnp.int32, (count, 1), 0)
+        scale = jnp.ones((count, 1), F32)
+        for k in range(ITEMS_MB):
+            value = jnp.where(flags_ref[ITEMS_MB * m + k] == flag, 0.25, 1.0)
+            scale = jnp.where(index >= k * length, value, scale)
+        return scale
+
+    def outer_tile(left, right, lo, hi, j, store):
+        start = j * (D // 2)
+        columns = pl.ds(start if isinstance(j, int) else pl.multiple_of(start, D // 2), D // 2)
+        a = left[:, lo:hi, columns].reshape(MB * (hi - lo), D // 2)
+        b = right[:, lo:hi, :].reshape(MB * (hi - lo), right.shape[-1])
+        store(dot_tn(a, b))
 
     def outer(left, right, lo, hi, store):
-        def tile(j):
-            columns = pl.ds(pl.multiple_of(j * (D // 2), D // 2), D // 2)
-            a = left[:, lo:hi, columns].reshape(MB * (hi - lo), D // 2)
-            b = right[:, lo:hi, :].reshape(MB * (hi - lo), right.shape[-1])
-            store(j, dot_tn(a, b))
-
-        pl.loop(0, 2)(tile)
+        pl.loop(0, 2)(
+            lambda j: outer_tile(left, right, lo, hi, j, p(store, j))
+        )
 
     def store_at(block, lo, hi):
         def store(j, value):
@@ -428,75 +722,57 @@
 
         return store
 
-    def ffn_outer():
-        for mod, (lo, hi) in enumerate(SPANS):
-            outer(alow, dup, lo, hi, store_at(1 + 4 * mod, 0, D))
-            outer(dyf, act, lo, hi, store_at(2 + 4 * mod, 0, D))
-
-    def attn_outer():
-        for mod, (lo, hi) in enumerate(SPANS):
-            outer(xlow, dqkv, lo, hi, store_at(4 * mod, 0, 3 * HW))
-            outer(dya, mixed, lo, hi, store_at(4 * mod, 3 * HW, D))
+    def ffn_piece(k):
+        mod, second = k // 2, k % 2
+        left, right = ((alow, dup), (dyf, act))[second]
+        outer(left, right, *SPANS[mod], store_at(1 + 4 * mod + second, 0, D))
+
+    def attn_piece(k):
+        mod, second = k // 2, k % 2
+        left, right = ((xlow, dqkv), (dya, mixed))[second]
+        outer(left, right, *SPANS[mod], store_at(4 * mod, *((0, 3 * HW), (3 * HW, D))[second]))
 
     def cross_outer():
-        def store(lo, hi):
-            def put(j, value):
-                wide[j, :, :, lo:hi] = value.reshape(16, 24, hi - lo)
+        def store(j, lo, hi):
+            def put(value):
+                value = value.astype(BF).reshape(2, 4, 2, 24, hi - lo)
+                g_ref[3, :, :, :, 24 * j : 24 * j + 24, lo:hi] = value
 
             return put
 
-        outer(midf, cdqkv, 0, R, store(0, 3 * HW))
-        outer(dyc, cmixed, 0, R, store(3 * HW, D))
-        for y in range(2):
-            for z in range(4):
-                for c in range(2):
-                    at = (y * 4 + z) * 2 + c
-                    both = jnp.concatenate([wide[0, at], wide[1, at]], axis=0)
-                    g_ref[3, y, z, c] = both.astype(BF)
-
-    def moved(src, dst, send_sem, recv_sem, device):
-        return pltpu.make_async_remote_copy(
-            src_ref=src, dst_ref=dst, send_sem=send_sem, recv_sem=recv_sem, device_id=device,
-            device_id_type=MESH,
-        )
+        for j in range(2):
+            outer_tile(midf, cdqkv, 0, R, j, store(j, 0, 3 * HW))
+            outer_tile(dyc, cmixed, 0, R, j, store(j, 3 * HW, D))
 
     def dw_copies(group, phase):
-        (a0, a1), (b0, b1) = group[1:]
-        sems = lambda k: (dw_send.at[group[0], k], dw_recv.at[group[0], k])
-        na, nb = slice(a0, a1), slice(b0, b1)
-        nbr = slice(b0 - 4, b1 - 4)
-        copies = []
+        index, y_first, lo, hi = group
+        sems = lambda k: (dw_send.at[index, k], dw_recv.at[index, k])
+        blocks = slice(lo, hi)
         if phase == 0:
-            copies.append(
-                moved(g_ref.at[na, :, :, 1 - core], from_core.at[na], *sems(0), other_core)
-            )
-            if b1 > b0:
-                copies.append(
-                    moved(g_ref.at[nb, :, :, 1 - core], from_core.at[nb], *sems(1), other_core)
+            src = g_ref.at[blocks, :, :, 1 - core]
+            return [moved(src, from_core.at[blocks], *sems(0), other_core)]
+        if y_first and phase == 1:
+            src = g_ref.at[blocks, 1 - y_at, :, core]
+            return [moved(src, from_y.at[blocks], *sems(1), other_y)]
+        if y_first:
+            return [
+                moved(
+                    g_ref.at[blocks, y_at, z_next(o), core], from_z.at[blocks, o - 1],
+                    *sems(1 + o), dp_device(y_at, z_next(o), core),
                 )
+                for o in (1, 2, 3)
+            ]
+        late = slice(lo - 4, hi - 4)
         if phase == 1:
-            copies.append(moved(g_ref.at[na, 1 - y_at, :, core], from_y.at[na], *sems(2), other_y))
-            if b1 > b0:
-                for o in (1, 2, 3):
-                    copies.append(
-                        moved(
-                            g_ref.at[nb, :, z_next(o), core], from_zs.at[nbr, o - 1], *sems(2 + o),
-                            dp_device(y_at, z_next(o), core),
-                        )
-                    )
-        if phase == 2:
-            for o in (1, 2, 3):
-                copies.append(
-                    moved(
-                        g_ref.at[na, y_at, z_next(o), core], from_z.at[na, o - 1], *sems(5 + o),
-                        dp_device(y_at, z_next(o), core),
-                    )
+            return [
+                moved(
+                    g_ref.at[blocks, :, z_next(o), core], from_zs.at[late, o - 1],
+                    *sems(1 + o), dp_device(y_at, z_next(o), core),
                 )
-            if b1 > b0:
-                copies.append(
-                    moved(g_ref.at[nb, 1 - y_at, z_at, core], from_ys.at[nbr], *sems(9), other_y)
-                )
-        return copies
+                for o in (1, 2, 3)
+            ]
+        src = g_ref.at[blocks, 1 - y_at, z_at, core]
+        return [moved(src, from_ys.at[late], *sems(1), other_y)]
 
     def dw_start(group, phase):
         for copy in dw_copies(group, phase):
@@ -505,47 +781,40 @@
     def dw_finish(group, phase):
         for copy in dw_copies(group, phase):
             copy.wait()
-        (a0, a1), (b0, b1) = group[1:]
-        if phase == 0:
-            for lo, hi in ((a0, a1), (b0, b1)):
-
-                def add(k, lo=lo):
-                    b, y = lo + k // 2, lax.rem(k, 2)
+        index, y_first, lo, hi = group
+
+        def add(b):
+            if phase == 0:
+                for y in range(2):
                     mine = g_ref[b, y, :, core].astype(F32)
                     g_ref[b, y, :, core] = (mine + from_core[b, y].astype(F32)).astype(BF)
-
-                pl.loop(0, 2 * (hi - lo))(add)
-        if phase == 1:
-
-            def add_a(b):
+            elif phase == 1 and y_first:
                 mine = g_ref[b, y_at, :, core].astype(F32)
                 g_ref[b, y_at, :, core] = (mine + from_y[b].astype(F32)).astype(BF)
-
-            def add_b(b):
+            elif phase == 1:
                 total = g_ref[b, :, z_at, core].astype(F32)
                 for o in range(3):
                     total = total + from_zs[b - 4, o].astype(F32)
                 g_ref[b, :, z_at, core] = total.astype(BF)
-
-            pl.loop(a0, a1)(add_a)
-            pl.loop(b0, b1)(add_b)
-        if phase == 2:
-
-            def last_a(b):
+            else:
                 total = g_ref[b, y_at, z_at, core].astype(F32)
-                for o in range(3):
+                for o in range(3 if y_first else 0):
                     total = total + from_z[b, o].astype(F32)
+                if not y_first:
+                    total = total + from_ys[b - 4].astype(F32)
                 dw_ref[b] = total
 
-            def last_b(b):
-                dw_ref[b] = g_ref[b, y_at, z_at, core].astype(F32) + from_ys[b - 4].astype(F32)
-
-            pl.loop(a0, a1)(last_a)
-            pl.loop(b0, b1)(last_b)
-
-    FFN = (0, (1, 3), (5, 7))
-    ATTN = (1, (0, 1), (4, 5))
-    CROSS = (2, (3, 4), (4, 4))
+        pl.loop(lo, hi)(add)
+
+    def dw_turn(group, phase):
+        dw_finish(group, phase)
+        dw_start(group, phase + 1)
+
+    FFN_W = (0, True, 1, 3)
+    FFN_R = (1, False, 5, 7)
+    ATTN_W = (2, True, 0, 1)
+    ATTN_R = (3, False, 4, 5)
+    CROSS = (4, True, 3, 4)
 
     def sm_copies(step):
         sems = lambda k: (sm_send.at[k], sm_recv.at[k])
@@ -572,6 +841,12 @@
         for copy in sm_copies(step):
             copy.wait()
 
+    def small_norms_all():
+        for k in range(15):
+            sums_t[me, k : k + 1, :] = jnp.where(me < 2, row_sums[k], 0.0)
+        sums_t[me, 15:16, :] = jnp.zeros((1, D), F32)
+        sm_start(0)
+
     def small_norms():
         sums_t[me] = jnp.zeros((16, D), F32)
         for l in range(2):
@@ -582,8 +857,6 @@
                 sums_t[me, at + 1 : at + 2, :] = jnp.sum(
                     jnp.where(is_word, 0.0, a), axis=0, keepdims=True
                 )
-        for k in range(3):
-            sums_t[me, 12 + k : 13 + k, :] = jnp.sum(acc[6 + k], axis=0, keepdims=True)
         sm_start(0)
 
     def small_biases():
@@ -613,138 +886,203 @@
     def packet():
         return moved(pack.at[0], pack.at[1], pk_send, pk_recv, partner)
 
-    def each(*steps):
+    def each(*steps, after=()):
         def body(m):
             for step in steps:
                 step(m)
+            for k, extra in enumerate(after):
+                if extra is not None:
+                    pl.when(m == k)(extra)
 
         pl.loop(0, MB)(body)
 
-    @pl.when(cross)
-    def _():
-        each(cross_a)
-        each(cross_b)
-        each(cross_c)
-
-    each(layer_a)
-    each(layer_b)
-    each(layer_c)
+    def then(*steps):
+        def run():
+            for step in steps:
+                step()
+
+        return run
+
+    def pair(step):
+        pl.loop(0, 2)(step)
 
     @pl.when(head)
     def _():
         def to_partner(m):
             midf[m, own] = layer_d(m).astype(BF)
-            sec_copy(midf, m).start()
+            first = m // 2
+            for k, t in enumerate((first, 3 - first)):
+                mid_copy(m, k, t).start()
+
+        def to_others(m):
+            first = m // 2
+            for k, t in enumerate((1 - first, 2 + first)):
+                mid_copy(m, 2 + k, t).start()
 
         def from_partner(m):
-            sec_copy(midf, m).wait_send()
-            sec_copy(back, m).wait_recv()
+            for k in range(TENSOR):
+                mid_copy(m, k, 0).wait_send()
+            back_arrive(m)
             back_e(m, back[m, own].astype(F32))
 
-        each(to_partner)
-        each(from_partner)
-
-    @pl.when(cross)
-    def _():
-        def scales(m, flag, first, later):
-            value = jnp.where(flags_ref[ITEMS_MB * m] == flag, 0.25, 1.0)
-            scale = jnp.full((C, 1), value, F32)
-            for k in range(1, ITEMS_MB):
-                value = jnp.where(flags_ref[ITEMS_MB * m + k] == flag, 0.25, 1.0)
-                scale = jnp.where(row >= first + k * later, value, scale)
-            return scale
-
-        def turn(m):
-            h = layer_d(m)
-            scale = jnp.where(is_word, scales(m, 1, 0, WORDS), scales(m, 0, RW, REGIONS))
-            back_e(m, x_ref[m, own].astype(F32) * scale)
-            ybuf[m, own] = h.astype(BF)
-
-        each(turn)
-
-    each(back_f)
-
-    @pl.when(head)
-    def _():
-        ffn_outer()
-        dw_start(FFN, 0)
-
-    each(back_g)
-
-    @pl.when(head)
-    def _():
-        dw_finish(FFN, 0)
-        dw_start(FFN, 1)
-
-    each(back_h)
-
-    @pl.when(head)
-    def _():
         def last(m):
             ybuf[m, own] = (res[m] + rs_finish(m)).astype(BF)
             ag_start(ybuf, m, y_send, y_recv)
 
-        attn_outer()
-        dw_start(ATTN, 0)
+        wait_weights(0, 1)
+        each(layer_a)
+        wait_weights(2, 3)
+        each(layer_b)
+        each(layer_c)
+        each(to_partner)
+        each(to_others)
+        each(from_partner)
+        each(back_f)
+        ffn_piece(2)
+        ffn_piece(3)
+        dw_start(FFN_R, 0)
+        each(
+            back_g,
+            after=(
+                p(ffn_piece, 0),
+                then(p(dw_turn, FFN_R, 0), p(ffn_piece, 1), p(dw_start, FFN_W, 0)),
+            ),
+        )
         small_norms()
-        each(last)
+        each(back_h, after=(p(dw_turn, FFN_W, 0),))
+        attn_piece(2)
+        attn_piece(3)
+        dw_start(ATTN_R, 0)
+        attn_piece(0)
+        attn_piece(1)
+        dw_start(ATTN_W, 0)
         small_biases()
-        dw_finish(FFN, 1)
+        each(last, after=(p(dw_turn, ATTN_R, 0), p(dw_turn, FFN_R, 1), p(dw_turn, ATTN_W, 0)))
         small_y()
-        dw_start(FFN, 2)
-        dw_finish(ATTN, 0)
-        dw_start(ATTN, 1)
+        dw_turn(FFN_W, 1)
         small_z()
 
     @pl.when(cross)
     def _():
-        each(cross_back_a)
-        each(cross_back_b)
-        each(cross_back_c)
-        each(lambda m: ag_start(ybuf, m, y_send, y_recv))
-        ffn_outer()
-        dw_start(FFN, 0)
-        small_norms()
-        attn_outer()
-        dw_start(ATTN, 0)
-        dw_finish(FFN, 0)
-        dw_start(FFN, 1)
-        small_biases()
+        gather_start("x", CWQKV, CWO, WQKV, WO)
+        for copy in bias_copies():
+            copy.start()
+        gather_start("x", W2, W1)
+        gather_wait("x", CWQKV, CWO)
+        gather_start("z", CWQKV, CWO)
+        gather_wait("x", WQKV, WO)
+        gather_start("z", WQKV, WO)
+        gather_wait("x", W2, W1)
+        gather_start("y", W1)
+        gather_start("z", W2)
+        gather_wait("z", CWQKV, CWO)
+        gather_start("core", CWQKV, CWO)
+        gather_wait("y", W1)
+        gather_start("z", W1)
+        gather_wait("z", WQKV, WO)
+        gather_start("y", WQKV, WO)
+        for copy in bias_copies():
+            copy.wait()
+        gather_wait("core", CWQKV, CWO)
+        wait_weights(0, 1, 2, 3, 4, 5)
+        cross_forward(0)
+        gather_wait("z", W2)
+        gather_start("y", W2)
+        gather_wait("y", WQKV, WO)
+        gather_start("core", WQKV, WO)
+        cross_forward(1)
+        gather_wait("core", WQKV, WO)
+        attn_forward(0)
+        gather_wait("z", W1)
+        gather_wait("y", W2)
+        gather_start("core", W1, W2)
+        attn_forward(1)
+        gather_wait("core", W1, W2)
+        pair(ffn_forward)
+        pair(ffn_turn)
+        pair(attn_backward)
+        pair(cross_backward)
+        pair(to_section_0)
+        mate_start_all(DYC)
+        mate_start(1, DUP)
+        mate_start_all(CDQKV)
+        small_norms_all()
+        mate_wait(CMIXED, XLOW, MIXED, ALOW, ACT, DYF)
+        mate_wait(DYC)
+        pass_start(DYC)
+        mate_start_all(DYA)
+        mate_wait(DUP)
+        mate_start_all(DQKV)
+        ffn_piece(2)
+        ffn_piece(3)
+        dw_start(FFN_R, 0)
+        ffn_piece(0)
+        ffn_piece(1)
+        dw_start(FFN_W, 0)
+        for mod, (lo, hi) in enumerate(SPANS):
+            bsum[mod] = column_sums(dup, lo, hi)
+        dw_turn(FFN_R, 0)
+        dw_turn(FFN_W, 0)
+        mate_wait(DYA)
+        pass_start(DYA)
+        for k in range(2):
+            mid_arrive(2 * (1 - set_of) + k)
+        mate_wait(CDQKV)
+        mate_start_all(YBUF)
+        pass_wait(DYC)
         cross_outer()
         dw_start(CROSS, 0)
-        dw_finish(ATTN, 0)
-        dw_start(ATTN, 1)
+        bqsum[2] = column_sums(cdqkv, 0, R)
+        dw_turn(CROSS, 0)
+        mate_wait(DQKV)
+        pass_wait(DYA)
+        attn_piece(2)
+        attn_piece(3)
+        dw_start(ATTN_R, 0)
+        attn_piece(0)
+        attn_piece(1)
+        dw_start(ATTN_W, 0)
+        for mod, (lo, hi) in enumerate(SPANS):
+            bqsum[mod] = column_sums(dqkv, lo, hi)
+        small_biases()
+        mate_wait(YBUF)
+        pass_start(YBUF)
+        dw_turn(FFN_R, 1)
+        dw_turn(CROSS, 1)
+        dw_turn(ATTN_R, 0)
+        dw_turn(ATTN_W, 0)
         small_y()
-        dw_finish(CROSS, 0)
-        dw_start(CROSS, 1)
+        dw_turn(FFN_W, 1)
         small_z()
-        dw_finish(FFN, 1)
-        dw_start(FFN, 2)
+        pass_wait(YBUF)
+        pair(lambda j: [copy.wait_send() for copy in back_copies(j)] and None)
 
     def write(m):
-        ag_finish(ybuf, m, y_send, y_recv)
+        @pl.when(head)
+        def _():
+            ag_finish(ybuf, m, y_send, y_recv)
+
         y_ref[m] = ybuf[m]
 
     each(write)
-    dw_finish(FFN, 2)
-    dw_finish(ATTN, 1)
-    dw_start(ATTN, 2)
+    dw_finish(FFN_R, 2)
+    dw_turn(ATTN_R, 1)
+    dw_turn(ATTN_W, 1)
+    dw_finish(FFN_W, 2)
     small_last()
 
     @pl.when(cross)
     def _():
-        each(lambda m: sec_copy(back, m).wait_send())
-        dw_finish(CROSS, 1)
-        dw_start(CROSS, 2)
         dw_finish(CROSS, 2)
         pack[0, :24] = dw_ref[3, :24]
         pack[0, 24:] = s_ref[...]
         packet().start()
         dc_ref[...] = dw_ref[3, 24:]
         sc_ref[...] = s_ref[...]
-        packet().wait_send()
-
-    dw_finish(ATTN, 2)
+
+    dw_finish(ATTN_W, 2)
+    dw_finish(ATTN_R, 2)
+    pl.when(cross)(lambda: packet().wait_send())
 
     @pl.when(head)
     def _():
@@ -824,6 +1162,7 @@
 
     vmem = pl.BlockSpec(memory_space=pltpu.VMEM)
     smem = pl.BlockSpec(memory_space=pltpu.SMEM)
+    hbm = pl.BlockSpec(memory_space=pl.ANY)
     mb_rows = lambda width, dtype: pltpu.VMEM((MB, R, width), dtype)
     own_rows = lambda count: pltpu.VMEM((count, MB, C, D), F32)
     y, g, s, dc, sc = pl.pallas_call(
@@ -835,7 +1174,7 @@
             jax.ShapeDtypeStruct((24, D), F32),
             jax.ShapeDtypeStruct((24, D), F32),
         ),
-        in_specs=[smem if k in (2, 3) else vmem for k in range(len(inputs))],
+        in_specs=[smem if k in (2, 3) else hbm if k in (4, 6, 7, 9, 13, 15) else vmem for k in range(len(inputs))],
         out_specs=[vmem] * 5,
         scratch_shapes=[
             mb_rows(D, BF),
@@ -860,19 +1199,39 @@
             pltpu.VMEM((MB, 3 * RR, RW), F32),
             pltpu.VMEM((MB, C, D), F32),
             pltpu.VMEM((MB, C, D), F32),
-            own_rows(3),
-            pltpu.VMEM((3, MB, C, 128), F32),
-            pltpu.VMEM((9, C, D), F32),
+            pltpu.VMEM((2, MB, C, D), F32),
+            pltpu.VMEM((2, MB, C, 128), F32),
+            pltpu.VMEM((6, C, D), F32),
             pltpu.VMEM((6, C, D), F32),
             pltpu.VMEM((2, 1, D), F32),
             pltpu.VMEM((3, 1, 3 * HW), F32),
+            pltpu.VMEM((2, 3 * HW, D), BF),
+            pltpu.VMEM((2, HW, D), BF),
+            pltpu.VMEM((2, D, D), BF),
+            pltpu.VMEM((2, D, D), BF),
+            pltpu.VMEM((3 * HW, D), BF),
+            pltpu.VMEM((HW, D), BF),
+            pltpu.VMEM((2, 3 * HW, D), BF),
+            pltpu.VMEM((2, HW, D), BF),
+            pltpu.VMEM((2, D, D), BF),
+            pltpu.VMEM((2, D, D), BF),
+            pltpu.VMEM((3 * HW, D), BF),
+            pltpu.VMEM((HW, D), BF),
+            pltpu.VMEM((3, 1, 3 * HW), F32),
+            pltpu.VMEM((2, 1, D), F32),
+            pltpu.VMEM((2, 2, R, D), BF),
+            *[pltpu.VMEM((2, R, w), BF) for w in (D, D, HW, 3 * HW, HW, 3 * HW)],
+            pltpu.VMEM((2, R, D), F32),
+            pltpu.VMEM((2, R, D), F32),
+            pltpu.VMEM((2, 2, R, D), F32),
+            pltpu.VMEM((2, 2, R, 128), F32),
+            pltpu.VMEM((16, 1, D), F32),
             pltpu.VMEM((7, 2, 4, 2, 48, D), BF),
             pltpu.VMEM((7, 2, 4, 48, D), BF),
             pltpu.VMEM((4, 4, 48, D), BF),
             pltpu.VMEM((3, 3, 2, 48, D), BF),
             pltpu.VMEM((4, 3, 48, D), BF),
             pltpu.VMEM((3, 48, D), BF),
-            pltpu.VMEM((2, 16, 24, D), F32),
             pltpu.VMEM((3, 24, D), F32),
             pltpu.VMEM((TENSOR, 16, D), F32),
             pltpu.VMEM((24, D), F32),
@@ -880,17 +1239,24 @@
             pltpu.VMEM((3, 24, D), F32),
             pltpu.VMEM((2, 48, D), F32),
             *[pltpu.SemaphoreType.DMA((MB, TENSOR - 1)) for _ in range(6)],
-            pltpu.SemaphoreType.DMA((MB,)),
-            pltpu.SemaphoreType.DMA((MB,)),
-            pltpu.SemaphoreType.DMA((3, 10)),
-            pltpu.SemaphoreType.DMA((3, 10)),
+            pltpu.SemaphoreType.DMA((MB, TENSOR)),
+            pltpu.SemaphoreType.DMA((MB, TENSOR)),
+            pltpu.SemaphoreType.DMA((5, 5)),
+            pltpu.SemaphoreType.DMA((5, 5)),
             pltpu.SemaphoreType.DMA((8,)),
             pltpu.SemaphoreType.DMA((8,)),
             pltpu.SemaphoreType.DMA,
             pltpu.SemaphoreType.DMA,
+            pltpu.SemaphoreType.DMA((2, 2)),
+            pltpu.SemaphoreType.DMA((MB,)),
+            *[pltpu.SemaphoreType.DMA((2, 2, 2)) for _ in range(2)],
+            *[pltpu.SemaphoreType.DMA((12, 2)) for _ in range(2)],
+            *[pltpu.SemaphoreType.DMA((8, 6)) for _ in range(2)],
+            *[pltpu.SemaphoreType.DMA((6, 2)) for _ in range(2)],
+            pltpu.SemaphoreType.DMA((6,)),
         ],
         compiler_params=pltpu.CompilerParams(
-            collective_id=0, has_side_effects=True, vmem_limit_bytes=60 * 2**20
+            collective_id=0, has_side_effects=True, vmem_limit_bytes=63 * 2**20
         ),
     )(*inputs)
 

time: 210 us -> 183 us (0.87)
  Pallas kernels: 208 us -> 182 us
    pallas_call x1, Pallas kernels: 205 us -> 179 us  [local(): pl.pallas_call(kernel, out_shape=(jax.ShapeDtypeStruct((MB, R, D), BF), j...]
where the time goes in v3:
time: 183 us
  Pallas kernels  182 us (99%)
    pallas_call x1, Pallas kernels, local(): pl.pallas_call(kernel, out_shape=(jax.ShapeDtypeStruct((MB, R, D), BF), j...  179 us

profile of v3, /device:TPU:0, one launch (start us, length us, event | category | flops | bytes accessed | tf_op | source)
XLA Modules:
  0.0 182.8 jit_solution(3894161567750427643)
XLA Ops:
  0.7 178.7 %shard_map.314 = (bf16[4,128,768]{2,1,0:T(8,128)(2,1)}, f32[7,48,768]{2,1,0:T(8,128)}, f32[24,768]{1,0:T(8,128)}, f32[24,768]{1,0:T(8,128)}, f32[24,768]{1,0:T(8,128)}) custom-call(bf16[1,20,8,768]{3,2,1,0:T(8,128)(2,1)} %bitcast.30, bf16[1,36,8,768]{3,2,1,0:T(8,128)(2,1)} %bitcast.29, s32[8]{0:T(128)} %lengths_ref.1, s32[8]{0:T(128)} %flags_ref.1, ...), custom_call_target="tpu_custom_call" | custom-call | tf_op jit(solution)/shard_map/pallas_call | solution.py:1168
  179.4 3.3 %shard_map.315 = (f32[1,20,8,768]{3,2,1,0:T(8,128)}, f32[1,36,8,768]{3,2,1,0:T(8,128)}, f32[1,2,3,48,192]{4,3,2,1,0:T(8,128)}, f32[1,2,3,2,4]{4,3,2,1,0:T(2,128)...) custom-call(bf16[4,128,768]{2,1,0:T(8,128)(2,1)} %get-tuple-element., ...), custom_call_target="tpu_custom_call" | custom-call | tf_op jit(solution)/shard_map/pallas_call | solution.py:1273

commit v4 on v3

--- a/solution.py
+++ b/solution.py
@@ -202,282 +202,12 @@
     load_weights(0, 1, 2, 3)
     pl.when(cross)(lambda: load_weights(4, 5))
 
-    row = lax.broadcasted_iota(jnp.int32, (C, 1), 0) + me * C
-    is_word = row < RW
-    for k, ref in enumerate((out_bias_ref, gain_ref, shift_ref)):
-        for l in range(2):
-            rowp[2 * k + l] = jnp.where(is_word, ref[0, 0, l : l + 1, :], ref[0, 1, l : l + 1, :])
-
-    def side_by_side(rows):
-        return jnp.concatenate(rows, axis=1)
-
-    for mod in range(2):
-        b1_ref[mod] = side_by_side(
-            [b1_in_ref[0, k, mod : mod + 1, :] for k in range(D // 128)]
-        )
-    for k, ref in enumerate((qv_bias_ref.at[0, 0], qv_bias_ref.at[0, 1], cqv_bias_ref)):
-        heads = lambda j: [ref[h, j : j + 1, :] for h in range(LOCAL_HEADS)]
-        bqkv_ref[k] = side_by_side([*heads(0), jnp.zeros((1, HW), F32), *heads(1)])
-    for k, ref in enumerate((cout_bias_ref, cgain_ref, cshift_ref)):
-        cvec_ref[k : k + 1, :] = ref[...].reshape(1, D)
-
-    for ref, (lo, hi), length in zip((words_ref, regions_ref), SPANS, (WORDS, REGIONS)):
-        given = ref[0].astype(F32).reshape(ITEMS_LOCAL * length, D).astype(BF)
-        placed = dot(spread(hi - lo, length), given).astype(BF)
-        x_ref[:, lo:hi, :] = placed.reshape(MB, hi - lo, D)
-    acc[...] = jnp.zeros_like(acc)
-    bsum[...] = jnp.zeros_like(bsum)
-    bqsum[...] = jnp.zeros_like(bqsum)
-    row_sums[...] = jnp.zeros_like(row_sums)
-
-    pl.semaphore_wait(barrier, 12)
-
     def moved(src, dst, send_sem, recv_sem, device):
         return pltpu.make_async_remote_copy(
             src_ref=src, dst_ref=dst, send_sem=send_sem, recv_sem=recv_sem, device_id=device,
             device_id_type=MESH,
         )
 
-    def rs_copies(m):
-        return [
-            pltpu.make_async_remote_copy(
-                src_ref=send.at[m, rows_of(lax.rem(me + o, TENSOR))],
-                dst_ref=recv.at[m, o - 1],
-                send_sem=rs_send.at[m, o - 1],
-                recv_sem=rs_recv.at[m, o - 1],
-                device_id=peer(o),
-                device_id_type=MESH,
-            )
-            for o in range(1, TENSOR)
-        ]
-
-    def rs_start(m):
-        for copy in rs_copies(m):
-            copy.start()
-
-    def rs_finish(m):
-        for copy in rs_copies(m):
-            copy.wait()
-        total = send[m, own].astype(F32)
-        for o in range(TENSOR - 1):
-            total = total + recv[m, o].astype(F32)
-        return total
-
-    def ag_copies(buf, m, ss, rs):
-        return [
-            pltpu.make_async_remote_copy(
-                src_ref=buf.at[m, own],
-                dst_ref=buf.at[m, own],
-                send_sem=ss.at[m, o - 1],
-                recv_sem=rs.at[m, o - 1],
-                device_id=peer(o),
-                device_id_type=MESH,
-            )
-            for o in range(1, TENSOR)
-        ]
-
-    def ag_start(buf, m, ss=ag_send, rs=ag_recv):
-        for copy in ag_copies(buf, m, ss, rs):
-            copy.start()
-
-    def ag_finish(buf, m, ss=ag_send, rs=ag_recv):
-        for copy in ag_copies(buf, m, ss, rs):
-            copy.wait()
-
-    def mid_copy(m, k, t):
-        return moved(
-            midf.at[m, own], midf.at[m, own], sec_send.at[m, k], sec_recv.at[m, me],
-            {"section": 1 - sec, "tensor": t},
-        )
-
-    def mid_arrive(m):
-        for t in range(TENSOR):
-            rows = midf.at[m, pl.ds(t * C, C)]
-            moved(rows, rows, sec_send.at[m, 0], sec_recv.at[m, t], partner).wait_recv()
-
-    def back_copies(j):
-        m = 2 * set_of + j
-        first = 2 * (me // 2)
-        return [
-            moved(
-                back.at[m, rows_of(first + k)], back.at[m, rows_of(first + k)],
-                back_send.at[j, k], back_recv.at[m], {"section": 1 - sec, "tensor": first + k},
-            )
-            for k in range(2)
-        ]
-
-    def back_arrive(m):
-        rows = back.at[m, own]
-        moved(rows, rows, back_send.at[0, 0], back_recv.at[m], partner).wait_recv()
-
-    def save_norm(l, m, n, r):
-        nrm[l, m] = n
-        rstd[l, m] = jnp.broadcast_to(r, (C, 128))
-
-    def norm_step_back(l, m, dh, gain):
-        n = nrm[l, m]
-        dr = norm_back(dh, n, rstd[l, m][:, :1], gain)
-        low = dr.astype(BF)
-        acc[3 * l] += dh * n
-        acc[3 * l + 1] += dh
-        acc[3 * l + 2] += low.astype(F32)
-        res[m] = dr
-        return low
-
-    def word_keys(m, q_rows, q_len):
-        return key_mask(
-            q_rows, q_len, RW, WORDS, [lengths_ref[ITEMS_MB * m + k] for k in range(ITEMS_MB)]
-        )
-
-    def region_keys(q_rows, q_len):
-        return key_mask(q_rows, q_len, RR, REGIONS)
-
-    def layer_a(m):
-        xlow[m] = x_ref[m]
-        cur[m] = x_ref[m, own].astype(F32)
-        for mod, (lo, hi) in enumerate(SPANS):
-            out = (dot_nt(xlow[m, lo:hi], wqkv_ref[mod]) + bqkv_ref[mod]).astype(BF)
-            q, k, v = out[:, :HW], out[:, HW : 2 * HW], out[:, 2 * HW :]
-            qkv[0, m, lo:hi], qkv[1, m, lo:hi], qkv[2, m, lo:hi] = q, k, v
-            if mod == 0:
-                probs, mix = attend(q, k, v, word_keys(m, RW, WORDS))
-                p_w[m] = probs
-            else:
-                probs, mix = attend(q, k, v, region_keys(RR, REGIONS))
-                p_r[m] = probs
-            mixed[m, lo:hi] = mix
-            send[m, lo:hi] = dot(mix, wo_ref[mod]).astype(BF)
-        rs_start(m)
-
-    def layer_b(m):
-        r = cur[m] + rs_finish(m) + rowp[0]
-        n, rs, h = norm_forward(r, rowp[2], rowp[4])
-        save_norm(0, m, n, rs)
-        cur[m] = h
-        alow[m, own] = h.astype(BF)
-        ag_start(alow, m)
-
-    def layer_c(m):
-        ag_finish(alow, m)
-        for mod, (lo, hi) in enumerate(SPANS):
-            up = dot(alow[m, lo:hi], w1_ref[mod]) + b1_ref[mod]
-            cdf = 0.5 * (1.0 + lax.erf(up * (0.5**0.5)))
-            dgelu[m, lo:hi] = cdf + up * jnp.exp(-0.5 * up * up) * 0.3989422804014327
-            active = (up * cdf).astype(BF)
-            act[m, lo:hi] = active
-            send[m, lo:hi] = dot(active, w2_ref[mod]).astype(BF)
-        rs_start(m)
-
-    def layer_d(m):
-        r = cur[m] + rs_finish(m) + rowp[1]
-        n, rs, h = norm_forward(r, rowp[3], rowp[5])
-        save_norm(1, m, n, rs)
-        return h
-
-    def back_e(m, dh):
-        low = norm_step_back(1, m, dh, rowp[3])
-        dyf[m, own] = low
-        ag_start(dyf, m)
-
-    def back_f(m):
-        ag_finish(dyf, m)
-        for mod, (lo, hi) in enumerate(SPANS):
-            d = (dot_nt(dyf[m, lo:hi], w2_ref[mod]) * dgelu[m, lo:hi]).astype(BF)
-            dup[m, lo:hi] = d
-            bsum[mod] += jnp.sum(d.astype(F32), axis=0, keepdims=True)
-            send[m, lo:hi] = dot_nt(d, w1_ref[mod]).astype(BF)
-        rs_start(m)
-
-    def back_g(m):
-        dh = res[m] + rs_finish(m)
-        low = norm_step_back(0, m, dh, rowp[2])
-        dya[m, own] = low
-        ag_start(dya, m)
-
-    def back_h(m):
-        ag_finish(dya, m)
-        for mod, (lo, hi) in enumerate(SPANS):
-            dmix = dot_nt(dya[m, lo:hi], wo_ref[mod]).astype(BF)
-            probs = p_w[m] if mod == 0 else p_r[m]
-            parts = attend_back(
-                dmix, probs, qkv[0, m, lo:hi], qkv[1, m, lo:hi], qkv[2, m, lo:hi]
-            )
-            d = jnp.concatenate(parts, axis=1)
-            dqkv[m, lo:hi] = d
-            bqsum[mod] += jnp.sum(d.astype(F32), axis=0, keepdims=True)
-            send[m, lo:hi] = dot(d, wqkv_ref[mod]).astype(BF)
-        rs_start(m)
-
-    def block_of(j):
-        return 2 * set_of + j
-
-    def ar_copy(j, mod, turn):
-        lo, hi = SPANS[mod]
-        return moved(
-            send.at[j, lo:hi], got.at[turn, j, lo:hi], ar_send.at[turn, j, mod], ar_recv.at[turn, j, mod],
-            halver,
-        )
-
-    def ar_start(j, mod, turn, part):
-        lo, hi = SPANS[mod]
-        send[j, lo:hi] = part.astype(BF)
-        ar_copy(j, mod, turn).start()
-
-    def ar_finish(j, mod, turn):
-        lo, hi = SPANS[mod]
-        ar_copy(j, mod, turn).wait()
-        return send[j, lo:hi].astype(F32) + got[turn, j, lo:hi].astype(F32)
-
-    shared = (xlow, alow, dyf, dya, dyc, ybuf)
-    for_mate = ((act_m, act), (dup_m, dup), (mixed_m, mixed), (dqkv_m, dqkv), (cmixed_m, cmixed), (cdqkv_m, cdqkv))
-    XLOW, ALOW, DYF, DYA, DYC, YBUF, ACT, DUP, MIXED, DQKV, CMIXED, CDQKV = range(12)
-
-    halves = (DYA, DYC, YBUF)
-
-    def half_rows(which):
-        return pl.ds(pl.multiple_of(which * (R // 2), R // 2), R // 2)
-
-    def mate_copy(k, j, arriving=False):
-        if k < 6:
-            src = dst = shared[k]
-            src = src.at[block_of(j)]
-        else:
-            src, dst = for_mate[k - 6]
-            src = src.at[j]
-        dst = dst.at[2 * (1 - set_of) + j if arriving else block_of(j)]
-        if k in halves:
-            src, dst = src.at[half_rows(me // 2)], dst.at[half_rows(me // 2)]
-        return moved(src, dst, mt_send.at[k, j], mt_recv.at[k, j], mate)
-
-    def mate_start(j, *kinds):
-        for k in kinds:
-            mate_copy(k, j).start()
-
-    def mate_start_all(*kinds):
-        for k in kinds:
-            for j in range(2):
-                mate_copy(k, j).start()
-
-    def mate_wait(*kinds):
-        for k in kinds:
-            for j in range(2):
-                mate_copy(k, j, True).wait_recv()
-                mate_copy(k, j).wait_send()
-
-    def pass_copy(k, j, arriving=False):
-        rows = half_rows(1 - me // 2 if arriving else me // 2)
-        place = shared[k].at[2 * (1 - set_of) + j, rows]
-        return moved(place, place, ps_send.at[k, j], ps_recv.at[k, j], halver)
-
-    def pass_start(k):
-        for j in range(2):
-            pass_copy(k, j).start()
-
-    def pass_wait(k):
-        for j in range(2):
-            pass_copy(k, j, True).wait_recv()
-            pass_copy(k, j).wait_send()
-
     both_mods = slice(0, 2)
     half_columns = pl.ds(pl.multiple_of(core * (D // 2), D // 2), D // 2)
 
@@ -489,8 +219,8 @@
         (wqkv_in, wqkv_m, 3 * HW // 4, True), (wo_in, wo_m, HW // 4, True),
         (w1_in, w1_m, D // 4, True), (w2_in, w2_m, D // 4, True),
     )
-    Y_FIRST = (W1,) = (4,)
-    CWQKV, CWO, WQKV, WO, W2 = 0, 1, 2, 3, 5
+    CWQKV, CWO, WQKV, WO, W1, W2 = range(6)
+    Y_FIRST = (WQKV, W1)
 
     def gather_copies(k, step):
         src, dst, count, by_mod = gathered[k]
@@ -520,6 +250,286 @@
             for copy in gather_copies(k, step):
                 copy.wait()
 
+    @pl.when(cross)
+    def _():
+        pl.semaphore_wait(barrier, 12)
+        gather_start("x", CWQKV, CWO, WQKV, WO, W2, W1)
+
+    row = lax.broadcasted_iota(jnp.int32, (C, 1), 0) + me * C
+    is_word = row < RW
+    for k, ref in enumerate((out_bias_ref, gain_ref, shift_ref)):
+        for l in range(2):
+            rowp[2 * k + l] = jnp.where(is_word, ref[0, 0, l : l + 1, :], ref[0, 1, l : l + 1, :])
+
+    def side_by_side(rows):
+        return jnp.concatenate(rows, axis=1)
+
+    for mod in range(2):
+        b1_ref[mod] = side_by_side(
+            [b1_in_ref[0, k, mod : mod + 1, :] for k in range(D // 128)]
+        )
+    for k, ref in enumerate((qv_bias_ref.at[0, 0], qv_bias_ref.at[0, 1], cqv_bias_ref)):
+        heads = lambda j: [ref[h, j : j + 1, :] for h in range(LOCAL_HEADS)]
+        bqkv_ref[k] = side_by_side([*heads(0), jnp.zeros((1, HW), F32), *heads(1)])
+    for k, ref in enumerate((cout_bias_ref, cgain_ref, cshift_ref)):
+        cvec_ref[k : k + 1, :] = ref[...].reshape(1, D)
+
+    for ref, (lo, hi), length in zip((words_ref, regions_ref), SPANS, (WORDS, REGIONS)):
+        given = ref[0].astype(F32).reshape(ITEMS_LOCAL * length, D).astype(BF)
+        placed = dot(spread(hi - lo, length), given).astype(BF)
+        x_ref[:, lo:hi, :] = placed.reshape(MB, hi - lo, D)
+    acc[...] = jnp.zeros_like(acc)
+    bsum[...] = jnp.zeros_like(bsum)
+    bqsum[...] = jnp.zeros_like(bqsum)
+    row_sums[...] = jnp.zeros_like(row_sums)
+
+
+    def rs_copies(m):
+        return [
+            pltpu.make_async_remote_copy(
+                src_ref=send.at[m, rows_of(lax.rem(me + o, TENSOR))],
+                dst_ref=recv.at[m, o - 1],
+                send_sem=rs_send.at[m, o - 1],
+                recv_sem=rs_recv.at[m, o - 1],
+                device_id=peer(o),
+                device_id_type=MESH,
+            )
+            for o in range(1, TENSOR)
+        ]
+
+    def rs_start(m):
+        for copy in rs_copies(m):
+            copy.start()
+
+    def rs_finish(m):
+        for copy in rs_copies(m):
+            copy.wait()
+        total = send[m, own].astype(F32)
+        for o in range(TENSOR - 1):
+            total = total + recv[m, o].astype(F32)
+        return total
+
+    def ag_copies(buf, m, ss, rs):
+        return [
+            pltpu.make_async_remote_copy(
+                src_ref=buf.at[m, own],
+                dst_ref=buf.at[m, own],
+                send_sem=ss.at[m, o - 1],
+                recv_sem=rs.at[m, o - 1],
+                device_id=peer(o),
+                device_id_type=MESH,
+            )
+            for o in range(1, TENSOR)
+        ]
+
+    def ag_start(buf, m, ss=ag_send, rs=ag_recv):
+        for copy in ag_copies(buf, m, ss, rs):
+            copy.start()
+
+    def ag_finish(buf, m, ss=ag_send, rs=ag_recv):
+        for copy in ag_copies(buf, m, ss, rs):
+            copy.wait()
+
+    def mid_copy(m):
+        rows = midf.at[m, own]
+        return moved(rows, rows, sec_send.at[m], sec_recv.at[m], partner)
+
+    def mid_relay(m):
+        mid_copy(m).wait_recv()
+        ag_start(midf, m)
+
+    def back_copies(j):
+        m = 2 * set_of + j
+        first = 2 * (me // 2)
+        return [
+            moved(
+                back.at[m, rows_of(first + k)], back.at[m, rows_of(first + k)],
+                back_send.at[j, k], back_recv.at[m], {"section": 1 - sec, "tensor": first + k},
+            )
+            for k in range(2)
+        ]
+
+    def back_arrive(m):
+        rows = back.at[m, own]
+        moved(rows, rows, back_send.at[0, 0], back_recv.at[m], partner).wait_recv()
+
+    def save_norm(l, m, n, r):
+        nrm[l, m] = n
+        rstd[l, m] = jnp.broadcast_to(r, (C, 128))
+
+    def norm_step_back(l, m, dh, gain):
+        n = nrm[l, m]
+        dr = norm_back(dh, n, rstd[l, m][:, :1], gain)
+        low = dr.astype(BF)
+        acc[3 * l] += dh * n
+        acc[3 * l + 1] += dh
+        acc[3 * l + 2] += low.astype(F32)
+        res[m] = dr
+        return low
+
+    def word_keys(m, q_rows, q_len):
+        return key_mask(
+            q_rows, q_len, RW, WORDS, [lengths_ref[ITEMS_MB * m + k] for k in range(ITEMS_MB)]
+        )
+
+    def region_keys(q_rows, q_len):
+        return key_mask(q_rows, q_len, RR, REGIONS)
+
+    def layer_a(m):
+        xlow[m] = x_ref[m]
+        cur[m] = x_ref[m, own].astype(F32)
+        for mod, (lo, hi) in enumerate(SPANS):
+            out = (dot_nt(xlow[m, lo:hi], wqkv_ref[mod]) + bqkv_ref[mod]).astype(BF)
+            q, k, v = out[:, :HW], out[:, HW : 2 * HW], out[:, 2 * HW :]
+            qkv[0, m, lo:hi], qkv[1, m, lo:hi], qkv[2, m, lo:hi] = q, k, v
+            if mod == 0:
+                probs, mix = attend(q, k, v, word_keys(m, RW, WORDS))
+                p_w[m] = probs
+            else:
+                probs, mix = attend(q, k, v, region_keys(RR, REGIONS))
+                p_r[m] = probs
+            mixed[m, lo:hi] = mix
+            send[m, lo:hi] = dot(mix, wo_ref[mod]).astype(BF)
+
+        @pl.when(m == 1)
+        def _():
+            pl.semaphore_wait(barrier, 12)
+            rs_start(0)
+
+        @pl.when(m >= 1)
+        def _():
+            rs_start(m)
+
+
+    def layer_b(m):
+        r = cur[m] + rs_finish(m) + rowp[0]
+        n, rs, h = norm_forward(r, rowp[2], rowp[4])
+        save_norm(0, m, n, rs)
+        cur[m] = h
+        alow[m, own] = h.astype(BF)
+        ag_start(alow, m)
+
+    def layer_c(m):
+        ag_finish(alow, m)
+        for mod, (lo, hi) in enumerate(SPANS):
+            up = dot(alow[m, lo:hi], w1_ref[mod]) + b1_ref[mod]
+            cdf = 0.5 * (1.0 + lax.erf(up * (0.5**0.5)))
+            dgelu[m, lo:hi] = cdf + up * jnp.exp(-0.5 * up * up) * 0.3989422804014327
+            active = (up * cdf).astype(BF)
+            act[m, lo:hi] = active
+            send[m, lo:hi] = dot(active, w2_ref[mod]).astype(BF)
+        rs_start(m)
+
+    def layer_d(m):
+        r = cur[m] + rs_finish(m) + rowp[1]
+        n, rs, h = norm_forward(r, rowp[3], rowp[5])
+        save_norm(1, m, n, rs)
+        return h
+
+    def back_e(m, dh):
+        low = norm_step_back(1, m, dh, rowp[3])
+        dyf[m, own] = low
+        ag_start(dyf, m)
+
+    def back_f(m):
+        ag_finish(dyf, m)
+        for mod, (lo, hi) in enumerate(SPANS):
+            d = (dot_nt(dyf[m, lo:hi], w2_ref[mod]) * dgelu[m, lo:hi]).astype(BF)
+            dup[m, lo:hi] = d
+            bsum[mod] += jnp.sum(d.astype(F32), axis=0, keepdims=True)
+            send[m, lo:hi] = dot_nt(d, w1_ref[mod]).astype(BF)
+        rs_start(m)
+
+    def back_g(m):
+        dh = res[m] + rs_finish(m)
+        low = norm_step_back(0, m, dh, rowp[2])
+        dya[m, own] = low
+        ag_start(dya, m)
+
+    def back_h(m):
+        ag_finish(dya, m)
+        for mod, (lo, hi) in enumerate(SPANS):
+            dmix = dot_nt(dya[m, lo:hi], wo_ref[mod]).astype(BF)
+            probs = p_w[m] if mod == 0 else p_r[m]
+            parts = attend_back(
+                dmix, probs, qkv[0, m, lo:hi], qkv[1, m, lo:hi], qkv[2, m, lo:hi]
+            )
+            d = jnp.concatenate(parts, axis=1)
+            dqkv[m, lo:hi] = d
+            bqsum[mod] += jnp.sum(d.astype(F32), axis=0, keepdims=True)
+            send[m, lo:hi] = dot(d, wqkv_ref[mod]).astype(BF)
+        rs_start(m)
+
+    def block_of(j):
+        return 2 * set_of + j
+
+    def ar_copy(j, mod, turn):
+        lo, hi = SPANS[mod]
+        return moved(
+            send.at[j, lo:hi], got.at[turn, j, lo:hi], ar_send.at[turn, j, mod], ar_recv.at[turn, j, mod],
+            halver,
+        )
+
+    def ar_start(j, mod, turn, part):
+        lo, hi = SPANS[mod]
+        send[j, lo:hi] = part.astype(BF)
+        ar_copy(j, mod, turn).start()
+
+    def ar_finish(j, mod, turn):
+        lo, hi = SPANS[mod]
+        ar_copy(j, mod, turn).wait()
+        return send[j, lo:hi].astype(F32) + got[turn, j, lo:hi].astype(F32)
+
+    shared = (xlow, alow, dyf, dya, dyc, ybuf)
+    for_mate = ((act_m, act), (dup_m, dup), (mixed_m, mixed), (dqkv_m, dqkv), (cmixed_m, cmixed), (cdqkv_m, cdqkv))
+    XLOW, ALOW, DYF, DYA, DYC, YBUF, ACT, DUP, MIXED, DQKV, CMIXED, CDQKV = range(12)
+
+    halves = (XLOW, DYA, DYC, YBUF)
+
+    def half_rows(which):
+        return pl.ds(pl.multiple_of(which * (R // 2), R // 2), R // 2)
+
+    def mate_copy(k, j, arriving=False):
+        if k < 6:
+            src = dst = shared[k]
+            src = src.at[block_of(j)]
+        else:
+            src, dst = for_mate[k - 6]
+            src = src.at[j]
+        dst = dst.at[2 * (1 - set_of) + j if arriving else block_of(j)]
+        if k in halves:
+            src, dst = src.at[half_rows(me // 2)], dst.at[half_rows(me // 2)]
+        return moved(src, dst, mt_send.at[k, j], mt_recv.at[k, j], mate)
+
+    def mate_start(j, *kinds):
+        for k in kinds:
+            mate_copy(k, j).start()
+
+    def mate_start_all(*kinds):
+        for k in kinds:
+            for j in range(2):
+                mate_copy(k, j).start()
+
+    def mate_wait(*kinds):
+        for k in kinds:
+            for j in range(2):
+                mate_copy(k, j, True).wait_recv()
+                mate_copy(k, j).wait_send()
+
+    def pass_copy(k, j, arriving=False):
+        rows = half_rows(1 - me // 2 if arriving else me // 2)
+        place = shared[k].at[2 * (1 - set_of) + j, rows]
+        return moved(place, place, ps_send.at[k, j], ps_recv.at[k, j], halver)
+
+    def pass_start(k):
+        for j in range(2):
+            pass_copy(k, j).start()
+
+    def pass_wait(k):
+        for j in range(2):
+            pass_copy(k, j, True).wait_recv()
+            pass_copy(k, j).wait_send()
+
     def bias_copies():
         return [
             moved(bqkv_ref, bqkv_m, ga_send.at[6, 0], ga_recv.at[6, 0], mate),
@@ -537,26 +547,27 @@
 
     def cross_forward(j):
         m = block_of(j)
-        mid_arrive(m)
+        ag_finish(midf, m)
         mid = midf[m]
-        part = None
         shards = ((cwqkv_ref, bqkv_ref, cwo_ref, cmixed, m), (cwqkv_m, bqkv_m, cwo_m, cmixed_m, j))
+        qkvs = []
         for sh, (w, bias, w_out, keep, at) in enumerate(shards):
-            slot = 2 * sh + j
             out = (dot_nt(mid, w[...]) + bias[2]).astype(BF)
             q, k, v = out[:, :HW], out[:, HW : 2 * HW], out[:, 2 * HW :]
-            cqkv[0, slot], cqkv[1, slot], cqkv[2, slot] = q, k, v
-            probs, mix = attend(q[:RW], k[RW:], v[RW:], region_keys(RW, WORDS))
-            cp_w[slot] = probs
-            keep[at, :RW] = mix
-            probs, mix = attend(q[RW:], k[:RW], v[:RW], word_keys(m, RR, REGIONS))
-            cp_r[slot] = probs
-            keep[at, RW:] = mix
-            one = dot(keep[at], w_out[...])
-            part = one if part is None else part + one
+            cqkv[0, 2 * sh + j], cqkv[1, 2 * sh + j], cqkv[2, 2 * sh + j] = q, k, v
+            qkvs.append((q, k, v))
         for mod, (lo, hi) in enumerate(SPANS):
-            ar_start(j, mod, 0, part[lo:hi])
-        mate_start(j, CMIXED)
+            others = slice(*SPANS[1 - mod])
+            part = None
+            for sh, (w, bias, w_out, keep, at) in enumerate(shards):
+                q, k, v = qkvs[sh]
+                mask = region_keys(RW, WORDS) if mod == 0 else word_keys(m, RR, REGIONS)
+                probs, mix = attend(q[lo:hi], k[others], v[others], mask)
+                (cp_w, cp_r)[mod][2 * sh + j] = probs
+                keep[at, lo:hi] = mix
+                one = dot(mix, w_out[...])
+                part = one if part is None else part + one
+            ar_start(j, mod, 0, part)
 
     def attn_forward(j):
         m = block_of(j)
@@ -586,7 +597,7 @@
                 one = dot(mix, w_out[mod])
                 part = one if part is None else part + one
             ar_start(j, mod, 1, part)
-        mate_start(j, XLOW, MIXED)
+        mate_start(j, XLOW)
 
     def ffn_forward(j):
         m = block_of(j)
@@ -600,11 +611,15 @@
             alow[m, lo:hi] = low
             part = None
             for sh, (w, bias, w_out, keep, at) in enumerate(shards):
+                if mod == 0 and sh == 1:
+                    pl.when(j == 0)(lambda: gather_wait("core", W1))
                 up = dot(low, w[mod]) + bias[mod]
                 cdf = 0.5 * (1.0 + lax.erf(up * (0.5**0.5)))
                 dgelu[2 * sh + j, lo:hi] = cdf + up * jnp.exp(-0.5 * up * up) * 0.3989422804014327
                 active = (up * cdf).astype(BF)
                 keep[at, lo:hi] = active
+                if mod == 0 and sh == 1:
+                    pl.when(j == 0)(lambda: gather_wait("core", W2))
                 one = dot(active, w_out[mod])
                 part = one if part is None else part + one
             ar_start(j, mod, 0, part)
@@ -632,8 +647,7 @@
                 one = dot_nt(d, w_in[mod])
                 part = one if part is None else part + one
             ar_start(j, mod, 1, part)
-        mate_start(j, DYF)
-        pl.when(j == 0)(lambda: mate_start(0, DUP))
+        mate_start(j, DYF, DUP)
 
     def attn_backward(j):
         m = block_of(j)
@@ -725,7 +739,7 @@
     def ffn_piece(k):
         mod, second = k // 2, k % 2
         left, right = ((alow, dup), (dyf, act))[second]
-        outer(left, right, *SPANS[mod], store_at(1 + 4 * mod + second, 0, D))
+        outer(left, right, *SPANS[mod], store_at((5, 1)[second] + mod, 0, D))
 
     def attn_piece(k):
         mod, second = k // 2, k % 2
@@ -810,11 +824,8 @@
         dw_finish(group, phase)
         dw_start(group, phase + 1)
 
-    FFN_W = (0, True, 1, 3)
-    FFN_R = (1, False, 5, 7)
-    ATTN_W = (2, True, 0, 1)
-    ATTN_R = (3, False, 4, 5)
-    CROSS = (4, True, 3, 4)
+    OUT_W, OUT_R, IN_W, IN_R = (0, True, 1, 2), (1, True, 2, 3), (2, False, 5, 6), (3, False, 6, 7)
+    ATTN_W, ATTN_R, CROSS = (4, True, 0, 1), (5, False, 4, 5), (6, True, 3, 4)
 
     def sm_copies(step):
         sems = lambda k: (sm_send.at[k], sm_recv.at[k])
@@ -910,18 +921,10 @@
     def _():
         def to_partner(m):
             midf[m, own] = layer_d(m).astype(BF)
-            first = m // 2
-            for k, t in enumerate((first, 3 - first)):
-                mid_copy(m, k, t).start()
-
-        def to_others(m):
-            first = m // 2
-            for k, t in enumerate((1 - first, 2 + first)):
-                mid_copy(m, 2 + k, t).start()
+            mid_copy(m).start()
 
         def from_partner(m):
-            for k in range(TENSOR):
-                mid_copy(m, k, 0).wait_send()
+            mid_copy(m).wait_send()
             back_arrive(m)
             back_e(m, back[m, own].astype(F32))
 
@@ -935,125 +938,142 @@
         each(layer_b)
         each(layer_c)
         each(to_partner)
-        each(to_others)
         each(from_partner)
         each(back_f)
-        ffn_piece(2)
-        ffn_piece(3)
-        dw_start(FFN_R, 0)
         each(
             back_g,
             after=(
-                p(ffn_piece, 0),
-                then(p(dw_turn, FFN_R, 0), p(ffn_piece, 1), p(dw_start, FFN_W, 0)),
+                then(p(ffn_piece, 2), p(dw_start, IN_R, 0)),
+                then(p(ffn_piece, 3), p(dw_start, OUT_R, 0)),
+                then(p(dw_turn, IN_R, 0), p(ffn_piece, 0), p(dw_start, IN_W, 0)),
+                then(p(dw_turn, OUT_R, 0), p(ffn_piece, 1), p(dw_start, OUT_W, 0)),
             ),
         )
         small_norms()
-        each(back_h, after=(p(dw_turn, FFN_W, 0),))
+        each(
+            back_h,
+            after=(
+                then(p(dw_turn, IN_W, 0), p(dw_turn, OUT_W, 0)), None, p(dw_turn, IN_R, 1),
+                p(dw_turn, OUT_R, 1),
+            ),
+        )
+        small_biases()
         attn_piece(2)
         attn_piece(3)
         dw_start(ATTN_R, 0)
+        small_y()
         attn_piece(0)
         attn_piece(1)
         dw_start(ATTN_W, 0)
-        small_biases()
-        each(last, after=(p(dw_turn, ATTN_R, 0), p(dw_turn, FFN_R, 1), p(dw_turn, ATTN_W, 0)))
-        small_y()
-        dw_turn(FFN_W, 1)
+        dw_turn(ATTN_R, 0)
+        dw_turn(IN_W, 1)
+        dw_turn(ATTN_W, 0)
+        dw_turn(OUT_W, 1)
+        each(last)
         small_z()
 
     @pl.when(cross)
     def _():
-        gather_start("x", CWQKV, CWO, WQKV, WO)
         for copy in bias_copies():
             copy.start()
-        gather_start("x", W2, W1)
         gather_wait("x", CWQKV, CWO)
         gather_start("z", CWQKV, CWO)
         gather_wait("x", WQKV, WO)
-        gather_start("z", WQKV, WO)
+        gather_start("y", WQKV)
+        gather_start("z", WO)
         gather_wait("x", W2, W1)
         gather_start("y", W1)
-        gather_start("z", W2)
+        gather_wait("y", WQKV)
+        gather_start("z", WQKV)
         gather_wait("z", CWQKV, CWO)
         gather_start("core", CWQKV, CWO)
+        gather_start("z", W2)
+        gather_wait("z", WO)
+        gather_start("y", WO)
         gather_wait("y", W1)
         gather_start("z", W1)
-        gather_wait("z", WQKV, WO)
-        gather_start("y", WQKV, WO)
         for copy in bias_copies():
             copy.wait()
         gather_wait("core", CWQKV, CWO)
+        gather_wait("y", WO)
+        gather_wait("z", WQKV)
+        gather_start("core", WQKV, WO)
         wait_weights(0, 1, 2, 3, 4, 5)
+        pl.loop(0, 3)(mid_relay)
+        pl.when(set_of == 1)(lambda: mid_relay(3))
         cross_forward(0)
+        pl.when(set_of == 0)(lambda: mid_relay(3))
         gather_wait("z", W2)
         gather_start("y", W2)
-        gather_wait("y", WQKV, WO)
-        gather_start("core", WQKV, WO)
         cross_forward(1)
         gather_wait("core", WQKV, WO)
         attn_forward(0)
         gather_wait("z", W1)
+        gather_start("core", W1)
+        attn_forward(1)
         gather_wait("y", W2)
-        gather_start("core", W1, W2)
-        attn_forward(1)
-        gather_wait("core", W1, W2)
+        gather_start("core", W2)
         pair(ffn_forward)
         pair(ffn_turn)
         pair(attn_backward)
         pair(cross_backward)
         pair(to_section_0)
-        mate_start_all(DYC)
-        mate_start(1, DUP)
-        mate_start_all(CDQKV)
+        mate_wait(XLOW, ALOW, ACT, DYF, DUP)
+        mate_start_all(DYC, CDQKV, CMIXED)
+        pass_start(XLOW)
+        ffn_piece(2)
+        dw_start(IN_R, 0)
+        ffn_piece(3)
+        dw_start(OUT_R, 0)
+        ffn_piece(0)
+        dw_start(IN_W, 0)
+        dw_turn(IN_R, 0)
+        ffn_piece(1)
+        dw_start(OUT_W, 0)
+        dw_turn(OUT_R, 0)
         small_norms_all()
-        mate_wait(CMIXED, XLOW, MIXED, ALOW, ACT, DYF)
+        for mod, (lo, hi) in enumerate(SPANS):
+            bsum[mod] = column_sums(dup, lo, hi)
+        dw_turn(IN_W, 0)
+        dw_turn(OUT_W, 0)
         mate_wait(DYC)
         pass_start(DYC)
-        mate_start_all(DYA)
-        mate_wait(DUP)
-        mate_start_all(DQKV)
-        ffn_piece(2)
-        ffn_piece(3)
-        dw_start(FFN_R, 0)
-        ffn_piece(0)
-        ffn_piece(1)
-        dw_start(FFN_W, 0)
-        for mod, (lo, hi) in enumerate(SPANS):
-            bsum[mod] = column_sums(dup, lo, hi)
-        dw_turn(FFN_R, 0)
-        dw_turn(FFN_W, 0)
-        mate_wait(DYA)
-        pass_start(DYA)
+        mate_start_all(DYA, DQKV, MIXED)
         for k in range(2):
-            mid_arrive(2 * (1 - set_of) + k)
-        mate_wait(CDQKV)
-        mate_start_all(YBUF)
+            ag_finish(midf, 2 * (1 - set_of) + k)
+        mate_wait(CDQKV, CMIXED)
         pass_wait(DYC)
         cross_outer()
         dw_start(CROSS, 0)
         bqsum[2] = column_sums(cdqkv, 0, R)
         dw_turn(CROSS, 0)
-        mate_wait(DQKV)
+        mate_wait(DYA)
+        pass_start(DYA)
+        dw_turn(IN_R, 1)
+        dw_turn(OUT_R, 1)
+        dw_turn(IN_W, 1)
+        dw_turn(OUT_W, 1)
+        mate_wait(DQKV, MIXED)
+        mate_start_all(YBUF)
+        pass_wait(XLOW)
         pass_wait(DYA)
+        for mod, (lo, hi) in enumerate(SPANS):
+            bqsum[mod] = column_sums(dqkv, lo, hi)
+        small_biases()
         attn_piece(2)
         attn_piece(3)
         dw_start(ATTN_R, 0)
+        small_y()
         attn_piece(0)
         attn_piece(1)
         dw_start(ATTN_W, 0)
-        for mod, (lo, hi) in enumerate(SPANS):
-            bqsum[mod] = column_sums(dqkv, lo, hi)
-        small_biases()
+        dw_turn(CROSS, 1)
+        dw_turn(ATTN_R, 0)
+        small_z()
+        dw_turn(ATTN_W, 0)
         mate_wait(YBUF)
         pass_start(YBUF)
-        dw_turn(FFN_R, 1)
-        dw_turn(CROSS, 1)
-        dw_turn(ATTN_R, 0)
-        dw_turn(ATTN_W, 0)
-        small_y()
-        dw_turn(FFN_W, 1)
-        small_z()
+        dw_finish(CROSS, 2)
         pass_wait(YBUF)
         pair(lambda j: [copy.wait_send() for copy in back_copies(j)] and None)
 
@@ -1064,16 +1084,17 @@
 
         y_ref[m] = ybuf[m]
 
+    dw_finish(IN_R, 2)
+    dw_finish(OUT_R, 2)
+    dw_turn(ATTN_R, 1)
+    dw_finish(IN_W, 2)
+    dw_finish(OUT_W, 2)
+    dw_turn(ATTN_W, 1)
+    small_last()
     each(write)
-    dw_finish(FFN_R, 2)
-    dw_turn(ATTN_R, 1)
-    dw_turn(ATTN_W, 1)
-    dw_finish(FFN_W, 2)
-    small_last()
 
     @pl.when(cross)
     def _():
-        dw_finish(CROSS, 2)
         pack[0, :24] = dw_ref[3, :24]
         pack[0, 24:] = s_ref[...]
         packet().start()
@@ -1112,8 +1133,8 @@
         for j in range(3):
             qkv_g[0, mod, j] = attn[:, j * HW : (j + 1) * HW]
         out_g[0, mod] = attn[:, 3 * HW :]
-        in_g[0, mod] = dw_ref[4 * mod + 1]
-        ffo_g[0, mod] = dw_ref[4 * mod + 2]
+        in_g[0, mod] = dw_ref[5 + mod]
+        ffo_g[0, mod] = dw_ref[1 + mod]
     columns = from_column(small, 48 * place)[:, :48]
     for mod in range(2):
         for l in range(2):
@@ -1239,10 +1260,10 @@
             pltpu.VMEM((3, 24, D), F32),
             pltpu.VMEM((2, 48, D), F32),
             *[pltpu.SemaphoreType.DMA((MB, TENSOR - 1)) for _ in range(6)],
-            pltpu.SemaphoreType.DMA((MB, TENSOR)),
-            pltpu.SemaphoreType.DMA((MB, TENSOR)),
-            pltpu.SemaphoreType.DMA((5, 5)),
-            pltpu.SemaphoreType.DMA((5, 5)),
+            pltpu.SemaphoreType.DMA((MB,)),
+            pltpu.SemaphoreType.DMA((MB,)),
+            pltpu.SemaphoreType.DMA((7, 5)),
+            pltpu.SemaphoreType.DMA((7, 5)),
             pltpu.SemaphoreType.DMA((8,)),
             pltpu.SemaphoreType.DMA((8,)),
             pltpu.SemaphoreType.DMA,

time: 183 us -> 166 us (0.907)
  Pallas kernels: 182 us -> 165 us
    pallas_call x1, Pallas kernels: 179 us -> 161 us  [local(): pl.pallas_call(kernel, out_shape=(jax.ShapeDtypeStruct((MB, R, D), BF), j...]
where the time goes in v4:
time: 166 us
  Pallas kernels  165 us (99%)
    pallas_call x1, Pallas kernels, local(): pl.pallas_call(kernel, out_shape=(jax.ShapeDtypeStruct((MB, R, D), BF), j...  161 us

profile of v4, /device:TPU:0, one launch (start us, length us, event | category | flops | bytes accessed | tf_op | source)
XLA Modules:
  0.0 165.6 jit_solution(7623391789629565688)
XLA Ops:
  0.7 161.5 %shard_map.314 = (bf16[4,128,768]{2,1,0:T(8,128)(2,1)}, f32[7,48,768]{2,1,0:T(8,128)}, f32[24,768]{1,0:T(8,128)}, f32[24,768]{1,0:T(8,128)}, f32[24,768]{1,0:T(8,128)}) custom-call(bf16[1,20,8,768]{3,2,1,0:T(8,128)(2,1)} %bitcast.30, bf16[1,36,8,768]{3,2,1,0:T(8,128)(2,1)} %bitcast.29, s32[8]{0:T(128)} %lengths_ref.1, s32[8]{0:T(128)} %flags_ref.1, ...), custom_call_target="tpu_custom_call" | custom-call | tf_op jit(solution)/shard_map/pallas_call | solution.py:1189
  162.1 3.3 %shard_map.315 = (f32[1,20,8,768]{3,2,1,0:T(8,128)}, f32[1,36,8,768]{3,2,1,0:T(8,128)}, f32[1,2,3,48,192]{4,3,2,1,0:T(8,128)}, f32[1,2,3,2,4]{4,3,2,1,0:T(2,128)...) custom-call(bf16[4,128,768]{2,1,0:T(8,128)(2,1)} %get-tuple-element., ...), custom_call_target="tpu_custom_call" | custom-call | tf_op jit(solution)/shard_map/pallas_call | solution.py:1294

commit v5 on v4

--- a/solution.py
+++ b/solution.py
@@ -227,18 +227,20 @@
         sems = lambda i: (ga_send.at[k, i], ga_recv.at[k, i])
         at = lambda mods, rows: (mods, rows, half_columns) if by_mod else (rows, half_columns)
         mine = at(y_at, z_rows(z_at, count))
+        column = at(y_at, slice(0, 4 * count)) if by_mod else None
         if step == "x":
-            return [moved(src.at[mine], dst.at[mine], *sems(0), mate)]
+            part = column if k == W2 else mine
+            return [moved(src.at[part], dst.at[part], *sems(0), mate)]
         if step == "y":
-            place = dst.at[mine] if k in Y_FIRST else dst.at[at(y_at, slice(0, 4 * count))]
+            place = dst.at[mine] if k in Y_FIRST else dst.at[column]
             return [moved(place, place, *sems(1), other_y)]
         if step == "z":
             place = dst.at[at(both_mods if k in Y_FIRST else y_at, z_rows(z_at, count))]
             return [
-                moved(place, place, *sems(1 + o), dp_device(y_at, z_next(o), core)) for o in (1, 2, 3)
+                moved(place, place, *sems(2), dp_device(y_at, z_next(o), core)) for o in (1, 2, 3)
             ]
         place = dst.at[at(both_mods, slice(0, 4 * count))]
-        return [moved(place, place, *sems(5), other_core)]
+        return [moved(place, place, *sems(3), other_core)]
 
     def gather_start(step, *arrays):
         for k in arrays:
@@ -247,13 +249,19 @@
 
     def gather_wait(step, *arrays):
         for k in arrays:
-            for copy in gather_copies(k, step):
-                copy.wait()
+            if step != "z":
+                gather_copies(k, step)[0].wait()
+                continue
+            _, dst, count, by_mod = gathered[k]
+            rows = slice(0, 3 * count)
+            mods = both_mods if k in Y_FIRST else y_at
+            place = dst.at[(mods, rows, half_columns) if by_mod else (rows, half_columns)]
+            moved(place, place, ga_send.at[k, 2], ga_recv.at[k, 2], mate).wait()
 
     @pl.when(cross)
     def _():
         pl.semaphore_wait(barrier, 12)
-        gather_start("x", CWQKV, CWO, WQKV, WO, W2, W1)
+        gather_start("x", CWQKV, CWO, WQKV, WO, W1, W2)
 
     row = lax.broadcasted_iota(jnp.int32, (C, 1), 0) + me * C
     is_word = row < RW
@@ -289,8 +297,8 @@
             pltpu.make_async_remote_copy(
                 src_ref=send.at[m, rows_of(lax.rem(me + o, TENSOR))],
                 dst_ref=recv.at[m, o - 1],
-                send_sem=rs_send.at[m, o - 1],
-                recv_sem=rs_recv.at[m, o - 1],
+                send_sem=rs_send.at[m],
+                recv_sem=rs_recv.at[m],
                 device_id=peer(o),
                 device_id_type=MESH,
             )
@@ -302,8 +310,7 @@
             copy.start()
 
     def rs_finish(m):
-        for copy in rs_copies(m):
-            copy.wait()
+        moved(recv.at[m], recv.at[m], rs_send.at[m], rs_recv.at[m], peer(1)).wait()
         total = send[m, own].astype(F32)
         for o in range(TENSOR - 1):
             total = total + recv[m, o].astype(F32)
@@ -314,8 +321,8 @@
             pltpu.make_async_remote_copy(
                 src_ref=buf.at[m, own],
                 dst_ref=buf.at[m, own],
-                send_sem=ss.at[m, o - 1],
-                recv_sem=rs.at[m, o - 1],
+                send_sem=ss.at[m],
+                recv_sem=rs.at[m],
                 device_id=peer(o),
                 device_id_type=MESH,
             )
@@ -327,8 +334,8 @@
             copy.start()
 
     def ag_finish(buf, m, ss=ag_send, rs=ag_recv):
-        for copy in ag_copies(buf, m, ss, rs):
-            copy.wait()
+        three = buf.at[m, pl.ds(0, (TENSOR - 1) * C)]
+        moved(three, three, ss.at[m], rs.at[m], peer(1)).wait()
 
     def mid_copy(m):
         rows = midf.at[m, own]
@@ -344,14 +351,14 @@
         return [
             moved(
                 back.at[m, rows_of(first + k)], back.at[m, rows_of(first + k)],
-                back_send.at[j, k], back_recv.at[m], {"section": 1 - sec, "tensor": first + k},
+                back_send.at[j], back_recv.at[m], {"section": 1 - sec, "tensor": first + k},
             )
             for k in range(2)
         ]
 
     def back_arrive(m):
         rows = back.at[m, own]
-        moved(rows, rows, back_send.at[0, 0], back_recv.at[m], partner).wait_recv()
+        moved(rows, rows, back_send.at[0], back_recv.at[m], partner).wait_recv()
 
     def save_norm(l, m, n, r):
         nrm[l, m] = n
@@ -391,16 +398,6 @@
             mixed[m, lo:hi] = mix
             send[m, lo:hi] = dot(mix, wo_ref[mod]).astype(BF)
 
-        @pl.when(m == 1)
-        def _():
-            pl.semaphore_wait(barrier, 12)
-            rs_start(0)
-
-        @pl.when(m >= 1)
-        def _():
-            rs_start(m)
-
-
     def layer_b(m):
         r = cur[m] + rs_finish(m) + rowp[0]
         n, rs, h = norm_forward(r, rowp[2], rowp[4])
@@ -484,22 +481,22 @@
     for_mate = ((act_m, act), (dup_m, dup), (mixed_m, mixed), (dqkv_m, dqkv), (cmixed_m, cmixed), (cdqkv_m, cdqkv))
     XLOW, ALOW, DYF, DYA, DYC, YBUF, ACT, DUP, MIXED, DQKV, CMIXED, CDQKV = range(12)
 
-    halves = (XLOW, DYA, DYC, YBUF)
+    halves = (XLOW, DYF, DYA, DYC, YBUF)
 
     def half_rows(which):
         return pl.ds(pl.multiple_of(which * (R // 2), R // 2), R // 2)
 
-    def mate_copy(k, j, arriving=False):
+    def mate_copy(k, j):
         if k < 6:
             src = dst = shared[k]
             src = src.at[block_of(j)]
         else:
             src, dst = for_mate[k - 6]
             src = src.at[j]
-        dst = dst.at[2 * (1 - set_of) + j if arriving else block_of(j)]
+        dst = dst.at[block_of(j)]
         if k in halves:
             src, dst = src.at[half_rows(me // 2)], dst.at[half_rows(me // 2)]
-        return moved(src, dst, mt_send.at[k, j], mt_recv.at[k, j], mate)
+        return moved(src, dst, mt_send.at[k], mt_recv.at[k], mate)
 
     def mate_start(j, *kinds):
         for k in kinds:
@@ -512,28 +509,25 @@
 
     def mate_wait(*kinds):
         for k in kinds:
-            for j in range(2):
-                mate_copy(k, j, True).wait_recv()
-                mate_copy(k, j).wait_send()
-
-    def pass_copy(k, j, arriving=False):
-        rows = half_rows(1 - me // 2 if arriving else me // 2)
-        place = shared[k].at[2 * (1 - set_of) + j, rows]
-        return moved(place, place, ps_send.at[k, j], ps_recv.at[k, j], halver)
+            place = (shared[k] if k < 6 else for_mate[k - 6][1]).at[pl.ds(2 * (1 - set_of), 2)]
+            if k in halves:
+                place = place.at[:, half_rows(me // 2)]
+            moved(place, place, mt_send.at[k], mt_recv.at[k], mate).wait()
+
+    def pass_copy(k):
+        place = shared[k].at[pl.ds(2 * (1 - set_of), 2), half_rows(me // 2)]
+        return moved(place, place, ps_send.at[k], ps_recv.at[k], halver)
 
     def pass_start(k):
-        for j in range(2):
-            pass_copy(k, j).start()
+        pass_copy(k).start()
 
     def pass_wait(k):
-        for j in range(2):
-            pass_copy(k, j, True).wait_recv()
-            pass_copy(k, j).wait_send()
+        pass_copy(k).wait()
 
     def bias_copies():
         return [
             moved(bqkv_ref, bqkv_m, ga_send.at[6, 0], ga_recv.at[6, 0], mate),
-            moved(b1_ref, b1_m, ga_send.at[7, 0], ga_recv.at[7, 0], mate),
+            moved(b1_ref, b1_m, ga_send.at[6, 1], ga_recv.at[6, 1], mate),
         ]
 
     def save_norm_f(l, j, lo, hi, n, r):
@@ -568,6 +562,7 @@
                 one = dot(mix, w_out[...])
                 part = one if part is None else part + one
             ar_start(j, mod, 0, part)
+        mate_start(j, CMIXED)
 
     def attn_forward(j):
         m = block_of(j)
@@ -597,7 +592,7 @@
                 one = dot(mix, w_out[mod])
                 part = one if part is None else part + one
             ar_start(j, mod, 1, part)
-        mate_start(j, XLOW)
+        mate_start(j, XLOW, MIXED)
 
     def ffn_forward(j):
         m = block_of(j)
@@ -772,7 +767,7 @@
             return [
                 moved(
                     g_ref.at[blocks, y_at, z_next(o), core], from_z.at[blocks, o - 1],
-                    *sems(1 + o), dp_device(y_at, z_next(o), core),
+                    *sems(2), dp_device(y_at, z_next(o), core),
                 )
                 for o in (1, 2, 3)
             ]
@@ -781,7 +776,7 @@
             return [
                 moved(
                     g_ref.at[blocks, :, z_next(o), core], from_zs.at[late, o - 1],
-                    *sems(1 + o), dp_device(y_at, z_next(o), core),
+                    *sems(2), dp_device(y_at, z_next(o), core),
                 )
                 for o in (1, 2, 3)
             ]
@@ -793,9 +788,12 @@
             copy.start()
 
     def dw_finish(group, phase):
-        for copy in dw_copies(group, phase):
-            copy.wait()
         index, y_first, lo, hi = group
+        if phase == (2 if y_first else 1):
+            place = from_z.at[slice(lo, hi)] if y_first else from_zs.at[slice(lo - 4, hi - 4)]
+            moved(place, place, dw_send.at[index, 2], dw_recv.at[index, 2], other_core).wait()
+        else:
+            dw_copies(group, phase)[0].wait()
 
         def add(b):
             if phase == 0:
@@ -831,15 +829,15 @@
         sems = lambda k: (sm_send.at[k], sm_recv.at[k])
         if step == 0:
             return [
-                moved(sums_t.at[me], sums_t.at[me], *sems(o - 1), peer(o)) for o in range(1, TENSOR)
+                moved(sums_t.at[me], sums_t.at[me], *sems(0), peer(o)) for o in range(1, TENSOR)
             ]
         if step == 1:
-            return [moved(sums.at[0], sums_c, *sems(3), other_core)]
+            return [moved(sums.at[0], sums_c, *sems(1), other_core)]
         if step == 2:
-            return [moved(sums.at[1], sums_y, *sems(4), other_y)]
+            return [moved(sums.at[1], sums_y, *sems(2), other_y)]
         return [
             moved(
-                sums.at[2], sums_z.at[o - 1], *sems(4 + o), dp_device(y_at, z_next(o), core)
+                sums.at[2], sums_z.at[o - 1], *sems(3), dp_device(y_at, z_next(o), core)
             )
             for o in (1, 2, 3)
         ]
@@ -849,8 +847,11 @@
             copy.start()
 
     def sm_wait(step):
-        for copy in sm_copies(step):
-            copy.wait()
+        if step in (0, 3):
+            place = sums_z if step == 3 else sums_t.at[pl.ds(0, TENSOR - 1)]
+            moved(place, place, sm_send.at[step], sm_recv.at[step], other_core).wait()
+        else:
+            sm_copies(step)[0].wait()
 
     def small_norms_all():
         for k in range(15):
@@ -897,15 +898,15 @@
     def packet():
         return moved(pack.at[0], pack.at[1], pk_send, pk_recv, partner)
 
-    def each(*steps, after=()):
+    def each(*steps, first=0, last=MB, after=()):
         def body(m):
             for step in steps:
                 step(m)
             for k, extra in enumerate(after):
                 if extra is not None:
-                    pl.when(m == k)(extra)
-
-        pl.loop(0, MB)(body)
+                    pl.when(m == first + k)(extra)
+
+        pl.loop(first, last)(body)
 
     def then(*steps):
         def run():
@@ -932,45 +933,59 @@
             ybuf[m, own] = (res[m] + rs_finish(m)).astype(BF)
             ag_start(ybuf, m, y_send, y_recv)
 
+        front, rear = dict(first=0, last=2), dict(first=2, last=4)
         wait_weights(0, 1)
-        each(layer_a)
-        wait_weights(2, 3)
-        each(layer_b)
-        each(layer_c)
-        each(to_partner)
-        each(from_partner)
-        each(back_f)
         each(
-            back_g,
+            layer_a,
             after=(
-                then(p(ffn_piece, 2), p(dw_start, IN_R, 0)),
-                then(p(ffn_piece, 3), p(dw_start, OUT_R, 0)),
-                then(p(dw_turn, IN_R, 0), p(ffn_piece, 0), p(dw_start, IN_W, 0)),
-                then(p(dw_turn, OUT_R, 0), p(ffn_piece, 1), p(dw_start, OUT_W, 0)),
+                None, then(p(pl.semaphore_wait, barrier, 12), p(rs_start, 0), p(rs_start, 1)),
+                p(rs_start, 2),
             ),
         )
-        small_norms()
+        each(layer_b, **front)
+        rs_start(3)
+        layer_b(2)
+        wait_weights(2, 3)
+        each(layer_c, **front)
+        layer_b(3)
+        layer_c(2)
+        each(to_partner, **front)
+        layer_c(3)
+        each(to_partner, **rear)
+        each(from_partner, last=3)
+        each(back_f, after=(p(from_partner, 3), None, p(back_g, 0), p(back_g, 1)))
+        ffn_piece(2)
+        dw_start(IN_R, 0)
+        ffn_piece(3)
+        dw_start(OUT_R, 0)
+        back_g(2)
+        ffn_piece(0)
+        dw_start(IN_W, 0)
+        dw_turn(IN_R, 0)
+        ffn_piece(1)
+        dw_start(OUT_W, 0)
+        dw_turn(OUT_R, 0)
+        back_g(3)
         each(
             back_h,
             after=(
-                then(p(dw_turn, IN_W, 0), p(dw_turn, OUT_W, 0)), None, p(dw_turn, IN_R, 1),
-                p(dw_turn, OUT_R, 1),
+                then(p(dw_turn, IN_W, 0), p(dw_turn, OUT_W, 0)), small_norms, None, then(p(dw_turn, IN_R, 1), p(dw_turn, OUT_R, 1)),
             ),
         )
-        small_biases()
         attn_piece(2)
         attn_piece(3)
         dw_start(ATTN_R, 0)
-        small_y()
+        small_biases()
         attn_piece(0)
         attn_piece(1)
         dw_start(ATTN_W, 0)
+        small_y()
         dw_turn(ATTN_R, 0)
-        dw_turn(IN_W, 1)
         dw_turn(ATTN_W, 0)
         dw_turn(OUT_W, 1)
+        small_z()
+        dw_turn(IN_W, 1)
         each(last)
-        small_z()
 
     @pl.when(cross)
     def _():
@@ -981,30 +996,40 @@
         gather_wait("x", WQKV, WO)
         gather_start("y", WQKV)
         gather_start("z", WO)
-        gather_wait("x", W2, W1)
+        gather_wait("x", W1)
         gather_start("y", W1)
         gather_wait("y", WQKV)
         gather_start("z", WQKV)
         gather_wait("z", CWQKV, CWO)
         gather_start("core", CWQKV, CWO)
-        gather_start("z", W2)
         gather_wait("z", WO)
         gather_start("y", WO)
         gather_wait("y", W1)
         gather_start("z", W1)
+        gather_wait("x", W2)
+        gather_start("y", W2)
         for copy in bias_copies():
             copy.wait()
         gather_wait("core", CWQKV, CWO)
-        gather_wait("y", WO)
-        gather_wait("z", WQKV)
-        gather_start("core", WQKV, WO)
         wait_weights(0, 1, 2, 3, 4, 5)
         pl.loop(0, 3)(mid_relay)
-        pl.when(set_of == 1)(lambda: mid_relay(3))
+
+        @pl.when(set_of == 1)
+        def _():
+            gather_wait("y", WO)
+            gather_wait("z", WQKV)
+            gather_start("core", WQKV, WO)
+            mid_relay(3)
+
         cross_forward(0)
-        pl.when(set_of == 0)(lambda: mid_relay(3))
-        gather_wait("z", W2)
-        gather_start("y", W2)
+
+        @pl.when(set_of == 0)
+        def _():
+            gather_wait("y", WO)
+            gather_wait("z", WQKV)
+            gather_start("core", WQKV, WO)
+            mid_relay(3)
+
         cross_forward(1)
         gather_wait("core", WQKV, WO)
         attn_forward(0)
@@ -1018,30 +1043,32 @@
         pair(attn_backward)
         pair(cross_backward)
         pair(to_section_0)
-        mate_wait(XLOW, ALOW, ACT, DYF, DUP)
-        mate_start_all(DYC, CDQKV, CMIXED)
-        pass_start(XLOW)
+        mate_wait(CMIXED, XLOW, MIXED, ALOW, ACT, DYF, DUP)
+        pass_start(DYF)
+        mate_start_all(DYC, CDQKV)
         ffn_piece(2)
         dw_start(IN_R, 0)
-        ffn_piece(3)
-        dw_start(OUT_R, 0)
         ffn_piece(0)
         dw_start(IN_W, 0)
         dw_turn(IN_R, 0)
+        dw_turn(IN_W, 0)
+        pass_wait(DYF)
+        pass_start(XLOW)
+        ffn_piece(3)
+        dw_start(OUT_R, 0)
         ffn_piece(1)
         dw_start(OUT_W, 0)
         dw_turn(OUT_R, 0)
         small_norms_all()
         for mod, (lo, hi) in enumerate(SPANS):
             bsum[mod] = column_sums(dup, lo, hi)
-        dw_turn(IN_W, 0)
         dw_turn(OUT_W, 0)
         mate_wait(DYC)
         pass_start(DYC)
-        mate_start_all(DYA, DQKV, MIXED)
+        mate_start_all(DYA, DQKV)
         for k in range(2):
             ag_finish(midf, 2 * (1 - set_of) + k)
-        mate_wait(CDQKV, CMIXED)
+        mate_wait(CDQKV)
         pass_wait(DYC)
         cross_outer()
         dw_start(CROSS, 0)
@@ -1053,7 +1080,8 @@
         dw_turn(OUT_R, 1)
         dw_turn(IN_W, 1)
         dw_turn(OUT_W, 1)
-        mate_wait(DQKV, MIXED)
+        dw_turn(CROSS, 1)
+        mate_wait(DQKV)
         mate_start_all(YBUF)
         pass_wait(XLOW)
         pass_wait(DYA)
@@ -1067,7 +1095,6 @@
         attn_piece(0)
         attn_piece(1)
         dw_start(ATTN_W, 0)
-        dw_turn(CROSS, 1)
         dw_turn(ATTN_R, 0)
         small_z()
         dw_turn(ATTN_W, 0)
@@ -1075,7 +1102,9 @@
         pass_start(YBUF)
         dw_finish(CROSS, 2)
         pass_wait(YBUF)
-        pair(lambda j: [copy.wait_send() for copy in back_copies(j)] and None)
+        for j in range(2):
+            rows = back.at[block_of(j), pl.ds(0, 2 * C)]
+            moved(rows, rows, back_send.at[j], back_recv.at[0], partner).wait_send()
 
     def write(m):
         @pl.when(head)
@@ -1087,9 +1116,9 @@
     dw_finish(IN_R, 2)
     dw_finish(OUT_R, 2)
     dw_turn(ATTN_R, 1)
+    dw_turn(ATTN_W, 1)
     dw_finish(IN_W, 2)
     dw_finish(OUT_W, 2)
-    dw_turn(ATTN_W, 1)
     small_last()
     each(write)
 
@@ -1259,21 +1288,21 @@
             pltpu.VMEM((24, D), F32),
             pltpu.VMEM((3, 24, D), F32),
             pltpu.VMEM((2, 48, D), F32),
-            *[pltpu.SemaphoreType.DMA((MB, TENSOR - 1)) for _ in range(6)],
+            *[pltpu.SemaphoreType.DMA((MB,)) for _ in range(6)],
             pltpu.SemaphoreType.DMA((MB,)),
             pltpu.SemaphoreType.DMA((MB,)),
-            pltpu.SemaphoreType.DMA((7, 5)),
-            pltpu.SemaphoreType.DMA((7, 5)),
-            pltpu.SemaphoreType.DMA((8,)),
-            pltpu.SemaphoreType.DMA((8,)),
+            pltpu.SemaphoreType.DMA((7, 3)),
+            pltpu.SemaphoreType.DMA((7, 3)),
+            pltpu.SemaphoreType.DMA((4,)),
+            pltpu.SemaphoreType.DMA((4,)),
             pltpu.SemaphoreType.DMA,
             pltpu.SemaphoreType.DMA,
-            pltpu.SemaphoreType.DMA((2, 2)),
+            pltpu.SemaphoreType.DMA((2,)),
             pltpu.SemaphoreType.DMA((MB,)),
             *[pltpu.SemaphoreType.DMA((2, 2, 2)) for _ in range(2)],
-            *[pltpu.SemaphoreType.DMA((12, 2)) for _ in range(2)],
-            *[pltpu.SemaphoreType.DMA((8, 6)) for _ in range(2)],
-            *[pltpu.SemaphoreType.DMA((6, 2)) for _ in range(2)],
+            *[pltpu.SemaphoreType.DMA((12,)) for _ in range(2)],
+            *[pltpu.SemaphoreType.DMA((7, 4)) for _ in range(2)],
+            *[pltpu.SemaphoreType.DMA((6,)) for _ in range(2)],
             pltpu.SemaphoreType.DMA((6,)),
         ],
         compiler_params=pltpu.CompilerParams(

time: 166 us -> 162 us (0.976)
  Pallas kernels: 165 us -> 161 us
    pallas_call x1, Pallas kernels: 161 us -> 158 us  [local(): pl.pallas_call(kernel, out_shape=(jax.ShapeDtypeStruct((MB, R, D), BF), j...]
where the time goes in v5:
time: 162 us
  Pallas kernels  161 us (99%)
    pallas_call x1, Pallas kernels, local(): pl.pallas_call(kernel, out_shape=(jax.ShapeDtypeStruct((MB, R, D), BF), j...  158 us
    pallas_call x1, Pallas kernels, local(): pl.pallas_call(arrange, out_shape=tuple((jax.ShapeDtypeStruct(shape, F32)...  3.27 us

profile of v5, /device:TPU:0, one launch (start us, length us, event | category | flops | bytes accessed | tf_op | source)
XLA Modules:
  0.0 161.8 jit_solution(1974434700531086461)
XLA Ops:
  0.7 157.7 %shard_map.314 = (bf16[4,128,768]{2,1,0:T(8,128)(2,1)}, f32[7,48,768]{2,1,0:T(8,128)}, f32[24,768]{1,0:T(8,128)}, f32[24,768]{1,0:T(8,128)}, f32[24,768]{1,0:T(8,128)}) custom-call(bf16[1,20,8,768]{3,2,1,0:T(8,128)(2,1)} %bitcast.30, bf16[1,36,8,768]{3,2,1,0:T(8,128)(2,1)} %bitcast.29, s32[8]{0:T(128)} %lengths_ref.1, s32[8]{0:T(128)} %flags_ref.1, ...), custom_call_target="tpu_custom_call" | custom-call | tf_op jit(solution)/shard_map/pallas_call | solution.py:1218
  158.4 3.3 %shard_map.315 = (f32[1,20,8,768]{3,2,1,0:T(8,128)}, f32[1,36,8,768]{3,2,1,0:T(8,128)}, f32[1,2,3,48,192]{4,3,2,1,0:T(8,128)}, f32[1,2,3,2,4]{4,3,2,1,0:T(2,128)...) custom-call(bf16[4,128,768]{2,1,0:T(8,128)(2,1)} %get-tuple-element., ...), custom_call_target="tpu_custom_call" | custom-call | tf_op jit(solution)/shard_map/pallas_call | solution.py:1323

commit v6 on v5

--- a/solution.py
+++ b/solution.py
@@ -95,24 +95,39 @@
     return mask
 
 
-def attend(q, k, v, mask):
-    scores = dot_nt(by_head(q), k) * SCALING
-    mask = jnp.concatenate([mask] * LOCAL_HEADS, axis=0)
-    scores = jnp.where(mask, scores, MASKED)
-    e = jnp.exp(scores - jnp.max(scores, axis=-1, keepdims=True))
-    probs = e / jnp.sum(e, axis=-1, keepdims=True)
-    mixed = join_heads(dot(probs.astype(BF), v)).astype(BF)
-    return probs, mixed
-
-
-def attend_back(dmix, probs, q, k, v):
-    d3 = by_head(dmix)
-    dp = dot_nt(d3, v)
-    ds = (probs * (dp - jnp.sum(probs * dp, axis=-1, keepdims=True))).astype(BF)
-    dv = dot_tn(probs.astype(BF), d3).astype(BF)
-    dq = (join_heads(dot(ds, k)) * SCALING).astype(BF)
-    dk = (dot_tn(ds, by_head(q)) * SCALING).astype(BF)
-    return dq, dk, dv
+def attend(cases):
+    masks = [jnp.concatenate([mask] * LOCAL_HEADS, axis=0) for _, _, _, mask in cases]
+    scores = [dot_nt(by_head(q), k) * SCALING for q, k, _, _ in cases]
+    scores = [jnp.where(mask, score, MASKED) for mask, score in zip(masks, scores)]
+    es = [jnp.exp(score - jnp.max(score, axis=-1, keepdims=True)) for score in scores]
+    probs = [e / jnp.sum(e, axis=-1, keepdims=True) for e in es]
+    mixed = [dot(p.astype(BF), v) for p, (_, _, v, _) in zip(probs, cases)]
+    return [(p, join_heads(mix).astype(BF)) for p, mix in zip(probs, mixed)]
+
+
+def attend_back(cases):
+    d3s = [by_head(dmix) for dmix, _, _, _, _ in cases]
+    dps = [dot_nt(d3, v) for d3, (_, _, _, _, v) in zip(d3s, cases)]
+    dss = [
+        (probs * (dp - jnp.sum(probs * dp, axis=-1, keepdims=True))).astype(BF)
+        for dp, (_, probs, _, _, _) in zip(dps, cases)
+    ]
+    dqs = [dot(ds, k) for ds, (_, _, _, k, _) in zip(dss, cases)]
+    dks = [dot_tn(ds, by_head(q)) for ds, (_, _, q, _, _) in zip(dss, cases)]
+    dvs = [dot_tn(probs.astype(BF), d3) for d3, (_, probs, _, _, _) in zip(d3s, cases)]
+    return [
+        ((join_heads(dq) * SCALING).astype(BF), (dk * SCALING).astype(BF), dv.astype(BF))
+        for dq, dk, dv in zip(dqs, dks, dvs)
+    ]
+
+
+def split_qkv(out):
+    return out[:, :HW], out[:, HW : 2 * HW], out[:, 2 * HW :]
+
+
+def gelu(up):
+    cdf = 0.5 * (1.0 + lax.erf(up * (0.5**0.5)))
+    return (up * cdf).astype(BF), cdf + up * jnp.exp(-0.5 * up * up) * 0.3989422804014327
 
 
 def norm_forward(r, gain, shift):
@@ -137,10 +152,10 @@
     y_ref, dw_ref, s_ref, dc_ref, sc_ref,
     x_ref, bqkv_ref, b1_ref, cvec_ref, send, recv, xlow, midf, alow, dyf, dya, dyc, ybuf, back,
     qkv, mixed, dqkv, cqkv, cmixed, cdqkv, act, dup, dgelu,
-    p_w, p_r, cp_w, cp_r, cur, res, nrm, rstd, acc, rowp, bsum, bqsum,
+    p_w, p_r, cp_w, cp_r, cur, res, nrm, rstd, packed, gathered_end, total_ref, low_ref, bsum, bqsum,
     wqkv_ref, wo_ref, w1_ref, w2_ref, cwqkv_ref, cwo_ref, wqkv_m, wo_m, w1_m, w2_m, cwqkv_m, cwo_m, bqkv_m, b1_m,
-    got, act_m, dup_m, mixed_m, dqkv_m, cmixed_m, cdqkv_m, cur_f, res_f, nrm_f, rstd_f, row_sums,
-    g_ref, from_core, from_y, from_zs, from_z, from_ys, sums, sums_t, sums_c, sums_y, sums_z, pack,
+    got, tails, got_tails, act_m, dup_m, mixed_m, dqkv_m, cmixed_m, cdqkv_m, cur_f, res_f, nrm_f, rstd_f, row_sums,
+    g_ref, from_core, from_y, from_zs, from_h, from_z, from_ys, sums, total, sums_t, sums_c, sums_y, sums_z, pack,
     rs_send, rs_recv, ag_send, ag_recv, y_send, y_recv, sec_send, sec_recv,
     dw_send, dw_recv, sm_send, sm_recv, pk_send, pk_recv,
     back_send, back_recv, ar_send, ar_recv, mt_send, mt_recv, ga_send, ga_recv, ps_send, ps_recv, loads,
@@ -150,13 +165,9 @@
     me = lax.axis_index("tensor")
     head = sec == 0
     cross = sec == 1
-    own = pl.ds(pl.multiple_of(me * C, C), C)
 
     def peer(o):
         return {"tensor": lax.rem(me + o, TENSOR)}
-
-    def rows_of(t):
-        return pl.ds(pl.multiple_of(t * C, C), C)
 
     partner = {"section": 1 - sec}
     place = lax.axis_index("dp")
@@ -263,12 +274,6 @@
         pl.semaphore_wait(barrier, 12)
         gather_start("x", CWQKV, CWO, WQKV, WO, W1, W2)
 
-    row = lax.broadcasted_iota(jnp.int32, (C, 1), 0) + me * C
-    is_word = row < RW
-    for k, ref in enumerate((out_bias_ref, gain_ref, shift_ref)):
-        for l in range(2):
-            rowp[2 * k + l] = jnp.where(is_word, ref[0, 0, l : l + 1, :], ref[0, 1, l : l + 1, :])
-
     def side_by_side(rows):
         return jnp.concatenate(rows, axis=1)
 
@@ -286,91 +291,186 @@
         given = ref[0].astype(F32).reshape(ITEMS_LOCAL * length, D).astype(BF)
         placed = dot(spread(hi - lo, length), given).astype(BF)
         x_ref[:, lo:hi, :] = placed.reshape(MB, hi - lo, D)
-    acc[...] = jnp.zeros_like(acc)
     bsum[...] = jnp.zeros_like(bsum)
     bqsum[...] = jnp.zeros_like(bqsum)
     row_sums[...] = jnp.zeros_like(row_sums)
 
 
-    def rs_copies(m):
-        return [
-            pltpu.make_async_remote_copy(
-                src_ref=send.at[m, rows_of(lax.rem(me + o, TENSOR))],
-                dst_ref=recv.at[m, o - 1],
-                send_sem=rs_send.at[m],
-                recv_sem=rs_recv.at[m],
-                device_id=peer(o),
-                device_id_type=MESH,
-            )
-            for o in range(1, TENSOR)
-        ]
+    def place_of(t, m):
+        return lax.rem(t + m, TENSOR)
+
+    def rows_at(at):
+        return pl.ds(pl.multiple_of(48 * at - 16 * (at // 2), 16), C)
+
+    def by_place(at, heavy, light):
+        pl.when(at != 3)(heavy)
+        pl.when(at == 3)(light)
+
+    WORD_END, REGION_END = pl.ds(32, 16), pl.ds(112, 16)
+    no_rows = jnp.zeros((8, D), F32)
+
+    def pack_rows(words_end, regions_end):
+        return jnp.concatenate([words_end, regions_end], axis=0).astype(BF)
+
+    def wait_rows(m, ss, rs, sent, received):
+        out, come = send.at[m, pl.ds(0, sent)], send.at[m, pl.ds(0, received)]
+        moved(out, out, ss.at[m], rs.at[m], peer(1)).wait_send()
+        moved(come, come, ss.at[m], rs.at[m], peer(1)).wait_recv()
+
+    def own_rows_of(ref, m):
+        at = place_of(me, m)
+
+        def heavy():
+            low_ref[...] = ref[m, rows_at(at)]
+
+        def light():
+            low_ref[0:16] = ref[m, WORD_END]
+            low_ref[16:32] = ref[m, REGION_END]
+
+        by_place(at, heavy, light)
+        return low_ref[...]
+
+    def put_own_rows(ref, m, low):
+        at = place_of(me, m)
+
+        def heavy():
+            ref[m, rows_at(at)] = low
+
+        def light():
+            ref[m, WORD_END] = low[:16]
+            ref[m, REGION_END] = low[16:]
+
+        by_place(at, heavy, light)
+
+    def put_parts(m, parts):
+        for (lo, hi), part in zip(SPANS, parts):
+            send[m, lo:hi] = part.astype(BF)
+        packed[m] = pack_rows(parts[0][32:40], parts[1][64:72])
 
     def rs_start(m):
-        for copy in rs_copies(m):
-            copy.start()
+        for o in range(1, TENSOR):
+            at = place_of(me + o, m)
+
+            def heavy(o=o, at=at):
+                src, dst = send.at[m, rows_at(at)], recv.at[m, o - 1]
+                moved(src, dst, rs_send.at[m], rs_recv.at[m], peer(o)).start()
+
+            def light(o=o):
+                src, dst = packed.at[m], recv.at[m, o - 1, pl.ds(0, 16)]
+                moved(src, dst, rs_send.at[m], rs_recv.at[m], peer(o)).start()
+
+            by_place(at, heavy, light)
 
     def rs_finish(m):
-        moved(recv.at[m], recv.at[m], rs_send.at[m], rs_recv.at[m], peer(1)).wait()
-        total = send[m, own].astype(F32)
-        for o in range(TENSOR - 1):
-            total = total + recv[m, o].astype(F32)
-        return total
-
-    def ag_copies(buf, m, ss, rs):
-        return [
-            pltpu.make_async_remote_copy(
-                src_ref=buf.at[m, own],
-                dst_ref=buf.at[m, own],
-                send_sem=ss.at[m],
-                recv_sem=rs.at[m],
-                device_id=peer(o),
-                device_id_type=MESH,
-            )
-            for o in range(1, TENSOR)
-        ]
-
-    def ag_start(buf, m, ss=ag_send, rs=ag_recv):
-        for copy in ag_copies(buf, m, ss, rs):
-            copy.start()
+        at = place_of(me, m)
+
+        def heavy():
+            wait_rows(m, rs_send, rs_recv, 80, 96)
+            total = send[m, rows_at(at)].astype(F32)
+            for o in range(TENSOR - 1):
+                total = total + recv[m, o].astype(F32)
+            total_ref[...] = total
+
+        def light():
+            wait_rows(m, rs_send, rs_recv, 96, 48)
+            total = packed[m].astype(F32)
+            for o in range(TENSOR - 1):
+                total = total + recv[m, o, 0:16].astype(F32)
+            total_ref[...] = jnp.concatenate([total[:8], no_rows, total[8:], no_rows], axis=0)
+
+        by_place(at, heavy, light)
+        return total_ref[...]
+
+    def ag_start(buf, m, low, ss=ag_send, rs=ag_recv):
+        put_own_rows(buf, m, low)
+        at = place_of(me, m)
+
+        def heavy():
+            rows = buf.at[m, rows_at(at)]
+            for o in range(1, TENSOR):
+                moved(rows, rows, ss.at[m], rs.at[m], peer(o)).start()
+
+        def light():
+            wide = low.astype(F32)
+            gathered_end[m] = pack_rows(wide[:8], wide[16:24])
+            for o in range(1, TENSOR):
+                end = gathered_end.at[m]
+                moved(end, end, ss.at[m], rs.at[m], peer(o)).start()
+
+        by_place(at, heavy, light)
 
     def ag_finish(buf, m, ss=ag_send, rs=ag_recv):
-        three = buf.at[m, pl.ds(0, (TENSOR - 1) * C)]
-        moved(three, three, ss.at[m], rs.at[m], peer(1)).wait()
-
-    def mid_copy(m):
-        rows = midf.at[m, own]
-        return moved(rows, rows, sec_send.at[m], sec_recv.at[m], partner)
+        def heavy():
+            wait_rows(m, ss, rs, 96, 80)
+            end = gathered_end[m].astype(F32)
+            buf[m, WORD_END] = pack_rows(end[:8], no_rows)
+            buf[m, REGION_END] = pack_rows(end[8:], no_rows)
+
+        def light():
+            wait_rows(m, ss, rs, 48, 96)
+
+        by_place(place_of(me, m), heavy, light)
+
+    def start_rows(ref, m, at, ss, rs, *devices):
+        def heavy():
+            rows = ref.at[m, rows_at(at)]
+            for device in devices:
+                moved(rows, rows, ss, rs, device).start()
+
+        def light():
+            for end in (WORD_END, REGION_END):
+                rows = ref.at[m, end]
+                for device in devices:
+                    moved(rows, rows, ss, rs, device).start()
+
+        by_place(at, heavy, light)
+
+    def some_rows(ref, m, count, ss, rs):
+        rows = ref.at[m, pl.ds(0, count)]
+        return moved(rows, rows, ss, rs, partner)
+
+    def mid_start(m):
+        start_rows(midf, m, place_of(me, m), sec_send.at[m], sec_recv.at[m], partner)
 
     def mid_relay(m):
-        mid_copy(m).wait_recv()
-        ag_start(midf, m)
-
-    def back_copies(j):
+        some_rows(midf, m, C, sec_send.at[m], sec_recv.at[m]).wait_recv()
+        start_rows(midf, m, place_of(me, m), ag_send.at[m], ag_recv.at[m], peer(1), peer(2), peer(3))
+
+    def mid_finish(m):
+        some_rows(midf, m, 3 * C, ag_send.at[m], ag_recv.at[m]).wait()
+
+    def back_start(j):
         m = 2 * set_of + j
-        first = 2 * (me // 2)
-        return [
-            moved(
-                back.at[m, rows_of(first + k)], back.at[m, rows_of(first + k)],
-                back_send.at[j], back_recv.at[m], {"section": 1 - sec, "tensor": first + k},
-            )
-            for k in range(2)
-        ]
+        for k in range(2):
+            t = 2 * (me // 2) + k
+            device = {"section": 1 - sec, "tensor": t}
+            start_rows(back, m, place_of(t, m), back_send.at[j], back_recv.at[m], device)
 
     def back_arrive(m):
-        rows = back.at[m, own]
-        moved(rows, rows, back_send.at[0], back_recv.at[m], partner).wait_recv()
+        some_rows(back, m, C, back_send.at[0], back_recv.at[m]).wait_recv()
 
     def save_norm(l, m, n, r):
         nrm[l, m] = n
         rstd[l, m] = jnp.broadcast_to(r, (C, 128))
 
-    def norm_step_back(l, m, dh, gain):
+    def own_words(m):
+        at = place_of(me, m)
+        count = jnp.where(at == 0, C, jnp.where(at == 3, C // 2, 0))
+        return lax.broadcasted_iota(jnp.int32, (C, 1), 0) < count
+
+    def own_param(ref, l, m):
+        return jnp.where(own_words(m), ref[0, 0, l : l + 1, :], ref[0, 1, l : l + 1, :])
+
+    def norm_step_back(l, m, dh):
         n = nrm[l, m]
-        dr = norm_back(dh, n, rstd[l, m][:, :1], gain)
+        dr = norm_back(dh, n, rstd[l, m][:, :1], own_param(gain_ref, l, m))
         low = dr.astype(BF)
-        acc[3 * l] += dh * n
-        acc[3 * l + 1] += dh
-        acc[3 * l + 2] += low.astype(F32)
+        words_only = own_words(m)
+        for k, value in enumerate((dh * n, dh, low.astype(F32))):
+            part = jnp.where(words_only, value, 0.0)
+            at = 2 * (3 * l + k)
+            row_sums[at] += jnp.sum(part, axis=0, keepdims=True)
+            row_sums[at + 1] += jnp.sum(value - part, axis=0, keepdims=True)
         res[m] = dr
         return low
 
@@ -384,98 +484,105 @@
 
     def layer_a(m):
         xlow[m] = x_ref[m]
-        cur[m] = x_ref[m, own].astype(F32)
-        for mod, (lo, hi) in enumerate(SPANS):
-            out = (dot_nt(xlow[m, lo:hi], wqkv_ref[mod]) + bqkv_ref[mod]).astype(BF)
-            q, k, v = out[:, :HW], out[:, HW : 2 * HW], out[:, 2 * HW :]
-            qkv[0, m, lo:hi], qkv[1, m, lo:hi], qkv[2, m, lo:hi] = q, k, v
-            if mod == 0:
-                probs, mix = attend(q, k, v, word_keys(m, RW, WORDS))
-                p_w[m] = probs
-            else:
-                probs, mix = attend(q, k, v, region_keys(RR, REGIONS))
-                p_r[m] = probs
+        cur[m] = own_rows_of(x_ref, m).astype(F32)
+        outs = [
+            (dot_nt(xlow[m, lo:hi], wqkv_ref[mod]) + bqkv_ref[mod]).astype(BF)
+            for mod, (lo, hi) in enumerate(SPANS)
+        ]
+        for (lo, hi), out in zip(SPANS, outs):
+            for k, part in enumerate(split_qkv(out)):
+                qkv[k, m, lo:hi] = part
+        masks = (word_keys(m, RW, WORDS), region_keys(RR, REGIONS))
+        done = attend([(*split_qkv(out), mask) for out, mask in zip(outs, masks)])
+        for (lo, hi), keep, (probs, mix) in zip(SPANS, (p_w, p_r), done):
+            keep[m] = probs
             mixed[m, lo:hi] = mix
-            send[m, lo:hi] = dot(mix, wo_ref[mod]).astype(BF)
+        put_parts(m, [dot(mix, wo_ref[mod]) for mod, (_, mix) in enumerate(done)])
 
     def layer_b(m):
-        r = cur[m] + rs_finish(m) + rowp[0]
-        n, rs, h = norm_forward(r, rowp[2], rowp[4])
+        r = cur[m] + rs_finish(m) + own_param(out_bias_ref, 0, m)
+        n, rs, h = norm_forward(r, own_param(gain_ref, 0, m), own_param(shift_ref, 0, m))
         save_norm(0, m, n, rs)
         cur[m] = h
-        alow[m, own] = h.astype(BF)
-        ag_start(alow, m)
+        ag_start(alow, m, h.astype(BF))
 
     def layer_c(m):
         ag_finish(alow, m)
-        for mod, (lo, hi) in enumerate(SPANS):
-            up = dot(alow[m, lo:hi], w1_ref[mod]) + b1_ref[mod]
-            cdf = 0.5 * (1.0 + lax.erf(up * (0.5**0.5)))
-            dgelu[m, lo:hi] = cdf + up * jnp.exp(-0.5 * up * up) * 0.3989422804014327
-            active = (up * cdf).astype(BF)
+        ups = [dot(alow[m, lo:hi], w1_ref[mod]) + b1_ref[mod] for mod, (lo, hi) in enumerate(SPANS)]
+        pairs = [gelu(up) for up in ups]
+        put_parts(m, [dot(active, w2_ref[mod]) for mod, (active, _) in enumerate(pairs)])
+        rs_start(m)
+        for (lo, hi), (active, slope) in zip(SPANS, pairs):
             act[m, lo:hi] = active
-            send[m, lo:hi] = dot(active, w2_ref[mod]).astype(BF)
-        rs_start(m)
+            dgelu[m, lo:hi] = slope
 
     def layer_d(m):
-        r = cur[m] + rs_finish(m) + rowp[1]
-        n, rs, h = norm_forward(r, rowp[3], rowp[5])
+        r = cur[m] + rs_finish(m) + own_param(out_bias_ref, 1, m)
+        n, rs, h = norm_forward(r, own_param(gain_ref, 1, m), own_param(shift_ref, 1, m))
         save_norm(1, m, n, rs)
         return h
 
     def back_e(m, dh):
-        low = norm_step_back(1, m, dh, rowp[3])
-        dyf[m, own] = low
-        ag_start(dyf, m)
+        ag_start(dyf, m, norm_step_back(1, m, dh))
 
     def back_f(m):
         ag_finish(dyf, m)
+        dacts = [dot_nt(dyf[m, lo:hi], w2_ref[mod]) for mod, (lo, hi) in enumerate(SPANS)]
+        ds = [(dact * dgelu[m, lo:hi]).astype(BF) for dact, (lo, hi) in zip(dacts, SPANS)]
+        put_parts(m, [dot_nt(d, w1_ref[mod]) for mod, d in enumerate(ds)])
+        rs_start(m)
         for mod, (lo, hi) in enumerate(SPANS):
-            d = (dot_nt(dyf[m, lo:hi], w2_ref[mod]) * dgelu[m, lo:hi]).astype(BF)
-            dup[m, lo:hi] = d
-            bsum[mod] += jnp.sum(d.astype(F32), axis=0, keepdims=True)
-            send[m, lo:hi] = dot_nt(d, w1_ref[mod]).astype(BF)
-        rs_start(m)
+            dup[m, lo:hi] = ds[mod]
+            bsum[mod] += jnp.sum(ds[mod].astype(F32), axis=0, keepdims=True)
 
     def back_g(m):
         dh = res[m] + rs_finish(m)
-        low = norm_step_back(0, m, dh, rowp[2])
-        dya[m, own] = low
-        ag_start(dya, m)
+        ag_start(dya, m, norm_step_back(0, m, dh))
 
     def back_h(m):
         ag_finish(dya, m)
+        dmixs = [
+            dot_nt(dya[m, lo:hi], wo_ref[mod]).astype(BF) for mod, (lo, hi) in enumerate(SPANS)
+        ]
+        grads = attend_back([
+            (dmix, keep[m], *(qkv[k, m, lo:hi] for k in range(3)))
+            for dmix, keep, (lo, hi) in zip(dmixs, (p_w, p_r), SPANS)
+        ])
+        ds = [jnp.concatenate(grad, axis=1) for grad in grads]
+        put_parts(m, [dot(d, wqkv_ref[mod]) for mod, d in enumerate(ds)])
+        rs_start(m)
         for mod, (lo, hi) in enumerate(SPANS):
-            dmix = dot_nt(dya[m, lo:hi], wo_ref[mod]).astype(BF)
-            probs = p_w[m] if mod == 0 else p_r[m]
-            parts = attend_back(
-                dmix, probs, qkv[0, m, lo:hi], qkv[1, m, lo:hi], qkv[2, m, lo:hi]
-            )
-            d = jnp.concatenate(parts, axis=1)
-            dqkv[m, lo:hi] = d
-            bqsum[mod] += jnp.sum(d.astype(F32), axis=0, keepdims=True)
-            send[m, lo:hi] = dot(d, wqkv_ref[mod]).astype(BF)
-        rs_start(m)
+            dqkv[m, lo:hi] = ds[mod]
+            bqsum[mod] += jnp.sum(ds[mod].astype(F32), axis=0, keepdims=True)
 
     def block_of(j):
         return 2 * set_of + j
 
-    def ar_copy(j, mod, turn):
+    def ar_copies(j, mod, turn):
         lo, hi = SPANS[mod]
-        return moved(
-            send.at[j, lo:hi], got.at[turn, j, lo:hi], ar_send.at[turn, j, mod], ar_recv.at[turn, j, mod],
-            halver,
-        )
+        rows = slice(lo, hi - 16)
+        sems = lambda k: (ar_send.at[turn, j, 2 * mod + k], ar_recv.at[turn, j, 2 * mod + k])
+        return [
+            moved(send.at[j, rows], got.at[turn, j, rows], *sems(0), halver),
+            moved(tails.at[j, mod], got_tails.at[turn, j, mod], *sems(1), halver),
+        ]
 
     def ar_start(j, mod, turn, part):
         lo, hi = SPANS[mod]
-        send[j, lo:hi] = part.astype(BF)
-        ar_copy(j, mod, turn).start()
+        full = hi - lo - 16
+        send[j, lo : hi - 16] = part[:full].astype(BF)
+        tail = part[full : full + 8]
+        tails[j, mod] = jnp.concatenate([tail[:, : D // 2], tail[:, D // 2 :]], axis=0).astype(BF)
+        for copy in ar_copies(j, mod, turn):
+            copy.start()
 
     def ar_finish(j, mod, turn):
         lo, hi = SPANS[mod]
-        ar_copy(j, mod, turn).wait()
-        return send[j, lo:hi].astype(F32) + got[turn, j, lo:hi].astype(F32)
+        for copy in ar_copies(j, mod, turn):
+            copy.wait()
+        rows = send[j, lo : hi - 16].astype(F32) + got[turn, j, lo : hi - 16].astype(F32)
+        tail = tails[j, mod].astype(F32) + got_tails[turn, j, mod].astype(F32)
+        return jnp.concatenate([rows, jnp.concatenate([tail[:8], tail[8:]], axis=1), no_rows], axis=0)
 
     shared = (xlow, alow, dyf, dya, dyc, ybuf)
     for_mate = ((act_m, act), (dup_m, dup), (mixed_m, mixed), (dqkv_m, dqkv), (cmixed_m, cmixed), (cdqkv_m, cdqkv))
@@ -541,22 +648,22 @@
 
     def cross_forward(j):
         m = block_of(j)
-        ag_finish(midf, m)
+        mid_finish(m)
         mid = midf[m]
         shards = ((cwqkv_ref, bqkv_ref, cwo_ref, cmixed, m), (cwqkv_m, bqkv_m, cwo_m, cmixed_m, j))
         qkvs = []
         for sh, (w, bias, w_out, keep, at) in enumerate(shards):
             out = (dot_nt(mid, w[...]) + bias[2]).astype(BF)
-            q, k, v = out[:, :HW], out[:, HW : 2 * HW], out[:, 2 * HW :]
+            q, k, v = split_qkv(out)
             cqkv[0, 2 * sh + j], cqkv[1, 2 * sh + j], cqkv[2, 2 * sh + j] = q, k, v
             qkvs.append((q, k, v))
         for mod, (lo, hi) in enumerate(SPANS):
             others = slice(*SPANS[1 - mod])
+            mask = region_keys(RW, WORDS) if mod == 0 else word_keys(m, RR, REGIONS)
+            done = attend([(q[lo:hi], k[others], v[others], mask) for q, k, v in qkvs])
             part = None
             for sh, (w, bias, w_out, keep, at) in enumerate(shards):
-                q, k, v = qkvs[sh]
-                mask = region_keys(RW, WORDS) if mod == 0 else word_keys(m, RR, REGIONS)
-                probs, mix = attend(q[lo:hi], k[others], v[others], mask)
+                probs, mix = done[sh]
                 (cp_w, cp_r)[mod][2 * sh + j] = probs
                 keep[at, lo:hi] = mix
                 one = dot(mix, w_out[...])
@@ -576,18 +683,16 @@
             cur_f[j, lo:hi] = h
             low = h.astype(BF)
             xlow[m, lo:hi] = low
+            outs = [(dot_nt(low, w[mod]) + bias[mod]).astype(BF) for w, bias, _, _, _ in shards]
+            for sh, out in enumerate(outs):
+                for k, part in enumerate(split_qkv(out)):
+                    qkv[k, 2 * sh + j, lo:hi] = part
+            mask = word_keys(m, RW, WORDS) if mod == 0 else region_keys(RR, REGIONS)
+            done = attend([(*split_qkv(out), mask) for out in outs])
             part = None
             for sh, (w, bias, w_out, keep, at) in enumerate(shards):
-                slot = 2 * sh + j
-                out = (dot_nt(low, w[mod]) + bias[mod]).astype(BF)
-                q, k, v = out[:, :HW], out[:, HW : 2 * HW], out[:, 2 * HW :]
-                qkv[0, slot, lo:hi], qkv[1, slot, lo:hi], qkv[2, slot, lo:hi] = q, k, v
-                if mod == 0:
-                    probs, mix = attend(q, k, v, word_keys(m, RW, WORDS))
-                    p_w[slot] = probs
-                else:
-                    probs, mix = attend(q, k, v, region_keys(RR, REGIONS))
-                    p_r[slot] = probs
+                probs, mix = done[sh]
+                (p_w, p_r)[mod][2 * sh + j] = probs
                 keep[at, lo:hi] = mix
                 one = dot(mix, w_out[mod])
                 part = one if part is None else part + one
@@ -604,19 +709,16 @@
             cur_f[j, lo:hi] = h
             low = h.astype(BF)
             alow[m, lo:hi] = low
-            part = None
-            for sh, (w, bias, w_out, keep, at) in enumerate(shards):
-                if mod == 0 and sh == 1:
-                    pl.when(j == 0)(lambda: gather_wait("core", W1))
-                up = dot(low, w[mod]) + bias[mod]
-                cdf = 0.5 * (1.0 + lax.erf(up * (0.5**0.5)))
-                dgelu[2 * sh + j, lo:hi] = cdf + up * jnp.exp(-0.5 * up * up) * 0.3989422804014327
-                active = (up * cdf).astype(BF)
-                keep[at, lo:hi] = active
-                if mod == 0 and sh == 1:
-                    pl.when(j == 0)(lambda: gather_wait("core", W2))
-                one = dot(active, w_out[mod])
-                part = one if part is None else part + one
+            if mod == 0:
+                pl.when(j == 0)(lambda: gather_wait("core", W1))
+            ups = [dot(low, w[mod]) + bias[mod] for w, bias, _, _, _ in shards]
+            pairs = [gelu(up) for up in ups]
+            for sh, (_, _, _, keep, at) in enumerate(shards):
+                keep[at, lo:hi], dgelu[2 * sh + j, lo:hi] = pairs[sh]
+            if mod == 0:
+                pl.when(j == 0)(lambda: gather_wait("core", W2))
+            ones = [dot(active, w_out[mod]) for (active, _), (_, _, w_out, _, _) in zip(pairs, shards)]
+            part = ones[0] + ones[1]
             ar_start(j, mod, 0, part)
         mate_start(j, ALOW, ACT)
 
@@ -634,13 +736,13 @@
             res_f[j, lo:hi] = dr
             low = dr.astype(BF)
             dyf[m, lo:hi] = low
+            dacts = [dot_nt(low, w_out[mod]) for _, w_out, _, _ in shards]
+            ds = [(dact * dgelu[2 * sh + j, lo:hi]).astype(BF) for sh, dact in enumerate(dacts)]
+            ones = [dot_nt(d, w_in[mod]) for d, (w_in, _, _, _) in zip(ds, shards)]
+            part = ones[0] + ones[1]
+            for d, (_, _, keep, at) in zip(ds, shards):
+                keep[at, lo:hi] = d
             count_rows(1, mod, dh, n, low)
-            part = None
-            for sh, (w_in, w_out, keep, at) in enumerate(shards):
-                d = (dot_nt(low, w_out[mod]) * dgelu[2 * sh + j, lo:hi]).astype(BF)
-                keep[at, lo:hi] = d
-                one = dot_nt(d, w_in[mod])
-                part = one if part is None else part + one
             ar_start(j, mod, 1, part)
         mate_start(j, DYF, DUP)
 
@@ -655,15 +757,14 @@
             low = dr.astype(BF)
             dya[m, lo:hi] = low
             count_rows(0, mod, dh, n, low)
+            dmixs = [dot_nt(low, w_out[mod]).astype(BF) for _, w_out, _, _ in shards]
+            grads = attend_back([
+                (dmix, (p_w, p_r)[mod][2 * sh + j], *(qkv[k, 2 * sh + j, lo:hi] for k in range(3)))
+                for sh, dmix in enumerate(dmixs)
+            ])
             part = None
-            for sh, (w, w_out, keep, at) in enumerate(shards):
-                slot = 2 * sh + j
-                dmix = dot_nt(low, w_out[mod]).astype(BF)
-                probs = p_w[slot] if mod == 0 else p_r[slot]
-                parts = attend_back(
-                    dmix, probs, qkv[0, slot, lo:hi], qkv[1, slot, lo:hi], qkv[2, slot, lo:hi]
-                )
-                d = jnp.concatenate(parts, axis=1)
+            for grad, (w, _, keep, at) in zip(grads, shards):
+                d = jnp.concatenate(grad, axis=1)
                 keep[at, lo:hi] = d
                 one = dot(d, w[mod])
                 part = one if part is None else part + one
@@ -679,14 +780,18 @@
             low = dr.astype(BF)
             dyc[m, lo:hi] = low
             count_rows(2, mod, dh, n, low)
+        shards = ((cwqkv_ref, cwo_ref, cdqkv, m), (cwqkv_m, cwo_m, cdqkv_m, j))
+        dmixs = [dot_nt(dyc[m], w_out[...]).astype(BF) for _, w_out, _, _ in shards]
+        cases = []
+        for sh, dmix in enumerate(dmixs):
+            slot = 2 * sh + j
+            q, k, v = cqkv[0, slot], cqkv[1, slot], cqkv[2, slot]
+            cases.append((dmix[:RW], cp_w[slot], q[:RW], k[RW:], v[RW:]))
+            cases.append((dmix[RW:], cp_r[slot], q[RW:], k[:RW], v[:RW]))
+        grads = attend_back(cases)
         part = None
-        shards = ((cwqkv_ref, cwo_ref, cdqkv, m), (cwqkv_m, cwo_m, cdqkv_m, j))
-        for sh, (w, w_out, keep, at) in enumerate(shards):
-            slot = 2 * sh + j
-            dmix = dot_nt(dyc[m], w_out[...]).astype(BF)
-            q, k, v = cqkv[0, slot], cqkv[1, slot], cqkv[2, slot]
-            dq_w, dk_r, dv_r = attend_back(dmix[:RW], cp_w[slot], q[:RW], k[RW:], v[RW:])
-            dq_r, dk_w, dv_w = attend_back(dmix[RW:], cp_r[slot], q[RW:], k[:RW], v[:RW])
+        for sh, (w, _, keep, at) in enumerate(shards):
+            (dq_w, dk_r, dv_r), (dq_r, dk_w, dv_w) = grads[2 * sh : 2 * sh + 2]
             keep[at, :RW] = jnp.concatenate([dq_w, dk_w, dv_w], axis=1)
             keep[at, RW:] = jnp.concatenate([dq_r, dk_r, dv_r], axis=1)
             one = dot(keep[at], w[...])
@@ -698,8 +803,7 @@
         m = block_of(j)
         for mod, (lo, hi) in enumerate(SPANS):
             back[m, lo:hi] = (res_f[j, lo:hi] + ar_finish(j, mod, 1)).astype(BF)
-        for copy in back_copies(j):
-            copy.start()
+        back_start(j)
 
     def column_sums(buf, lo, hi):
         rows = buf[:, lo:hi, :].astype(F32).reshape(MB * (hi - lo), buf.shape[-1])
@@ -753,147 +857,165 @@
             outer_tile(midf, cdqkv, 0, R, j, store(j, 0, 3 * HW))
             outer_tile(dyc, cmixed, 0, R, j, store(j, 3 * HW, D))
 
+    Y, Z, EVEN, ODD = range(4)
+    even_z, odd_z = z_at + 1 - 2 * lax.rem(z_at, 2), 3 - z_at
+    LAST = {Y: 2, Z: 2, EVEN: 3, ODD: 3}
+
     def dw_copies(group, phase):
-        index, y_first, lo, hi = group
+        index, kind, b = group
         sems = lambda k: (dw_send.at[index, k], dw_recv.at[index, k])
-        blocks = slice(lo, hi)
         if phase == 0:
-            src = g_ref.at[blocks, :, :, 1 - core]
-            return [moved(src, from_core.at[blocks], *sems(0), other_core)]
-        if y_first and phase == 1:
-            src = g_ref.at[blocks, 1 - y_at, :, core]
-            return [moved(src, from_y.at[blocks], *sems(1), other_y)]
-        if y_first:
+            return [moved(g_ref.at[b, :, :, 1 - core], from_core.at[b], *sems(0), other_core)]
+        if kind == Y:
+            if phase == 1:
+                return [moved(g_ref.at[b, 1 - y_at, :, core], from_y.at[b], *sems(1), other_y)]
             return [
                 moved(
-                    g_ref.at[blocks, y_at, z_next(o), core], from_z.at[blocks, o - 1],
-                    *sems(2), dp_device(y_at, z_next(o), core),
+                    g_ref.at[b, y_at, z_next(o), core], from_z.at[b, o - 1], *sems(2),
+                    dp_device(y_at, z_next(o), core),
                 )
                 for o in (1, 2, 3)
             ]
-        late = slice(lo - 4, hi - 4)
-        if phase == 1:
+        if phase == LAST[kind]:
+            src = g_ref.at[b, 1 - y_at, z_at, core]
+            return [moved(src, from_ys.at[b - 4], *sems(1), other_y)]
+        if kind == Z:
             return [
                 moved(
-                    g_ref.at[blocks, :, z_next(o), core], from_zs.at[late, o - 1],
-                    *sems(2), dp_device(y_at, z_next(o), core),
+                    g_ref.at[b, :, z_next(o), core], from_zs.at[o - 1], *sems(2),
+                    dp_device(y_at, z_next(o), core),
                 )
                 for o in (1, 2, 3)
             ]
-        src = g_ref.at[blocks, 1 - y_at, z_at, core]
-        return [moved(src, from_ys.at[late], *sems(1), other_y)]
+        near, far = (even_z, odd_z) if kind == EVEN else (odd_z, even_z)
+        to = lambda z: dp_device(y_at, z, core)
+        if phase == 1:
+            beyond = 3 - near if kind == EVEN else near + 1 - 2 * lax.rem(near, 2)
+            return [
+                moved(g_ref.at[b, :, z, core], from_h.at[b - 5, k], *sems(2), to(near))
+                for k, z in enumerate((near, beyond))
+            ]
+        return [moved(g_ref.at[b, :, far, core], from_h.at[b - 5, 2], *sems(3), to(far))]
 
     def dw_start(group, phase):
         for copy in dw_copies(group, phase):
             copy.start()
 
     def dw_finish(group, phase):
-        index, y_first, lo, hi = group
-        if phase == (2 if y_first else 1):
-            place = from_z.at[slice(lo, hi)] if y_first else from_zs.at[slice(lo - 4, hi - 4)]
-            moved(place, place, dw_send.at[index, 2], dw_recv.at[index, 2], other_core).wait()
+        index, kind, b = group
+        together = None
+        if kind == Y and phase == 2:
+            together = from_z.at[b]
+        elif kind == Z and phase == 1:
+            together = from_zs
+        elif kind in (EVEN, ODD) and phase == 1:
+            together = from_h.at[b - 5, pl.ds(0, 2)]
+        if together is None:
+            dw_copies(group, phase)[0].wait()
         else:
-            dw_copies(group, phase)[0].wait()
-
-        def add(b):
-            if phase == 0:
-                for y in range(2):
-                    mine = g_ref[b, y, :, core].astype(F32)
-                    g_ref[b, y, :, core] = (mine + from_core[b, y].astype(F32)).astype(BF)
-            elif phase == 1 and y_first:
-                mine = g_ref[b, y_at, :, core].astype(F32)
-                g_ref[b, y_at, :, core] = (mine + from_y[b].astype(F32)).astype(BF)
-            elif phase == 1:
-                total = g_ref[b, :, z_at, core].astype(F32)
-                for o in range(3):
-                    total = total + from_zs[b - 4, o].astype(F32)
-                g_ref[b, :, z_at, core] = total.astype(BF)
-            else:
-                total = g_ref[b, y_at, z_at, core].astype(F32)
-                for o in range(3 if y_first else 0):
-                    total = total + from_z[b, o].astype(F32)
-                if not y_first:
-                    total = total + from_ys[b - 4].astype(F32)
-                dw_ref[b] = total
-
-        pl.loop(lo, hi)(add)
+            moved(together, together, dw_send.at[index, 2], dw_recv.at[index, 2], other_core).wait()
+
+        def add(place, *others):
+            total = g_ref[place].astype(F32)
+            for other in others:
+                total = total + other.astype(F32)
+            return total
+
+        if phase == 0:
+
+            def sum_y(y):
+                place = (b, y, slice(None), core)
+                g_ref[place] = add(place, from_core[b, y]).astype(BF)
+
+            pl.loop(0, 2)(sum_y)
+            return
+        mine = (b, y_at, z_at, core)
+        if phase == LAST[kind]:
+            others = [from_z[b, o] for o in range(3)] if kind == Y else [from_ys[b - 4]]
+            dw_ref[b] = add(mine, *others)
+            return
+        every = slice(None)
+        if kind == Y:
+            sums_of = [((b, y_at, every, core), [from_y[b]])]
+        elif kind == Z:
+            sums_of = [((b, every, z_at, core), [from_zs[o] for o in range(3)])]
+        elif phase == 1:
+            far = odd_z if kind == EVEN else even_z
+            sums_of = [((b, every, z, core), [from_h[b - 5, k]]) for k, z in enumerate((z_at, far))]
+        else:
+            sums_of = [((b, every, z_at, core), [from_h[b - 5, 2]])]
+        for place, others in sums_of:
+            g_ref[place] = add(place, *others).astype(BF)
 
     def dw_turn(group, phase):
         dw_finish(group, phase)
         dw_start(group, phase + 1)
 
-    OUT_W, OUT_R, IN_W, IN_R = (0, True, 1, 2), (1, True, 2, 3), (2, False, 5, 6), (3, False, 6, 7)
-    ATTN_W, ATTN_R, CROSS = (4, True, 0, 1), (5, False, 4, 5), (6, True, 3, 4)
-
-    def sm_copies(step):
-        sems = lambda k: (sm_send.at[k], sm_recv.at[k])
+    OUT_W, OUT_R, IN_W, IN_R = (0, Y, 1), (1, Y, 2), (2, EVEN, 5), (3, ODD, 6)
+    ATTN_W, ATTN_R, CROSS = (4, Y, 0), (5, Z, 4), (6, Y, 3)
+
+    def sm_copies(step, count):
+        sems = (sm_send.at[step], sm_recv.at[step])
         if step == 0:
-            return [
-                moved(sums_t.at[me], sums_t.at[me], *sems(0), peer(o)) for o in range(1, TENSOR)
-            ]
+            return [moved(sums_t.at[me], sums_t.at[me], *sems, peer(o)) for o in range(1, TENSOR)]
+        rows = pl.ds(0, count)
+        src = sums.at[step - 1, rows]
         if step == 1:
-            return [moved(sums.at[0], sums_c, *sems(1), other_core)]
+            return [moved(src, sums_c.at[rows], *sems, other_core)]
         if step == 2:
-            return [moved(sums.at[1], sums_y, *sems(2), other_y)]
+            return [moved(src, sums_y.at[rows], *sems, other_y)]
         return [
-            moved(
-                sums.at[2], sums_z.at[o - 1], *sems(3), dp_device(y_at, z_next(o), core)
-            )
-            for o in (1, 2, 3)
+            moved(src, sums_z.at[o - 1, rows], *sems, dp_device(y_at, z_next(o), core)) for o in (1, 2, 3)
         ]
 
-    def sm_start(step):
-        for copy in sm_copies(step):
+    def sm_start(step, count=32):
+        for copy in sm_copies(step, count):
             copy.start()
 
-    def sm_wait(step):
+    def sm_wait(step, count=32):
         if step in (0, 3):
-            place = sums_z if step == 3 else sums_t.at[pl.ds(0, TENSOR - 1)]
+            place = sums_z.at[:, pl.ds(0, count)] if step == 3 else sums_t.at[pl.ds(0, TENSOR - 1)]
             moved(place, place, sm_send.at[step], sm_recv.at[step], other_core).wait()
         else:
-            sm_copies(step)[0].wait()
-
-    def small_norms_all():
+            sm_copies(step, count)[0].wait()
+
+    def small_norms():
+        counts = jnp.logical_or(head, me < 2)
         for k in range(15):
-            sums_t[me, k : k + 1, :] = jnp.where(me < 2, row_sums[k], 0.0)
+            sums_t[me, k : k + 1, :] = jnp.where(counts, row_sums[k], 0.0)
         sums_t[me, 15:16, :] = jnp.zeros((1, D), F32)
         sm_start(0)
 
-    def small_norms():
-        sums_t[me] = jnp.zeros((16, D), F32)
-        for l in range(2):
-            for k in range(3):
-                a = acc[3 * l + k]
-                at = 2 * (3 * l + k)
-                sums_t[me, at : at + 1, :] = jnp.sum(jnp.where(is_word, a, 0.0), axis=0, keepdims=True)
-                sums_t[me, at + 1 : at + 2, :] = jnp.sum(
-                    jnp.where(is_word, 0.0, a), axis=0, keepdims=True
-                )
-        sm_start(0)
-
-    def small_biases():
+    def small_biases(count):
         sm_wait(0)
-        sums[0] = jnp.zeros((24, D), F32)
-        sums[0, :16] = sums_t[0] + sums_t[1] + sums_t[2] + sums_t[3]
+        total[...] = jnp.zeros((32, D), F32)
+        norms = sums_t[0] + sums_t[1] + sums_t[2] + sums_t[3]
+        total[0:12] = norms[:12]
+        total[16:19] = norms[12:15]
         for mod in range(2):
-            sums[0, 16 + mod : 17 + mod, :] = bsum[mod]
-        for k in range(3):
-            sums[0, 18 + k : 19 + k, : 3 * HW] = bqsum[k]
-        sm_start(1)
-
-    def small_y():
-        sm_wait(1)
-        sums[1] = sums[0] + sums_c[...]
-        sm_start(2)
-
-    def small_z():
-        sm_wait(2)
-        sums[2] = sums[1] + sums_y[...]
-        sm_start(3)
-
-    def small_last():
-        sm_wait(3)
-        s_ref[...] = sums[2] + sums_z[0] + sums_z[1] + sums_z[2]
+            total[12 + mod : 13 + mod, :] = bsum[mod]
+            total[14 + mod : 15 + mod, : 3 * HW] = bqsum[mod]
+        total[19:20, : 3 * HW] = bqsum[2]
+        sums[0] = total[...].astype(BF)
+        sm_start(1, count)
+
+    def small_y(count):
+        sm_wait(1, count)
+        total[:count] = total[:count] + sums_c[:count].astype(F32)
+        sums[1] = total[...].astype(BF)
+        sm_start(2, count)
+
+    def small_z(count):
+        sm_wait(2, count)
+        total[:count] = total[:count] + sums_y[:count].astype(F32)
+        sums[2] = total[...].astype(BF)
+        sm_start(3, count)
+
+    def small_last(count):
+        sm_wait(3, count)
+        for o in range(3):
+            total[:count] = total[:count] + sums_z[o, :count].astype(F32)
+        s_ref[...] = total[:24]
 
     def packet():
         return moved(pack.at[0], pack.at[1], pk_send, pk_recv, partner)
@@ -921,17 +1043,16 @@
     @pl.when(head)
     def _():
         def to_partner(m):
-            midf[m, own] = layer_d(m).astype(BF)
-            mid_copy(m).start()
+            put_own_rows(midf, m, layer_d(m).astype(BF))
+            mid_start(m)
 
         def from_partner(m):
-            mid_copy(m).wait_send()
+            some_rows(midf, m, C, sec_send.at[m], sec_recv.at[m]).wait_send()
             back_arrive(m)
-            back_e(m, back[m, own].astype(F32))
+            back_e(m, own_rows_of(back, m).astype(F32))
 
         def last(m):
-            ybuf[m, own] = (res[m] + rs_finish(m)).astype(BF)
-            ag_start(ybuf, m, y_send, y_recv)
+            ag_start(ybuf, m, (res[m] + rs_finish(m)).astype(BF), y_send, y_recv)
 
         front, rear = dict(first=0, last=2), dict(first=2, last=4)
         wait_weights(0, 1)
@@ -969,23 +1090,26 @@
         each(
             back_h,
             after=(
-                then(p(dw_turn, IN_W, 0), p(dw_turn, OUT_W, 0)), small_norms, None, then(p(dw_turn, IN_R, 1), p(dw_turn, OUT_R, 1)),
+                then(p(dw_turn, IN_W, 0), p(dw_turn, OUT_W, 0)), small_norms,
             ),
         )
         attn_piece(2)
         attn_piece(3)
         dw_start(ATTN_R, 0)
-        small_biases()
+        dw_turn(IN_R, 1)
+        dw_turn(OUT_R, 1)
         attn_piece(0)
+        dw_turn(ATTN_R, 0)
         attn_piece(1)
         dw_start(ATTN_W, 0)
-        small_y()
-        dw_turn(ATTN_R, 0)
+        dw_turn(IN_W, 1)
+        small_biases(16)
+        each(last)
         dw_turn(ATTN_W, 0)
+        small_y(16)
         dw_turn(OUT_W, 1)
-        small_z()
-        dw_turn(IN_W, 1)
-        each(last)
+        dw_turn(IN_R, 2)
+        small_z(16)
 
     @pl.when(cross)
     def _():
@@ -1059,7 +1183,7 @@
         ffn_piece(1)
         dw_start(OUT_W, 0)
         dw_turn(OUT_R, 0)
-        small_norms_all()
+        small_norms()
         for mod, (lo, hi) in enumerate(SPANS):
             bsum[mod] = column_sums(dup, lo, hi)
         dw_turn(OUT_W, 0)
@@ -1067,7 +1191,7 @@
         pass_start(DYC)
         mate_start_all(DYA, DQKV)
         for k in range(2):
-            ag_finish(midf, 2 * (1 - set_of) + k)
+            mid_finish(2 * (1 - set_of) + k)
         mate_wait(CDQKV)
         pass_wait(DYC)
         cross_outer()
@@ -1080,6 +1204,8 @@
         dw_turn(OUT_R, 1)
         dw_turn(IN_W, 1)
         dw_turn(OUT_W, 1)
+        dw_turn(IN_R, 2)
+        dw_turn(IN_W, 2)
         dw_turn(CROSS, 1)
         mate_wait(DQKV)
         mate_start_all(YBUF)
@@ -1087,16 +1213,16 @@
         pass_wait(DYA)
         for mod, (lo, hi) in enumerate(SPANS):
             bqsum[mod] = column_sums(dqkv, lo, hi)
-        small_biases()
+        small_biases(32)
         attn_piece(2)
         attn_piece(3)
         dw_start(ATTN_R, 0)
-        small_y()
+        small_y(32)
         attn_piece(0)
         attn_piece(1)
         dw_start(ATTN_W, 0)
         dw_turn(ATTN_R, 0)
-        small_z()
+        small_z(32)
         dw_turn(ATTN_W, 0)
         mate_wait(YBUF)
         pass_start(YBUF)
@@ -1113,13 +1239,15 @@
 
         y_ref[m] = ybuf[m]
 
-    dw_finish(IN_R, 2)
-    dw_finish(OUT_R, 2)
+    pl.when(head)(p(dw_turn, IN_W, 2))
     dw_turn(ATTN_R, 1)
     dw_turn(ATTN_W, 1)
-    dw_finish(IN_W, 2)
+    dw_finish(OUT_R, 2)
+    dw_finish(IN_R, 3)
+    dw_finish(IN_W, 3)
     dw_finish(OUT_W, 2)
-    small_last()
+    pl.when(head)(p(small_last, 16))
+    pl.when(cross)(p(small_last, 32))
     each(write)
 
     @pl.when(cross)
@@ -1173,13 +1301,13 @@
     columns = from_column(small, 8 * place)
     for mod in range(2):
         for k in range(6):
-            b1_g[0, k, mod : mod + 1, :] = columns[16 + mod : 17 + mod, 128 * k : 128 * k + 8]
+            b1_g[0, k, mod : mod + 1, :] = columns[12 + mod : 13 + mod, 128 * k : 128 * k + 8]
     columns = from_column(small, 4 * place)
     for mod in range(2):
         for j in range(2):
             for h in range(LOCAL_HEADS):
                 lo = 2 * j * HW + h * HEAD_DIM
-                qv_bias_g[0, mod, h, j : j + 1, :] = columns[18 + mod : 19 + mod, lo : lo + 4]
+                qv_bias_g[0, mod, h, j : j + 1, :] = columns[14 + mod : 15 + mod, lo : lo + 4]
     wide = dc_ref[...]
     for j in range(3):
         cqkv_g[j] = wide[:, j * HW : (j + 1) * HW]
@@ -1187,8 +1315,8 @@
     small = sc_ref[...]
     columns = from_column(small, 24 * both)
     for k, ref in enumerate((cgain_g, cshift_g, cobias_g)):
-        ref[...] = columns[12 + k, :24]
-    columns = from_column(small, 2 * both)[20:21]
+        ref[...] = columns[16 + k, :24]
+    columns = from_column(small, 2 * both)[19:20]
     for j in range(2):
         heads = []
         for h in range(LOCAL_HEADS):
@@ -1251,8 +1379,10 @@
             pltpu.VMEM((MB, C, D), F32),
             pltpu.VMEM((2, MB, C, D), F32),
             pltpu.VMEM((2, MB, C, 128), F32),
-            pltpu.VMEM((6, C, D), F32),
-            pltpu.VMEM((6, C, D), F32),
+            pltpu.VMEM((MB, 16, D), BF),
+            pltpu.VMEM((MB, 16, D), BF),
+            pltpu.VMEM((C, D), F32),
+            pltpu.VMEM((C, D), BF),
             pltpu.VMEM((2, 1, D), F32),
             pltpu.VMEM((3, 1, 3 * HW), F32),
             pltpu.VMEM((2, 3 * HW, D), BF),
@@ -1270,6 +1400,8 @@
             pltpu.VMEM((3, 1, 3 * HW), F32),
             pltpu.VMEM((2, 1, D), F32),
             pltpu.VMEM((2, 2, R, D), BF),
+            pltpu.VMEM((2, 2, 16, D // 2), BF),
+            pltpu.VMEM((2, 2, 2, 16, D // 2), BF),
             *[pltpu.VMEM((2, R, w), BF) for w in (D, D, HW, 3 * HW, HW, 3 * HW)],
             pltpu.VMEM((2, R, D), F32),
             pltpu.VMEM((2, R, D), F32),
@@ -1279,27 +1411,29 @@
             pltpu.VMEM((7, 2, 4, 2, 48, D), BF),
             pltpu.VMEM((7, 2, 4, 48, D), BF),
             pltpu.VMEM((4, 4, 48, D), BF),
-            pltpu.VMEM((3, 3, 2, 48, D), BF),
+            pltpu.VMEM((3, 2, 48, D), BF),
+            pltpu.VMEM((2, 3, 2, 48, D), BF),
             pltpu.VMEM((4, 3, 48, D), BF),
             pltpu.VMEM((3, 48, D), BF),
-            pltpu.VMEM((3, 24, D), F32),
+            pltpu.VMEM((3, 32, D), BF),
+            pltpu.VMEM((32, D), F32),
             pltpu.VMEM((TENSOR, 16, D), F32),
-            pltpu.VMEM((24, D), F32),
-            pltpu.VMEM((24, D), F32),
-            pltpu.VMEM((3, 24, D), F32),
+            pltpu.VMEM((32, D), BF),
+            pltpu.VMEM((32, D), BF),
+            pltpu.VMEM((3, 32, D), BF),
             pltpu.VMEM((2, 48, D), F32),
             *[pltpu.SemaphoreType.DMA((MB,)) for _ in range(6)],
             pltpu.SemaphoreType.DMA((MB,)),
             pltpu.SemaphoreType.DMA((MB,)),
-            pltpu.SemaphoreType.DMA((7, 3)),
-            pltpu.SemaphoreType.DMA((7, 3)),
+            pltpu.SemaphoreType.DMA((7, 4)),
+            pltpu.SemaphoreType.DMA((7, 4)),
             pltpu.SemaphoreType.DMA((4,)),
             pltpu.SemaphoreType.DMA((4,)),
             pltpu.SemaphoreType.DMA,
             pltpu.SemaphoreType.DMA,
             pltpu.SemaphoreType.DMA((2,)),
             pltpu.SemaphoreType.DMA((MB,)),
-            *[pltpu.SemaphoreType.DMA((2, 2, 2)) for _ in range(2)],
+            *[pltpu.SemaphoreType.DMA((2, 2, 4)) for _ in range(2)],
             *[pltpu.SemaphoreType.DMA((12,)) for _ in range(2)],
             *[pltpu.SemaphoreType.DMA((7, 4)) for _ in range(2)],
             *[pltpu.SemaphoreType.DMA((6,)) for _ in range(2)],

time: 162 us -> 152 us (0.938)
  Pallas kernels: 161 us -> 151 us
    pallas_call x1, Pallas kernels: 158 us -> 147 us  [local(): pl.pallas_call(kernel, out_shape=(jax.ShapeDtypeStruct((MB, R, D), BF), j...]
where the time goes in v6:
time: 152 us
  Pallas kernels  151 us (99%)
    pallas_call x1, Pallas kernels, local(): pl.pallas_call(kernel, out_shape=(jax.ShapeDtypeStruct((MB, R, D), BF), j...  147 us
    pallas_call x1, Pallas kernels, local(): pl.pallas_call(arrange, out_shape=tuple((jax.ShapeDtypeStruct(shape, F32)...  3.27 us

profile of v6, /device:TPU:0, one launch (start us, length us, event | category | flops | bytes accessed | tf_op | source)
XLA Modules:
  0.0 151.5 jit_solution(15774280704599865012)
XLA Ops:
  0.7 147.4 %shard_map.314 = (bf16[4,128,768]{2,1,0:T(8,128)(2,1)}, f32[7,48,768]{2,1,0:T(8,128)}, f32[24,768]{1,0:T(8,128)}, f32[24,768]{1,0:T(8,128)}, f32[24,768]{1,0:T(8,128)}) custom-call(bf16[1,20,8,768]{3,2,1,0:T(8,128)(2,1)} %bitcast.30, bf16[1,36,8,768]{3,2,1,0:T(8,128)(2,1)} %bitcast.29, s32[8]{0:T(128)} %lengths_ref.1, s32[8]{0:T(128)} %flags_ref.1, ...), custom_call_target="tpu_custom_call" | custom-call | tf_op jit(solution)/shard_map/pallas_call | solution.py:1346
  148.1 3.3 %shard_map.315 = (f32[1,20,8,768]{3,2,1,0:T(8,128)}, f32[1,36,8,768]{3,2,1,0:T(8,128)}, f32[1,2,3,48,192]{4,3,2,1,0:T(8,128)}, f32[1,2,3,2,4]{4,3,2,1,0:T(2,128)...) custom-call(bf16[4,128,768]{2,1,0:T(8,128)(2,1)} %get-tuple-element., ...), custom_call_target="tpu_custom_call" | custom-call | tf_op jit(solution)/shard_map/pallas_call | solution.py:1457

commit v7 on v6

--- a/solution.py
+++ b/solution.py
@@ -149,8 +149,8 @@
     words_ref, regions_ref, lengths_ref, flags_ref, wqkv_in, qv_bias_ref, wo_in, w1_in, b1_in_ref,
     w2_in, out_bias_ref, gain_ref, shift_ref, cwqkv_in, cqv_bias_ref, cwo_in, cout_bias_ref,
     cgain_ref, cshift_ref,
-    y_ref, dw_ref, s_ref, dc_ref, sc_ref,
-    x_ref, bqkv_ref, b1_ref, cvec_ref, send, recv, xlow, midf, alow, dyf, dya, dyc, ybuf, back,
+    y_out, dw_out, s_ref, dc_ref, sc_ref,
+    dw_ref, out_sems, x_ref, bqkv_ref, b1_ref, cvec_ref, send, recv, xlow, midf, alow, dyf, dya, dyc, ybuf, back,
     qkv, mixed, dqkv, cqkv, cmixed, cdqkv, act, dup, dgelu,
     p_w, p_r, cp_w, cp_r, cur, res, nrm, rstd, packed, gathered_end, total_ref, low_ref, bsum, bqsum,
     wqkv_ref, wo_ref, w1_ref, w2_ref, cwqkv_ref, cwo_ref, wqkv_m, wo_m, w1_m, w2_m, cwqkv_m, cwo_m, bqkv_m, b1_m,
@@ -272,7 +272,7 @@
     @pl.when(cross)
     def _():
         pl.semaphore_wait(barrier, 12)
-        gather_start("x", CWQKV, CWO, WQKV, WO, W1, W2)
+        gather_start("x", CWQKV, CWO, WQKV, WO, W1)
 
     def side_by_side(rows):
         return jnp.concatenate(rows, axis=1)
@@ -857,18 +857,34 @@
             outer_tile(midf, cdqkv, 0, R, j, store(j, 0, 3 * HW))
             outer_tile(dyc, cmixed, 0, R, j, store(j, 3 * HW, D))
 
-    Y, Z, EVEN, ODD = range(4)
+    Y, Z, EVEN, ODD, Y_EVEN, Y_ODD = range(6)
     even_z, odd_z = z_at + 1 - 2 * lax.rem(z_at, 2), 3 - z_at
-    LAST = {Y: 2, Z: 2, EVEN: 3, ODD: 3}
+    LAST = {Y: 2, Z: 2, EVEN: 3, ODD: 3, Y_EVEN: 3, Y_ODD: 3}
+    Y_FIRST_KINDS = (Y, Y_EVEN, Y_ODD)
+
+    def z_links(kind):
+        return (even_z, odd_z) if kind in (EVEN, Y_EVEN) else (odd_z, even_z)
+
+    def beyond(kind, near):
+        return 3 - near if kind in (EVEN, Y_EVEN) else near + 1 - 2 * lax.rem(near, 2)
 
     def dw_copies(group, phase):
         index, kind, b = group
         sems = lambda k: (dw_send.at[index, k], dw_recv.at[index, k])
         if phase == 0:
             return [moved(g_ref.at[b, :, :, 1 - core], from_core.at[b], *sems(0), other_core)]
+        to = lambda z: dp_device(y_at, z, core)
+        if kind in Y_FIRST_KINDS and phase == 1:
+            return [moved(g_ref.at[b, 1 - y_at, :, core], from_y.at[b], *sems(1), other_y)]
+        if kind in (Y_EVEN, Y_ODD):
+            near, far = z_links(kind)
+            if phase == 3:
+                return [moved(g_ref.at[b, y_at, far, core], from_z.at[b, 2], *sems(3), to(far))]
+            return [
+                moved(g_ref.at[b, y_at, z, core], from_z.at[b, k], *sems(2), to(near))
+                for k, z in enumerate((near, beyond(kind, near)))
+            ]
         if kind == Y:
-            if phase == 1:
-                return [moved(g_ref.at[b, 1 - y_at, :, core], from_y.at[b], *sems(1), other_y)]
             return [
                 moved(
                     g_ref.at[b, y_at, z_next(o), core], from_z.at[b, o - 1], *sems(2),
@@ -887,13 +903,11 @@
                 )
                 for o in (1, 2, 3)
             ]
-        near, far = (even_z, odd_z) if kind == EVEN else (odd_z, even_z)
-        to = lambda z: dp_device(y_at, z, core)
+        near, far = z_links(kind)
         if phase == 1:
-            beyond = 3 - near if kind == EVEN else near + 1 - 2 * lax.rem(near, 2)
             return [
                 moved(g_ref.at[b, :, z, core], from_h.at[b - 5, k], *sems(2), to(near))
-                for k, z in enumerate((near, beyond))
+                for k, z in enumerate((near, beyond(kind, near)))
             ]
         return [moved(g_ref.at[b, :, far, core], from_h.at[b - 5, 2], *sems(3), to(far))]
 
@@ -910,6 +924,8 @@
             together = from_zs
         elif kind in (EVEN, ODD) and phase == 1:
             together = from_h.at[b - 5, pl.ds(0, 2)]
+        elif kind in (Y_EVEN, Y_ODD) and phase == 2:
+            together = from_z.at[b, pl.ds(0, 2)]
         if together is None:
             dw_copies(group, phase)[0].wait()
         else:
@@ -931,17 +947,26 @@
             return
         mine = (b, y_at, z_at, core)
         if phase == LAST[kind]:
-            others = [from_z[b, o] for o in range(3)] if kind == Y else [from_ys[b - 4]]
+            if kind == Y:
+                others = [from_z[b, o] for o in range(3)]
+            elif kind in Y_FIRST_KINDS:
+                others = [from_z[b, 2]]
+            else:
+                others = [from_ys[b - 4]]
             dw_ref[b] = add(mine, *others)
+            if b != 3:
+                pltpu.make_async_copy(dw_ref.at[b], dw_out.at[b], out_sems.at[b]).start()
             return
         every = slice(None)
-        if kind == Y:
+        if kind in Y_FIRST_KINDS and phase == 1:
             sums_of = [((b, y_at, every, core), [from_y[b]])]
+        elif kind in (Y_EVEN, Y_ODD):
+            sums_of = [((b, y_at, z, core), [from_z[b, k]]) for k, z in enumerate((z_at, z_links(kind)[1]))]
         elif kind == Z:
             sums_of = [((b, every, z_at, core), [from_zs[o] for o in range(3)])]
         elif phase == 1:
-            far = odd_z if kind == EVEN else even_z
-            sums_of = [((b, every, z, core), [from_h[b - 5, k]]) for k, z in enumerate((z_at, far))]
+            places = (z_at, z_links(kind)[1])
+            sums_of = [((b, every, z, core), [from_h[b - 5, k]]) for k, z in enumerate(places)]
         else:
             sums_of = [((b, every, z_at, core), [from_h[b - 5, 2]])]
         for place, others in sums_of:
@@ -951,7 +976,7 @@
         dw_finish(group, phase)
         dw_start(group, phase + 1)
 
-    OUT_W, OUT_R, IN_W, IN_R = (0, Y, 1), (1, Y, 2), (2, EVEN, 5), (3, ODD, 6)
+    OUT_W, OUT_R, IN_W, IN_R = (0, Y_EVEN, 1), (1, Y_ODD, 2), (2, EVEN, 5), (3, ODD, 6)
     ATTN_W, ATTN_R, CROSS = (4, Y, 0), (5, Z, 4), (6, Y, 3)
 
     def sm_copies(step, count):
@@ -1096,25 +1121,31 @@
         attn_piece(2)
         attn_piece(3)
         dw_start(ATTN_R, 0)
+        dw_turn(OUT_R, 1)
         dw_turn(IN_R, 1)
-        dw_turn(OUT_R, 1)
         attn_piece(0)
         dw_turn(ATTN_R, 0)
         attn_piece(1)
         dw_start(ATTN_W, 0)
         dw_turn(IN_W, 1)
         small_biases(16)
-        each(last)
         dw_turn(ATTN_W, 0)
         small_y(16)
+        each(last)
         dw_turn(OUT_W, 1)
+        dw_turn(OUT_R, 2)
         dw_turn(IN_R, 2)
+        dw_turn(IN_W, 2)
+        dw_turn(OUT_W, 2)
+        dw_turn(ATTN_R, 1)
         small_z(16)
+        dw_turn(ATTN_W, 1)
 
     @pl.when(cross)
     def _():
         for copy in bias_copies():
             copy.start()
+        gather_start("x", W2)
         gather_wait("x", CWQKV, CWO)
         gather_start("z", CWQKV, CWO)
         gather_wait("x", WQKV, WO)
@@ -1130,13 +1161,14 @@
         gather_start("y", WO)
         gather_wait("y", W1)
         gather_start("z", W1)
-        gather_wait("x", W2)
-        gather_start("y", W2)
         for copy in bias_copies():
             copy.wait()
         gather_wait("core", CWQKV, CWO)
         wait_weights(0, 1, 2, 3, 4, 5)
-        pl.loop(0, 3)(mid_relay)
+        pl.loop(0, 2)(mid_relay)
+        gather_wait("x", W2)
+        gather_start("y", W2)
+        mid_relay(2)
 
         @pl.when(set_of == 1)
         def _():
@@ -1159,9 +1191,9 @@
         attn_forward(0)
         gather_wait("z", W1)
         gather_start("core", W1)
-        attn_forward(1)
         gather_wait("y", W2)
         gather_start("core", W2)
+        attn_forward(1)
         pair(ffn_forward)
         pair(ffn_turn)
         pair(attn_backward)
@@ -1203,10 +1235,6 @@
         dw_turn(IN_R, 1)
         dw_turn(OUT_R, 1)
         dw_turn(IN_W, 1)
-        dw_turn(OUT_W, 1)
-        dw_turn(IN_R, 2)
-        dw_turn(IN_W, 2)
-        dw_turn(CROSS, 1)
         mate_wait(DQKV)
         mate_start_all(YBUF)
         pass_wait(XLOW)
@@ -1218,48 +1246,53 @@
         attn_piece(3)
         dw_start(ATTN_R, 0)
         small_y(32)
+        dw_turn(OUT_W, 1)
         attn_piece(0)
         attn_piece(1)
         dw_start(ATTN_W, 0)
+        dw_turn(CROSS, 1)
+        small_z(32)
         dw_turn(ATTN_R, 0)
-        small_z(32)
         dw_turn(ATTN_W, 0)
+        dw_turn(IN_R, 2)
+        dw_turn(IN_W, 2)
+        dw_turn(OUT_R, 2)
+        dw_turn(OUT_W, 2)
         mate_wait(YBUF)
         pass_start(YBUF)
         dw_finish(CROSS, 2)
-        pass_wait(YBUF)
-        for j in range(2):
-            rows = back.at[block_of(j), pl.ds(0, 2 * C)]
-            moved(rows, rows, back_send.at[j], back_recv.at[0], partner).wait_send()
-
-    def write(m):
-        @pl.when(head)
-        def _():
-            ag_finish(ybuf, m, y_send, y_recv)
-
-        y_ref[m] = ybuf[m]
-
-    pl.when(head)(p(dw_turn, IN_W, 2))
-    dw_turn(ATTN_R, 1)
-    dw_turn(ATTN_W, 1)
-    dw_finish(OUT_R, 2)
-    dw_finish(IN_R, 3)
-    dw_finish(IN_W, 3)
-    dw_finish(OUT_W, 2)
-    pl.when(head)(p(small_last, 16))
-    pl.when(cross)(p(small_last, 32))
-    each(write)
-
-    @pl.when(cross)
-    def _():
+        small_last(32)
         pack[0, :24] = dw_ref[3, :24]
         pack[0, 24:] = s_ref[...]
         packet().start()
         dc_ref[...] = dw_ref[3, 24:]
         sc_ref[...] = s_ref[...]
-
+        dw_turn(ATTN_R, 1)
+        dw_turn(ATTN_W, 1)
+        pass_wait(YBUF)
+        for j in range(2):
+            rows = back.at[block_of(j), pl.ds(0, 2 * C)]
+            moved(rows, rows, back_send.at[j], back_recv.at[0], partner).wait_send()
+
+    def write(m):
+        @pl.when(head)
+        def _():
+            ag_finish(ybuf, m, y_send, y_recv)
+
+        pltpu.make_async_copy(ybuf.at[m], y_out.at[m], out_sems.at[7 + m]).start()
+
+    each(write)
+    dw_finish(OUT_R, 3)
+    dw_finish(IN_R, 3)
+    dw_finish(IN_W, 3)
+    dw_finish(OUT_W, 3)
+    pl.when(head)(p(small_last, 16))
     dw_finish(ATTN_W, 2)
     dw_finish(ATTN_R, 2)
+    for b in (0, 1, 2, 4, 5, 6):
+        pltpu.make_async_copy(dw_ref.at[b], dw_out.at[b], out_sems.at[b]).wait()
+    for m in range(MB):
+        pltpu.make_async_copy(ybuf.at[m], y_out.at[m], out_sems.at[7 + m]).wait()
     pl.when(cross)(lambda: packet().wait_send())
 
     @pl.when(head)
@@ -1353,8 +1386,10 @@
             jax.ShapeDtypeStruct((24, D), F32),
         ),
         in_specs=[smem if k in (2, 3) else hbm if k in (4, 6, 7, 9, 13, 15) else vmem for k in range(len(inputs))],
-        out_specs=[vmem] * 5,
+        out_specs=[hbm] * 2 + [vmem] * 3,
         scratch_shapes=[
+            pltpu.VMEM((7, 48, D), F32),
+            pltpu.SemaphoreType.DMA((7 + MB,)),
             mb_rows(D, BF),
             pltpu.VMEM((3, 1, 3 * HW), F32),
             pltpu.VMEM((2, 1, D), F32),

time: 152 us -> 149 us (0.980)
  Pallas kernels: 151 us -> 147 us
    pallas_call x1, Pallas kernels: 147 us -> 144 us  [local(): pl.pallas_call(kernel, out_shape=(jax.ShapeDtypeStruct((MB, R, D), BF), j...]
where the time goes in v7:
time: 149 us; the launch traced here: 148 us
  Pallas kernels  147 us (99%)
    pallas_call x1, Pallas kernels, local(): pl.pallas_call(kernel, out_shape=(jax.ShapeDtypeStruct((MB, R, D), BF), j...  144 us
    pallas_call x1, Pallas kernels, local(): pl.pallas_call(arrange, out_shape=tuple((jax.ShapeDtypeStruct(shape, F32)...  3.27 us

profile of v7, /device:TPU:0, one launch (start us, length us, event | category | flops | bytes accessed | tf_op | source)
XLA Modules:
  0.0 148.2 jit_solution(4372009467155037392)
XLA Ops:
  0.7 144.1 %shard_map.314 = (bf16[4,128,768]{2,1,0:T(8,128)(2,1)}, f32[7,48,768]{2,1,0:T(8,128)}, f32[24,768]{1,0:T(8,128)}, f32[24,768]{1,0:T(8,128)}, f32[24,768]{1,0:T(8,128)}) custom-call(bf16[1,20,8,768]{3,2,1,0:T(8,128)(2,1)} %bitcast.30, bf16[1,36,8,768]{3,2,1,0:T(8,128)(2,1)} %bitcast.29, s32[8]{0:T(128)} %lengths_ref.1, s32[8]{0:T(128)} %flags_ref.1, ...), custom_call_target="tpu_custom_call" | custom-call | tf_op jit(solution)/shard_map/pallas_call | solution.py:1379
  144.7 3.3 %shard_map.315 = (f32[1,20,8,768]{3,2,1,0:T(8,128)}, f32[1,36,8,768]{3,2,1,0:T(8,128)}, f32[1,2,3,48,192]{4,3,2,1,0:T(8,128)}, f32[1,2,3,2,4]{4,3,2,1,0:T(2,128)...) custom-call(bf16[4,128,768]{2,1,0:T(8,128)(2,1)} %get-tuple-element., ...), custom_call_target="tpu_custom_call" | custom-call | tf_op jit(solution)/shard_map/pallas_call | solution.py:1492

commit v8 on v7

--- a/solution.py
+++ b/solution.py
@@ -146,17 +146,18 @@
 
 
 def kernel(
-    words_ref, regions_ref, lengths_ref, flags_ref, wqkv_in, qv_bias_ref, wo_in, w1_in, b1_in_ref,
-    w2_in, out_bias_ref, gain_ref, shift_ref, cwqkv_in, cqv_bias_ref, cwo_in, cout_bias_ref,
-    cgain_ref, cshift_ref,
+    words_hbm, regions_hbm, lengths_hbm, flags_hbm, wqkv_in, qv_bias_hbm, wo_in, w1_in, b1_in_hbm,
+    w2_in, out_bias_hbm, gain_hbm, shift_hbm, cwqkv_in, cqv_bias_hbm, cwo_in, cout_bias_hbm,
+    cgain_hbm, cshift_hbm,
     y_out, dw_out, s_ref, dc_ref, sc_ref,
-    dw_ref, out_sems, x_ref, bqkv_ref, b1_ref, cvec_ref, send, recv, xlow, midf, alow, dyf, dya, dyc, ybuf, back,
+    words_ref, regions_ref, lengths_ref, flags_ref, qv_bias_ref, b1_in_ref, out_bias_ref, gain_ref, shift_ref, cqv_bias_ref, cout_bias_ref, cgain_ref, cshift_ref,
+    small_loads, dw_ref, out_sems, x_ref, bqkv_ref, b1_ref, cvec_ref, send, recv, xlow, midf, alow, dyf, dya, dyc, ybuf, back,
     qkv, mixed, dqkv, cqkv, cmixed, cdqkv, act, dup, dgelu,
     p_w, p_r, cp_w, cp_r, cur, res, nrm, rstd, packed, gathered_end, total_ref, low_ref, bsum, bqsum,
     wqkv_ref, wo_ref, w1_ref, w2_ref, cwqkv_ref, cwo_ref, wqkv_m, wo_m, w1_m, w2_m, cwqkv_m, cwo_m, bqkv_m, b1_m,
     got, tails, got_tails, act_m, dup_m, mixed_m, dqkv_m, cmixed_m, cdqkv_m, cur_f, res_f, nrm_f, rstd_f, row_sums,
     g_ref, from_core, from_y, from_zs, from_h, from_z, from_ys, sums, total, sums_t, sums_c, sums_y, sums_z, pack,
-    rs_send, rs_recv, ag_send, ag_recv, y_send, y_recv, sec_send, sec_recv,
+    x_send, rs_recv, ag_recv, y_recv, sec_recv,
     dw_send, dw_recv, sm_send, sm_recv, pk_send, pk_recv,
     back_send, back_recv, ar_send, ar_recv, mt_send, mt_recv, ga_send, ga_recv, ps_send, ps_recv, loads,
 ):
@@ -210,8 +211,15 @@
     for device in (other_core, other_y, *(dp_device(y_at, z_next(o), core) for o in (1, 2, 3))):
         pl.semaphore_signal(barrier, inc=1, device_id=device, device_id_type=MESH)
 
-    load_weights(0, 1, 2, 3)
-    pl.when(cross)(lambda: load_weights(4, 5))
+    small_inputs = tuple(
+        pltpu.make_async_copy(src, dst, small_loads.at[k])
+        for k, (src, dst) in enumerate((
+            (words_hbm, words_ref), (regions_hbm, regions_ref), (lengths_hbm, lengths_ref), (flags_hbm, flags_ref), (qv_bias_hbm, qv_bias_ref), (b1_in_hbm, b1_in_ref), (out_bias_hbm, out_bias_ref), (gain_hbm, gain_ref), (shift_hbm, shift_ref), (cqv_bias_hbm, cqv_bias_ref), (cout_bias_hbm, cout_bias_ref), (cgain_hbm, cgain_ref), (cshift_hbm, cshift_ref),
+        ))
+    )
+    for copy in small_inputs:
+        copy.start()
+    load_weights(0, 1)
 
     def moved(src, dst, send_sem, recv_sem, device):
         return pltpu.make_async_remote_copy(
@@ -235,7 +243,7 @@
 
     def gather_copies(k, step):
         src, dst, count, by_mod = gathered[k]
-        sems = lambda i: (ga_send.at[k, i], ga_recv.at[k, i])
+        sems = lambda i: (ga_send.at[k], ga_recv.at[k, i])
         at = lambda mods, rows: (mods, rows, half_columns) if by_mod else (rows, half_columns)
         mine = at(y_at, z_rows(z_at, count))
         column = at(y_at, slice(0, 4 * count)) if by_mod else None
@@ -267,13 +275,17 @@
             rows = slice(0, 3 * count)
             mods = both_mods if k in Y_FIRST else y_at
             place = dst.at[(mods, rows, half_columns) if by_mod else (rows, half_columns)]
-            moved(place, place, ga_send.at[k, 2], ga_recv.at[k, 2], mate).wait()
+            moved(place, place, ga_send.at[k], ga_recv.at[k, 2], mate).wait()
 
     @pl.when(cross)
     def _():
         pl.semaphore_wait(barrier, 12)
         gather_start("x", CWQKV, CWO, WQKV, WO, W1)
 
+    for copy in small_inputs:
+        copy.wait()
+    load_weights(2, 3)
+    pl.when(cross)(lambda: load_weights(4, 5))
     def side_by_side(rows):
         return jnp.concatenate(rows, axis=1)
 
@@ -353,11 +365,11 @@
 
             def heavy(o=o, at=at):
                 src, dst = send.at[m, rows_at(at)], recv.at[m, o - 1]
-                moved(src, dst, rs_send.at[m], rs_recv.at[m], peer(o)).start()
+                moved(src, dst, x_send.at[m], rs_recv.at[m], peer(o)).start()
 
             def light(o=o):
                 src, dst = packed.at[m], recv.at[m, o - 1, pl.ds(0, 16)]
-                moved(src, dst, rs_send.at[m], rs_recv.at[m], peer(o)).start()
+                moved(src, dst, x_send.at[m], rs_recv.at[m], peer(o)).start()
 
             by_place(at, heavy, light)
 
@@ -365,14 +377,14 @@
         at = place_of(me, m)
 
         def heavy():
-            wait_rows(m, rs_send, rs_recv, 80, 96)
+            wait_rows(m, x_send, rs_recv, 80, 96)
             total = send[m, rows_at(at)].astype(F32)
             for o in range(TENSOR - 1):
                 total = total + recv[m, o].astype(F32)
             total_ref[...] = total
 
         def light():
-            wait_rows(m, rs_send, rs_recv, 96, 48)
+            wait_rows(m, x_send, rs_recv, 96, 48)
             total = packed[m].astype(F32)
             for o in range(TENSOR - 1):
                 total = total + recv[m, o, 0:16].astype(F32)
@@ -381,7 +393,7 @@
         by_place(at, heavy, light)
         return total_ref[...]
 
-    def ag_start(buf, m, low, ss=ag_send, rs=ag_recv):
+    def ag_start(buf, m, low, ss=x_send, rs=ag_recv):
         put_own_rows(buf, m, low)
         at = place_of(me, m)
 
@@ -399,7 +411,7 @@
 
         by_place(at, heavy, light)
 
-    def ag_finish(buf, m, ss=ag_send, rs=ag_recv):
+    def ag_finish(buf, m, ss=x_send, rs=ag_recv):
         def heavy():
             wait_rows(m, ss, rs, 96, 80)
             end = gathered_end[m].astype(F32)
@@ -430,14 +442,14 @@
         return moved(rows, rows, ss, rs, partner)
 
     def mid_start(m):
-        start_rows(midf, m, place_of(me, m), sec_send.at[m], sec_recv.at[m], partner)
+        start_rows(midf, m, place_of(me, m), x_send.at[m], sec_recv.at[m], partner)
 
     def mid_relay(m):
-        some_rows(midf, m, C, sec_send.at[m], sec_recv.at[m]).wait_recv()
-        start_rows(midf, m, place_of(me, m), ag_send.at[m], ag_recv.at[m], peer(1), peer(2), peer(3))
+        some_rows(midf, m, C, x_send.at[m], sec_recv.at[m]).wait_recv()
+        start_rows(midf, m, place_of(me, m), x_send.at[m], ag_recv.at[m], peer(1), peer(2), peer(3))
 
     def mid_finish(m):
-        some_rows(midf, m, 3 * C, ag_send.at[m], ag_recv.at[m]).wait()
+        some_rows(midf, m, 3 * C, x_send.at[m], ag_recv.at[m]).wait()
 
     def back_start(j):
         m = 2 * set_of + j
@@ -561,7 +573,7 @@
     def ar_copies(j, mod, turn):
         lo, hi = SPANS[mod]
         rows = slice(lo, hi - 16)
-        sems = lambda k: (ar_send.at[turn, j, 2 * mod + k], ar_recv.at[turn, j, 2 * mod + k])
+        sems = lambda k: (ar_send.at[j, 2 * mod + k], ar_recv.at[turn, j, 2 * mod + k])
         return [
             moved(send.at[j, rows], got.at[turn, j, rows], *sems(0), halver),
             moved(tails.at[j, mod], got_tails.at[turn, j, mod], *sems(1), halver),
@@ -633,8 +645,8 @@
 
     def bias_copies():
         return [
-            moved(bqkv_ref, bqkv_m, ga_send.at[6, 0], ga_recv.at[6, 0], mate),
-            moved(b1_ref, b1_m, ga_send.at[6, 1], ga_recv.at[6, 1], mate),
+            moved(bqkv_ref, bqkv_m, ga_send.at[6], ga_recv.at[6, 0], mate),
+            moved(b1_ref, b1_m, ga_send.at[7], ga_recv.at[6, 1], mate),
         ]
 
     def save_norm_f(l, j, lo, hi, n, r):
@@ -870,7 +882,7 @@
 
     def dw_copies(group, phase):
         index, kind, b = group
-        sems = lambda k: (dw_send.at[index, k], dw_recv.at[index, k])
+        sems = lambda k: (dw_send.at[index], dw_recv.at[index, k])
         if phase == 0:
             return [moved(g_ref.at[b, :, :, 1 - core], from_core.at[b], *sems(0), other_core)]
         to = lambda z: dp_device(y_at, z, core)
@@ -929,7 +941,7 @@
         if together is None:
             dw_copies(group, phase)[0].wait()
         else:
-            moved(together, together, dw_send.at[index, 2], dw_recv.at[index, 2], other_core).wait()
+            moved(together, together, dw_send.at[index], dw_recv.at[index, 2], other_core).wait()
 
         def add(place, *others):
             total = g_ref[place].astype(F32)
@@ -980,7 +992,7 @@
     ATTN_W, ATTN_R, CROSS = (4, Y, 0), (5, Z, 4), (6, Y, 3)
 
     def sm_copies(step, count):
-        sems = (sm_send.at[step], sm_recv.at[step])
+        sems = (sm_send.at[0], sm_recv.at[step])
         if step == 0:
             return [moved(sums_t.at[me], sums_t.at[me], *sems, peer(o)) for o in range(1, TENSOR)]
         rows = pl.ds(0, count)
@@ -1000,7 +1012,7 @@
     def sm_wait(step, count=32):
         if step in (0, 3):
             place = sums_z.at[:, pl.ds(0, count)] if step == 3 else sums_t.at[pl.ds(0, TENSOR - 1)]
-            moved(place, place, sm_send.at[step], sm_recv.at[step], other_core).wait()
+            moved(place, place, sm_send.at[0], sm_recv.at[step], other_core).wait()
         else:
             sm_copies(step, count)[0].wait()
 
@@ -1072,12 +1084,12 @@
             mid_start(m)
 
         def from_partner(m):
-            some_rows(midf, m, C, sec_send.at[m], sec_recv.at[m]).wait_send()
+            some_rows(midf, m, C, x_send.at[m], sec_recv.at[m]).wait_send()
             back_arrive(m)
             back_e(m, own_rows_of(back, m).astype(F32))
 
         def last(m):
-            ag_start(ybuf, m, (res[m] + rs_finish(m)).astype(BF), y_send, y_recv)
+            ag_start(ybuf, m, (res[m] + rs_finish(m)).astype(BF), x_send, y_recv)
 
         front, rear = dict(first=0, last=2), dict(first=2, last=4)
         wait_weights(0, 1)
@@ -1085,10 +1097,11 @@
             layer_a,
             after=(
                 None, then(p(pl.semaphore_wait, barrier, 12), p(rs_start, 0), p(rs_start, 1)),
-                p(rs_start, 2),
             ),
         )
-        each(layer_b, **front)
+        layer_b(0)
+        rs_start(2)
+        layer_b(1)
         rs_start(3)
         layer_b(2)
         wait_weights(2, 3)
@@ -1099,18 +1112,19 @@
         layer_c(3)
         each(to_partner, **rear)
         each(from_partner, last=3)
-        each(back_f, after=(p(from_partner, 3), None, p(back_g, 0), p(back_g, 1)))
+        each(back_f, after=(p(from_partner, 3), None, p(back_g, 0)))
         ffn_piece(2)
         dw_start(IN_R, 0)
+        back_g(1)
         ffn_piece(3)
         dw_start(OUT_R, 0)
         back_g(2)
+        dw_turn(IN_R, 0)
         ffn_piece(0)
         dw_start(IN_W, 0)
-        dw_turn(IN_R, 0)
+        dw_turn(OUT_R, 0)
         ffn_piece(1)
         dw_start(OUT_W, 0)
-        dw_turn(OUT_R, 0)
         back_g(3)
         each(
             back_h,
@@ -1137,9 +1151,9 @@
         dw_turn(IN_R, 2)
         dw_turn(IN_W, 2)
         dw_turn(OUT_W, 2)
-        dw_turn(ATTN_R, 1)
         small_z(16)
         dw_turn(ATTN_W, 1)
+        dw_turn(ATTN_R, 1)
 
     @pl.when(cross)
     def _():
@@ -1224,7 +1238,10 @@
         mate_start_all(DYA, DQKV)
         for k in range(2):
             mid_finish(2 * (1 - set_of) + k)
+        dw_turn(IN_R, 1)
+        dw_turn(IN_W, 1)
         mate_wait(CDQKV)
+        dw_turn(OUT_R, 1)
         pass_wait(DYC)
         cross_outer()
         dw_start(CROSS, 0)
@@ -1232,9 +1249,10 @@
         dw_turn(CROSS, 0)
         mate_wait(DYA)
         pass_start(DYA)
-        dw_turn(IN_R, 1)
-        dw_turn(OUT_R, 1)
-        dw_turn(IN_W, 1)
+        dw_turn(OUT_W, 1)
+        dw_turn(IN_R, 2)
+        dw_turn(IN_W, 2)
+        dw_turn(OUT_R, 2)
         mate_wait(DQKV)
         mate_start_all(YBUF)
         pass_wait(XLOW)
@@ -1246,17 +1264,13 @@
         attn_piece(3)
         dw_start(ATTN_R, 0)
         small_y(32)
-        dw_turn(OUT_W, 1)
         attn_piece(0)
         attn_piece(1)
         dw_start(ATTN_W, 0)
         dw_turn(CROSS, 1)
+        dw_turn(ATTN_R, 0)
         small_z(32)
-        dw_turn(ATTN_R, 0)
         dw_turn(ATTN_W, 0)
-        dw_turn(IN_R, 2)
-        dw_turn(IN_W, 2)
-        dw_turn(OUT_R, 2)
         dw_turn(OUT_W, 2)
         mate_wait(YBUF)
         pass_start(YBUF)
@@ -1277,7 +1291,7 @@
     def write(m):
         @pl.when(head)
         def _():
-            ag_finish(ybuf, m, y_send, y_recv)
+            ag_finish(ybuf, m, x_send, y_recv)
 
         pltpu.make_async_copy(ybuf.at[m], y_out.at[m], out_sems.at[7 + m]).start()
 
@@ -1372,7 +1386,6 @@
     )
 
     vmem = pl.BlockSpec(memory_space=pltpu.VMEM)
-    smem = pl.BlockSpec(memory_space=pltpu.SMEM)
     hbm = pl.BlockSpec(memory_space=pl.ANY)
     mb_rows = lambda width, dtype: pltpu.VMEM((MB, R, width), dtype)
     own_rows = lambda count: pltpu.VMEM((count, MB, C, D), F32)
@@ -1385,9 +1398,14 @@
             jax.ShapeDtypeStruct((24, D), F32),
             jax.ShapeDtypeStruct((24, D), F32),
         ),
-        in_specs=[smem if k in (2, 3) else hbm if k in (4, 6, 7, 9, 13, 15) else vmem for k in range(len(inputs))],
+        in_specs=[hbm] * len(inputs),
         out_specs=[hbm] * 2 + [vmem] * 3,
         scratch_shapes=[
+            *[
+                (pltpu.SMEM if k in (2, 3) else pltpu.VMEM)(inputs[k].shape, inputs[k].dtype)
+                for k in (0, 1, 2, 3, 5, 8, 10, 11, 12, 14, 16, 17, 18)
+            ],
+            pltpu.SemaphoreType.DMA((13,)),
             pltpu.VMEM((7, 48, D), F32),
             pltpu.SemaphoreType.DMA((7 + MB,)),
             mb_rows(D, BF),
@@ -1457,20 +1475,20 @@
             pltpu.VMEM((32, D), BF),
             pltpu.VMEM((3, 32, D), BF),
             pltpu.VMEM((2, 48, D), F32),
-            *[pltpu.SemaphoreType.DMA((MB,)) for _ in range(6)],
-            pltpu.SemaphoreType.DMA((MB,)),
-            pltpu.SemaphoreType.DMA((MB,)),
+            *[pltpu.SemaphoreType.DMA((MB,)) for _ in range(5)],
+            pltpu.SemaphoreType.DMA((7,)),
             pltpu.SemaphoreType.DMA((7, 4)),
-            pltpu.SemaphoreType.DMA((7, 4)),
-            pltpu.SemaphoreType.DMA((4,)),
+            pltpu.SemaphoreType.DMA((1,)),
             pltpu.SemaphoreType.DMA((4,)),
             pltpu.SemaphoreType.DMA,
             pltpu.SemaphoreType.DMA,
             pltpu.SemaphoreType.DMA((2,)),
             pltpu.SemaphoreType.DMA((MB,)),
-            *[pltpu.SemaphoreType.DMA((2, 2, 4)) for _ in range(2)],
+            pltpu.SemaphoreType.DMA((2, 4)),
+            pltpu.SemaphoreType.DMA((2, 2, 4)),
             *[pltpu.SemaphoreType.DMA((12,)) for _ in range(2)],
-            *[pltpu.SemaphoreType.DMA((7, 4)) for _ in range(2)],
+            pltpu.SemaphoreType.DMA((8,)),
+            pltpu.SemaphoreType.DMA((7, 4)),
             *[pltpu.SemaphoreType.DMA((6,)) for _ in range(2)],
             pltpu.SemaphoreType.DMA((6,)),
         ],

time: 149 us -> 147 us (0.987)
  no operation moved by 1% of the time
where the time goes in v8:
time: 147 us
  Pallas kernels  146 us (99%)
    pallas_call x1, Pallas kernels, local(): pl.pallas_call(kernel, out_shape=(jax.ShapeDtypeStruct((MB, R, D), BF), j...  143 us
    pallas_call x1, Pallas kernels, local(): pl.pallas_call(arrange, out_shape=tuple((jax.ShapeDtypeStruct(shape, F32)...  3.27 us

profile of v8, /device:TPU:0, one launch (start us, length us, event | category | flops | bytes accessed | tf_op | source)
XLA Modules:
  0.0 147.1 jit_solution(6867122748908855695)
XLA Ops:
  0.7 143.0 %shard_map.314 = (bf16[4,128,768]{2,1,0:T(8,128)(2,1)}, f32[7,48,768]{2,1,0:T(8,128)}, f32[24,768]{1,0:T(8,128)}, f32[24,768]{1,0:T(8,128)}, f32[24,768]{1,0:T(8,128)}) custom-call(bf16[1,20,8,768]{3,2,1,0:T(8,128)(2,1)} %bitcast.30, bf16[1,36,8,768]{3,2,1,0:T(8,128)(2,1)} %bitcast.29, s32[8]{0:T(128)} %lengths_hbm.1, s32[8]{0:T(128)} %flags_hbm.1, ...), custom_call_target="tpu_custom_call" | custom-call | tf_op jit(solution)/shard_map/pallas_call | solution.py:1392
  143.6 3.3 %shard_map.315 = (f32[1,20,8,768]{3,2,1,0:T(8,128)}, f32[1,36,8,768]{3,2,1,0:T(8,128)}, f32[1,2,3,48,192]{4,3,2,1,0:T(8,128)}, f32[1,2,3,2,4]{4,3,2,1,0:T(2,128)...) custom-call(bf16[4,128,768]{2,1,0:T(8,128)(2,1)} %get-tuple-element., ...), custom_call_target="tpu_custom_call" | custom-call | tf_op jit(solution)/shard_map/pallas_call | solution.py:1510

commit v9 on v8

--- a/solution.py
+++ b/solution.py
@@ -725,13 +725,12 @@
                 pl.when(j == 0)(lambda: gather_wait("core", W1))
             ups = [dot(low, w[mod]) + bias[mod] for w, bias, _, _, _ in shards]
             pairs = [gelu(up) for up in ups]
-            for sh, (_, _, _, keep, at) in enumerate(shards):
-                keep[at, lo:hi], dgelu[2 * sh + j, lo:hi] = pairs[sh]
             if mod == 0:
                 pl.when(j == 0)(lambda: gather_wait("core", W2))
             ones = [dot(active, w_out[mod]) for (active, _), (_, _, w_out, _, _) in zip(pairs, shards)]
-            part = ones[0] + ones[1]
-            ar_start(j, mod, 0, part)
+            ar_start(j, mod, 0, ones[0] + ones[1])
+            for sh, (_, _, _, keep, at) in enumerate(shards):
+                keep[at, lo:hi], dgelu[2 * sh + j, lo:hi] = pairs[sh]
         mate_start(j, ALOW, ACT)
 
     def ffn_turn(j):
@@ -751,11 +750,10 @@
             dacts = [dot_nt(low, w_out[mod]) for _, w_out, _, _ in shards]
             ds = [(dact * dgelu[2 * sh + j, lo:hi]).astype(BF) for sh, dact in enumerate(dacts)]
             ones = [dot_nt(d, w_in[mod]) for d, (w_in, _, _, _) in zip(ds, shards)]
-            part = ones[0] + ones[1]
+            ar_start(j, mod, 1, ones[0] + ones[1])
             for d, (_, _, keep, at) in zip(ds, shards):
                 keep[at, lo:hi] = d
             count_rows(1, mod, dh, n, low)
-            ar_start(j, mod, 1, part)
         mate_start(j, DYF, DUP)
 
     def attn_backward(j):
@@ -768,7 +766,6 @@
             res_f[j, lo:hi] = dr
             low = dr.astype(BF)
             dya[m, lo:hi] = low
-            count_rows(0, mod, dh, n, low)
             dmixs = [dot_nt(low, w_out[mod]).astype(BF) for _, w_out, _, _ in shards]
             grads = attend_back([
                 (dmix, (p_w, p_r)[mod][2 * sh + j], *(qkv[k, 2 * sh + j, lo:hi] for k in range(3)))
@@ -781,6 +778,7 @@
                 one = dot(d, w[mod])
                 part = one if part is None else part + one
             ar_start(j, mod, 0, part)
+            count_rows(0, mod, dh, n, low)
 
     def cross_backward(j):
         m = block_of(j)

time: 147 us -> 147 us (level)
  no operation moved by 1% of the time
where the time goes in v9:
time: 147 us
  Pallas kernels  146 us (99%)
    pallas_call x1, Pallas kernels, local(): pl.pallas_call(kernel, out_shape=(jax.ShapeDtypeStruct((MB, R, D), BF), j...  143 us
    pallas_call x1, Pallas kernels, local(): pl.pallas_call(arrange, out_shape=tuple((jax.ShapeDtypeStruct(shape, F32)...  3.27 us

profile of v9, /device:TPU:0, one launch (start us, length us, event | category | flops | bytes accessed | tf_op | source)
XLA Modules:
  0.0 147.2 jit_solution(4085549395124980180)
XLA Ops:
  0.7 143.0 %shard_map.314 = (bf16[4,128,768]{2,1,0:T(8,128)(2,1)}, f32[7,48,768]{2,1,0:T(8,128)}, f32[24,768]{1,0:T(8,128)}, f32[24,768]{1,0:T(8,128)}, f32[24,768]{1,0:T(8,128)}) custom-call(bf16[1,20,8,768]{3,2,1,0:T(8,128)(2,1)} %bitcast.30, bf16[1,36,8,768]{3,2,1,0:T(8,128)(2,1)} %bitcast.29, s32[8]{0:T(128)} %lengths_hbm.1, s32[8]{0:T(128)} %flags_hbm.1, ...), custom_call_target="tpu_custom_call" | custom-call | tf_op jit(solution)/shard_map/pallas_call | solution.py:1390
  143.7 3.3 %shard_map.315 = (f32[1,20,8,768]{3,2,1,0:T(8,128)}, f32[1,36,8,768]{3,2,1,0:T(8,128)}, f32[1,2,3,48,192]{4,3,2,1,0:T(8,128)}, f32[1,2,3,2,4]{4,3,2,1,0:T(2,128)...) custom-call(bf16[4,128,768]{2,1,0:T(8,128)(2,1)} %get-tuple-element., ...), custom_call_target="tpu_custom_call" | custom-call | tf_op jit(solution)/shard_map/pallas_call | solution.py:1508
